TPU v7x, 32 devices: a whole 2x2x4 slice. The times are simulated.
32 devices in a mesh: ctx: 16 (over z, y, x), dp: 2 (over core).
Axes of the slice: x: 2, y: 2, z: 4, core: 2. Of those that a mesh axis runs over, the one named last changes fastest.
Arguments:
- queries: bfloat16 [2, 2048, 2048], P('dp', 'ctx'), may hold values from -110 to 110
- keys: bfloat16 [2, 2048, 512], P('dp', 'ctx'), may hold values from -4 to 4
- values: bfloat16 [2, 2048, 512], P('dp', 'ctx'), may hold values from -4 to 4
- grad_out: bfloat16 [2, 2048, 2048], P('dp', 'ctx'), may hold values from -12 to 12
- sinks: float32 [16], replicated, may hold values from 0 to 6
- doc_ids: int32 [2, 16], P('dp'), may hold values from 0 to 3, never falling along the last dimension, each value on 1 to 8 neighbouring positions
Outputs:
- grad_queries: bfloat16 [2, 2048, 2048], P('dp', 'ctx')
- grad_keys: bfloat16 [2, 2048, 512], P('dp', 'ctx')
- grad_values: bfloat16 [2, 2048, 512], P('dp', 'ctx')
- grad_sinks: float32 [16], replicated
All inputs are finite; a program needn't handle non-finite values.
Results may differ from a plain program's by a relative error of at most 0.017.
Values may be sent and summed in bfloat16 or wider, within the bound.
No kernel may reach another device: no remote copies, remote signals or barrier semaphores. Data moves between devices by JAX's collectives and lax.ppermute only.
A program may use at most 64 MiB of HBM per device.

v0:
```python
import jax
import jax.numpy as jnp
from jax import lax
from jax.sharding import PartitionSpec as P

BLOCK = 128
WINDOW = 512


def passed_along(value, axis, steps):
    count = lax.axis_size(axis)
    initial, last = (max(0, -steps), min(count, count - steps))
    return lax.ppermute(value, axis, [(source, source + steps) for source in range(initial, last)])


def local(queries, keys, values, grad_out, sinks, doc_ids):
    row_count = queries.shape[1]
    head_count = sinks.shape[0]
    head_size = queries.shape[2] // head_count
    kv_count = keys.shape[2] // head_size
    group_size = head_count // kv_count
    reach_count = -(-WINDOW // row_count)
    key_count = (reach_count + 1) * row_count
    shard_index = lax.axis_index("ctx")
    score_scale = head_size ** (-0.5)
    own_kv = jnp.stack([keys[0], values[0]])
    remote = []
    for distance in range(1, reach_count + 1):
        remote.append(passed_along(own_kv, "ctx", distance))
    window_kv = jnp.concatenate(remote[::-1] + [own_kv], axis=1)
    key_rows = window_kv[0].reshape(key_count, kv_count, head_size)
    value_rows = window_kv[1].reshape(key_count, kv_count, head_size)
    own_blocks = row_count // BLOCK
    doc_row = doc_ids[0]
    padded_docs = jnp.concatenate([jnp.full((reach_count * own_blocks,), -1, jnp.int32), doc_row])
    query_docs = lax.dynamic_slice_in_dim(doc_row, shard_index * own_blocks, own_blocks)
    key_docs = lax.dynamic_slice_in_dim(padded_docs, shard_index * own_blocks, key_count // BLOCK)
    same_doc = jnp.broadcast_to(
        query_docs[:, None, None, None] == key_docs[None, None, :, None],
        (own_blocks, BLOCK, key_count // BLOCK, BLOCK),
    ).reshape(row_count, key_count)
    offsets = (
        reach_count * row_count
        + jnp.arange(row_count, dtype=jnp.int32)[:, None]
        - jnp.arange(key_count, dtype=jnp.int32)[None, :]
    )
    allowed = same_doc & (offsets >= 0) & (offsets < WINDOW)
    query_rows = queries[0].reshape(row_count, kv_count, group_size, head_size)
    cotangent = grad_out[0].reshape(row_count, kv_count, group_size, head_size)
    sink_grid = sinks.reshape(kv_count, group_size)
    query_parts, key_parts, value_parts, sink_parts = ([], [], [], [])
    for member in range(kv_count):
        q_part = query_rows[:, member]
        g_part = cotangent[:, member]
        k_part = key_rows[:, member]
        v_part = value_rows[:, member]
        sink_col = sink_grid[member][:, None]
        scores = (
            jnp.einsum("tgd,kd->gtk", q_part, k_part, preferred_element_type=jnp.float32)
            * score_scale
        )
        masked = jnp.where(allowed[None], scores, -jnp.inf)
        top_score = jnp.maximum(jnp.max(masked, axis=-1), sink_col)
        raised = jnp.exp(masked - top_score[..., None])
        sink_weight = jnp.exp(sink_col - top_score)
        summed = sink_weight + jnp.sum(raised, axis=-1)
        probs = (raised / summed[..., None]).astype(jnp.bfloat16)
        attended = jnp.einsum("gtk,kd->tgd", probs, v_part, preferred_element_type=jnp.float32)
        delta = jnp.transpose(jnp.sum(g_part.astype(jnp.float32) * attended, axis=-1))
        sink_parts.append(-jnp.sum(sink_weight / summed * delta, axis=-1))
        grad_probs = jnp.einsum("tgd,kd->gtk", g_part, v_part, preferred_element_type=jnp.float32)
        grad_scores = (probs.astype(jnp.float32) * (grad_probs - delta[..., None])).astype(
            jnp.bfloat16
        )
        query_parts.append(
            (
                jnp.einsum("gtk,kd->tgd", grad_scores, k_part, preferred_element_type=jnp.float32)
                * score_scale
            ).astype(jnp.bfloat16)
        )
        key_parts.append(
            jnp.einsum("gtk,tgd->kd", grad_scores, q_part, preferred_element_type=jnp.float32)
            * score_scale
        )
        value_parts.append(
            jnp.einsum("gtk,tgd->kd", probs, g_part, preferred_element_type=jnp.float32)
        )
    grad_queries = jnp.stack(query_parts, axis=1).reshape(1, row_count, head_count * head_size)
    kv_grads = jnp.stack([jnp.stack(key_parts, axis=1), jnp.stack(value_parts, axis=1)]).reshape(
        2, key_count, kv_count * head_size
    )

    def share_for(distance):
        return lax.slice_in_dim(
            kv_grads,
            (reach_count - distance) * row_count,
            (reach_count - distance + 1) * row_count,
            axis=1,
        )

    running = share_for(0)
    for distance in range(1, reach_count + 1):
        running = running + passed_along(share_for(distance), "ctx", -distance)
    grad_sinks = lax.psum(jnp.concatenate(sink_parts), ("ctx", "dp"))
    return (
        grad_queries,
        running[0][None].astype(jnp.bfloat16),
        running[1][None].astype(jnp.bfloat16),
        grad_sinks,
    )


def solution(mesh):
    in_specs = (
        P("dp", "ctx", None),
        P("dp", "ctx", None),
        P("dp", "ctx", None),
        P("dp", "ctx", None),
        P(),
        P("dp", None),
    )
    out_specs = (P("dp", "ctx", None), P("dp", "ctx", None), P("dp", "ctx", None), P())
    return jax.shard_map(local, mesh=mesh, in_specs=in_specs, out_specs=out_specs, check_vma=False)
```

profile of v0, /device:TPU:2, one launch (start us, length us, event | category | flops | bytes accessed | tf_op | source)
XLA Modules:
  0.0 152.8 jit_solution(9922878642922415175)
XLA Ops:
  0.6 1.1 copy.49
  1.7 1.0 copy.50
  2.8 0.7 pad_maximum_fusion.4
  3.5 3.4 %collective-permute-start.3 = (bf16[2,128,512]{1,2,0:T(8,128)(2,1)}, bf16[2,128,512]{1,2,0:T(8,128)(2,1)S(1)}, u32[]{:S(2)}, u32[]{:S(2)}) collective-permute-start(bf16[2,128,512]{1,2,0:T(8,128)(2,1)} %pad_maximum_fusion.4), channel_id=1, source_target_pairs={{0,2},{2,4},{4,6},{6,8},{8,10},{10,12},{12,14},{14,16},{16,18},{18... | collective-permute-start | bytes 786440 | tf_op jit(solution)/shard_map/ppermute | solution.py:13
  6.9 4.1 %collective-permute-start.2 = (bf16[2,128,512]{1,2,0:T(8,128)(2,1)}, bf16[2,128,512]{1,2,0:T(8,128)(2,1)}, u32[]{:S(2)}, u32[]{:S(2)}) collective-permute-start(bf16[2,128,512]{1,2,0:T(8,128)(2,1)} %pad_maximum_fusion.4), channel_id=1, source_target_pairs={{0,4},{2,6},{4,8},{6,10},{8,12},{10,14},{12,16},{14,18},{16,20},{1... | collective-permute-start | bytes 786440 | tf_op jit(solution)/shard_map/ppermute | solution.py:13
  11.0 3.5 %collective-permute-start.1 = (bf16[2,128,512]{1,2,0:T(8,128)(2,1)}, bf16[2,128,512]{1,2,0:T(8,128)(2,1)}, u32[]{:S(2)}, u32[]{:S(2)}) collective-permute-start(bf16[2,128,512]{1,2,0:T(8,128)(2,1)} %pad_maximum_fusion.4), channel_id=1, source_target_pairs={{0,6},{2,8},{4,10},{6,12},{8,14},{10,16},{12,18},{14,20},{16,22},{... | collective-permute-start | bytes 786440 | tf_op jit(solution)/shard_map/ppermute | solution.py:13
  14.5 3.5 %collective-permute-start = (bf16[2,128,512]{1,2,0:T(8,128)(2,1)}, bf16[2,128,512]{1,2,0:T(8,128)(2,1)}, u32[]{:S(2)}, u32[]{:S(2)}) collective-permute-start(bf16[2,128,512]{1,2,0:T(8,128)(2,1)} %pad_maximum_fusion.4), channel_id=1, source_target_pairs={{0,8},{2,10},{4,12},{6,14},{8,16},{10,18},{12,20},{14,22},{16,24},... | collective-permute-start | bytes 786440 | tf_op jit(solution)/shard_map/ppermute | solution.py:13
  18.0 1.2 constant_dynamic-slice_fusion
  19.2 1.4 dynamic-slice_compare_fusion
  22.1 2.6 %collective-permute-done = bf16[2,128,512]{1,2,0:T(8,128)(2,1)} collective-permute-done((bf16[2,128,512]{1,2,0:T(8,128)(2,1)}, bf16[2,128,512]{1,2,0:T(8,128)(2,1)}, u32[]{:S(2)}, u32[]{:S(2)}) %collective-permute-start) | collective-permute-done | bytes 262176 | tf_op jit(solution)/shard_map/ppermute | solution.py:13
  24.7 1.0 constant_dynamic-update-slice_fusion.4
  25.7 1.0 constant_dynamic-update-slice_fusion.3
  26.8 1.0 constant_dynamic-update-slice_fusion.2
  29.0 1.1 convolution_bitcast_fusion.4
  31.0 0.9 fusion.44
  34.0 1.1 convolution_bitcast_fusion.5
  37.1 1.1 convolution_bitcast_fusion.6
  40.1 1.1 convolution_bitcast_fusion.7
  43.6 2.4 %pad_maximum_fusion.1 = f32[640,4,128]{0,2,1:T(8,128)} fusion(f32[640,1,128]{0,2,1:T(8,128)} %convolution_bitcast_fusion.4, f32[640,1,128]{0,2,1:T(8,128)} %convolution_bitcast_fusion.5, f32[640,1,128]{0,2,1:T(8,128)} %convolution_bitcast_fusion.6, f32[640,1,128]{0,2,1:T(8,128)} %convolution_bitcast_fusion.7), kind=kLoop, calls=%fused_computation.37 | loop fusion | flops 983040 | bytes 2621440 | tf_op jit(solution)/shard_map/stack | solution.py:89
  46.1 1.7 %copy.106 = f32[1,640,512]{2,1,0:T(8,128)S(1)} copy(f32[1,640,512]{1,2,0:T(8,128)} %bitcast.328) | data formatting | bytes 2621440 | tf_op jit(solution)/shard_map/stack | solution.py:89
  47.8 47.4 %psum.7 = f32[16]{0:T(128)} all-reduce(f32[16]{0:T(128)S(1)} %pad_maximum_fusion.5), channel_id=1, replica_groups=mesh['ctx'=16,'dp'=2] {'ctx','dp'}, use_global_device_ids=true, to_apply=%region_16.17 | all-reduce | flops 16 | bytes 128 | tf_op jit(solution)/shard_map/psum | solution.py:104
  95.2 1.3 fusion.55
  96.5 2.0 %collective-permute-start.4 = (f32[2,128,512]{2,1,0:T(8,128)}, f32[2,128,512]{2,1,0:T(8,128)}, u32[]{:S(2)}, u32[]{:S(2)}) collective-permute-start(f32[2,128,512]{2,1,0:T(8,128)} %get-tuple-element.12), channel_id=1, source_target_pairs={{2,0},{4,2},{6,4},{8,6},{10,8},{12,10},{14,12},{16,14},{18,16},{20... | collective-permute-start | bytes 1572872 | tf_op jit(solution)/shard_map/ppermute | solution.py:13
  98.5 1.3 collective-permute-start.5
  99.8 1.3 collective-permute-start.7
  101.1 1.4 collective-permute-start.6
  103.5 1.0 copy.107
  104.5 8.0 %collective-permute-done.4 = f32[2,128,512]{2,1,0:T(8,128)} collective-permute-done((f32[2,128,512]{2,1,0:T(8,128)}, f32[2,128,512]{2,1,0:T(8,128)}, u32[]{:S(2)}, u32[]{:S(2)}) %collective-permute-start.4) | collective-permute-done | bytes 524320 | tf_op jit(solution)/shard_map/ppermute | solution.py:13
  112.6 11.1 %collective-permute-done.5 = f32[2,128,512]{2,1,0:T(8,128)} collective-permute-done((f32[2,128,512]{2,1,0:T(8,128)}, f32[2,128,512]{2,1,0:T(8,128)}, u32[]{:S(2)}, u32[]{:S(2)}) %collective-permute-start.5) | collective-permute-done | bytes 524320 | tf_op jit(solution)/shard_map/ppermute | solution.py:13
  123.7 13.3 %collective-permute-done.7 = f32[2,128,512]{2,1,0:T(8,128)} collective-permute-done((f32[2,128,512]{2,1,0:T(8,128)}, f32[2,128,512]{2,1,0:T(8,128)}, u32[]{:S(2)}, u32[]{:S(2)}) %collective-permute-start.7) | collective-permute-done | bytes 524320 | tf_op jit(solution)/shard_map/ppermute | solution.py:13
  137.0 13.4 %collective-permute-done.6 = f32[2,128,512]{2,1,0:T(8,128)} collective-permute-done((f32[2,128,512]{2,1,0:T(8,128)}, f32[2,128,512]{2,1,0:T(8,128)}, u32[]{:S(2)}, u32[]{:S(2)}) %collective-permute-start.6) | collective-permute-done | bytes 524320 | tf_op jit(solution)/shard_map/ppermute | solution.py:13
  150.4 1.7 %fusion.54 = bf16[2,128,512]{2,1,0:T(8,128)(2,1)S(1)} fusion(f32[2,128,512]{2,1,0:T(8,128)} %collective-permute-done.7, f32[2,128,512]{2,1,0:T(8,128)} %collective-permute-done.6, f32[2,128,512]{2,1,0:T(8,128)} %collective-permute-done.5, f32[2,128,512]{2,1,0:T(8,128)} %collective-permute-done.4, f32[1,640,512]{2,1,0:T(8,128)S(1)} %copy.105, ...), kind=kLoop, calls=%fused_computation.96 | loop fusion | flops 786432 | bytes 4980736 | tf_op jit(solution)/shard_map/convert.1
  (83 shorter events, 13.4 us)
Async XLA Ops:
  0.6 20.1 %copy-start.6 = (bf16[1,128,2048]{2,1,0:T(8,128)(2,1)S(1)}, bf16[1,128,2048]{2,1,0:T(8,128)(2,1)}, u32[]{:S(2)}) copy-start(bf16[1,128,2048]{2,1,0:T(8,128)(2,1)} %param.9) | copy-start | bytes 1572868
  2.8 18.4 %copy-start.9 = (f32[16]{0:T(128)S(1)}, f32[16]{0:T(128)}, u32[]{:S(2)}) copy-start(f32[16]{0:T(128)} %param.10) | copy-start | bytes 196
  2.8 18.5 %copy-start.7 = (bf16[1,128,2048]{2,1,0:T(8,128)(2,1)S(1)}, bf16[1,128,2048]{2,1,0:T(8,128)(2,1)}, u32[]{:S(2)}) copy-start(bf16[1,128,2048]{2,1,0:T(8,128)(2,1)} %param.6) | copy-start | bytes 1572868
  3.5 24.3 %collective-permute-start.3 = (bf16[2,128,512]{1,2,0:T(8,128)(2,1)}, bf16[2,128,512]{1,2,0:T(8,128)(2,1)S(1)}, u32[]{:S(2)}, u32[]{:S(2)}) collective-permute-start(bf16[2,128,512]{1,2,0:T(8,128)(2,1)} %pad_maximum_fusion.4), channel_id=1, source_target_pairs={{0,2},{2,4},{4,6},{6,8},{8,10},{10,12},{12,14},{14,16},{16,18},{18... | collective-permute-start | bytes 786440 | tf_op jit(solution)/shard_map/ppermute | solution.py:13
  6.9 19.8 %collective-permute-start.2 = (bf16[2,128,512]{1,2,0:T(8,128)(2,1)}, bf16[2,128,512]{1,2,0:T(8,128)(2,1)}, u32[]{:S(2)}, u32[]{:S(2)}) collective-permute-start(bf16[2,128,512]{1,2,0:T(8,128)(2,1)} %pad_maximum_fusion.4), channel_id=1, source_target_pairs={{0,4},{2,6},{4,8},{6,10},{8,12},{10,14},{12,16},{14,18},{16,20},{1... | collective-permute-start | bytes 786440 | tf_op jit(solution)/shard_map/ppermute | solution.py:13
  11.0 14.7 %collective-permute-start.1 = (bf16[2,128,512]{1,2,0:T(8,128)(2,1)}, bf16[2,128,512]{1,2,0:T(8,128)(2,1)}, u32[]{:S(2)}, u32[]{:S(2)}) collective-permute-start(bf16[2,128,512]{1,2,0:T(8,128)(2,1)} %pad_maximum_fusion.4), channel_id=1, source_target_pairs={{0,6},{2,8},{4,10},{6,12},{8,14},{10,16},{12,18},{14,20},{16,22},{... | collective-permute-start | bytes 786440 | tf_op jit(solution)/shard_map/ppermute | solution.py:13
  14.5 10.2 %collective-permute-start = (bf16[2,128,512]{1,2,0:T(8,128)(2,1)}, bf16[2,128,512]{1,2,0:T(8,128)(2,1)}, u32[]{:S(2)}, u32[]{:S(2)}) collective-permute-start(bf16[2,128,512]{1,2,0:T(8,128)(2,1)} %pad_maximum_fusion.4), channel_id=1, source_target_pairs={{0,8},{2,10},{4,12},{6,14},{8,16},{10,18},{12,20},{14,22},{16,24},... | collective-permute-start | bytes 786440 | tf_op jit(solution)/shard_map/ppermute | solution.py:13
  28.1 5.0 %copy-start.4 = (bf16[1,640,512]{1,2,0:T(8,128)(2,1)}, bf16[1,640,512]{1,2,0:T(8,128)(2,1)S(1)}, u32[]{:S(2)}) copy-start(bf16[1,640,512]{1,2,0:T(8,128)(2,1)S(1)} %get-tuple-element.17) | copy-start | bytes 1966084
  39.1 0.9 copy-start
  42.3 0.9 copy-start.2
  95.1 7.4 %copy-start.5 = (bf16[1,640,512]{1,2,0:T(8,128)(2,1)S(1)}, bf16[1,640,512]{1,2,0:T(8,128)(2,1)}, u32[]{:S(2)}) copy-start(bf16[1,640,512]{1,2,0:T(8,128)(2,1)} %copy-done.4) | copy-start | bytes 1966084
  95.1 7.7 %copy-start.1 = (bf16[4,128,640]{1,2,0:T(8,128)(2,1)S(1)}, bf16[4,128,640]{1,2,0:T(8,128)(2,1)}, u32[]{:S(2)}) copy-start(bf16[4,128,640]{1,2,0:T(8,128)(2,1)} %copy-done) | copy-start | bytes 1966084
  96.5 6.7 %copy-start.3 = (bf16[4,128,640]{1,2,0:T(8,128)(2,1)S(1)}, bf16[4,128,640]{1,2,0:T(8,128)(2,1)}, u32[]{:S(2)}) copy-start(bf16[4,128,640]{1,2,0:T(8,128)(2,1)} %copy-done.2) | copy-start | bytes 1966084
  96.5 16.1 %collective-permute-start.4 = (f32[2,128,512]{2,1,0:T(8,128)}, f32[2,128,512]{2,1,0:T(8,128)}, u32[]{:S(2)}, u32[]{:S(2)}) collective-permute-start(f32[2,128,512]{2,1,0:T(8,128)} %get-tuple-element.12), channel_id=1, source_target_pairs={{2,0},{4,2},{6,4},{8,6},{10,8},{12,10},{14,12},{16,14},{18,16},{20... | collective-permute-start | bytes 1572872 | tf_op jit(solution)/shard_map/ppermute | solution.py:13
  98.5 25.2 %collective-permute-start.5 = (f32[2,128,512]{2,1,0:T(8,128)}, f32[2,128,512]{2,1,0:T(8,128)}, u32[]{:S(2)}, u32[]{:S(2)}) collective-permute-start(f32[2,128,512]{2,1,0:T(8,128)} %get-tuple-element.13), channel_id=1, source_target_pairs={{4,0},{6,2},{8,4},{10,6},{12,8},{14,10},{16,12},{18,14},{20,16},{2... | collective-permute-start | bytes 1572872 | tf_op jit(solution)/shard_map/ppermute | solution.py:13
  99.8 37.2 %collective-permute-start.7 = (f32[2,128,512]{2,1,0:T(8,128)}, f32[2,128,512]{2,1,0:T(8,128)}, u32[]{:S(2)}, u32[]{:S(2)}) collective-permute-start(f32[2,128,512]{2,1,0:T(8,128)} %get-tuple-element.14), channel_id=1, source_target_pairs={{8,0},{10,2},{12,4},{14,6},{16,8},{18,10},{20,12},{22,14},{24,16},... | collective-permute-start | bytes 1572872 | tf_op jit(solution)/shard_map/ppermute | solution.py:13
  101.1 2.3 %copy-start.8 = (bf16[128,1,4,128]{0,3,2,1:T(8,128)(2,1)S(1)}, bf16[128,1,4,128]{0,3,2,1:T(8,128)(2,1)}, u32[]{:S(2)}) copy-start(bf16[128,1,4,128]{0,3,2,1:T(8,128)(2,1)} %fusion.44) | copy-start | bytes 393220
  101.1 49.2 %collective-permute-start.6 = (f32[2,128,512]{2,1,0:T(8,128)}, f32[2,128,512]{2,1,0:T(8,128)}, u32[]{:S(2)}, u32[]{:S(2)}) collective-permute-start(f32[2,128,512]{2,1,0:T(8,128)} %get-tuple-element.15), channel_id=1, source_target_pairs={{6,0},{8,2},{10,4},{12,6},{14,8},{16,10},{18,12},{20,14},{22,16},{... | collective-permute-start | bytes 1572872 | tf_op jit(solution)/shard_map/ppermute | solution.py:13
where the time goes:
time: 153 us
  waiting for transfers between devices  48.4 us (32%)
  blocking collectives  47.4 us (31%)
  starting transfers between devices  20.5 us (13%)
  matrix products  12.5 us (8%)
  local copies, waits for them, and re-layouts  12.1 us (8%)
  other arithmetic  10.8 us (7%)
    ppermute x8, waiting for transfers between devices, passed_along(): lax.ppermute(value, axis, [(source, source + steps) for source in range(i...  48.4 us
    psum x1, blocking collectives, local(): grad_sinks = lax.psum(jnp.concatenate(sink_parts), ('ctx', 'dp'))  47.4 us
    ppermute x8, starting transfers between devices, passed_along(): lax.ppermute(value, axis, [(source, source + steps) for source in range(i...  20.5 us
    unnamed x33, local copies, waits for them, and re-layouts  7.73 us
    dot_general x4, matrix products, local(): jnp.einsum('gtk,tgd->kd', probs, g_part, preferred_element_type=jnp.float32)  4.31 us
  transfers between devices with their start and end apart: 8, of which 5 were waited for; matrix products, arithmetic and copies ran while one was open for 6% of the time, Pallas kernels for 0%

commit v1 on v0

v1 whole, which is shorter than its diff:
```python
import functools

import jax
import jax.numpy as jnp
from jax import lax
from jax.experimental import pallas as pl
from jax.experimental.pallas import tpu as pltpu
from jax.sharding import PartitionSpec as P

WINDOW = 512
LOG2E = 1.4426950408889634
PARTS = 1

F32 = jnp.float32
BF16 = jnp.bfloat16


def dot_nt(a, b):
    return lax.dot_general(a, b, (((1,), (1,)), ((), ())), preferred_element_type=F32)


def dot_nn(a, b):
    return lax.dot_general(a, b, (((1,), (0,)), ((), ())), preferred_element_type=F32)


def dot_tn(a, b):
    return lax.dot_general(a, b, (((0,), (0,)), ((), ())), preferred_element_type=F32)


def attention_kernel(
    part, kv_heads, group, reach, rows, size,
    place_ref, docs_ref, sinks_ref, q_ref, g_ref, k_ref, v_ref, *refs,
):
    received, outs = refs[:reach], refs[reach:]
    if part:
        outs = outs[1:]
    dq_ref, dsink_ref, own_ref, zown_ref = outs[:4]
    message_refs = outs[4:]
    place = place_ref[0]
    slot = lax.rem(place, reach)
    doc = docs_ref[0, place]

    def same_doc(distance):
        other = docs_ref[0, jnp.maximum(place - distance, 0)]
        return jnp.logical_and(place >= distance, other == doc)

    in_plane = []
    for step in range(1, reach):
        partner = lax.bitwise_xor(slot, step)
        in_plane.append(same_doc(lax.rem(slot - partner + reach, reach)))
    z_cap = jnp.where(same_doc(reach), jnp.inf, -jnp.inf)
    scale = size ** (-0.5)
    to_log2 = scale * LOG2E
    columns = group * rows
    key_at = lax.broadcasted_iota(jnp.int32, (rows, columns), 0)
    query_at = lax.rem(lax.broadcasted_iota(jnp.int32, (rows, columns), 1), rows)
    causal = key_at <= query_at
    lane = lax.broadcasted_iota(jnp.int32, (1, 128), 1)
    sink_row = jnp.zeros((1, 128), F32)
    width = kv_heads * size

    for head in range(kv_heads):
        cut = slice(head * size, (head + 1) * size)
        cut_v = slice(width + head * size, width + (head + 1) * size)
        members = [slice((head * group + j) * size, (head * group + j + 1) * size) for j in range(group)]
        q = jnp.concatenate([q_ref[:, m] for m in members], axis=0)
        g = jnp.concatenate([g_ref[:, m] for m in members], axis=0)
        keys = jnp.concatenate([k_ref[:, cut]] + [r[:, cut] for r in received], axis=0)
        values = jnp.concatenate([v_ref[:, cut]] + [r[:, cut_v] for r in received], axis=0)
        scores = dot_nt(keys, q)
        gprobs = dot_nt(values, g)

        def block(x, i):
            return x[i * rows:(i + 1) * rows]

        s_blocks = [jnp.where(causal, block(scores, 0), jnp.minimum(block(scores, reach), z_cap))]
        t_blocks = [jnp.where(causal, block(gprobs, 0), block(gprobs, reach))]
        for i in range(1, reach):
            s_blocks.append(block(scores, i))
            t_blocks.append(block(gprobs, i))
        flags = [None] + in_plane
        top = jnp.concatenate(
            [jnp.full((1, rows), sinks_ref[(part * kv_heads + head) * group + j] * LOG2E, F32) for j in range(group)],
            axis=1,
        )
        sink_log = top
        for s, flag in zip(s_blocks, flags):
            high = jnp.max(s, axis=0, keepdims=True) * to_log2
            top = jnp.maximum(top, high if flag is None else jnp.where(flag, high, -jnp.inf))
        sink_weight = jnp.exp2(sink_log - top)
        summed = sink_weight
        raised = []
        for s, flag in zip(s_blocks, flags):
            e = jnp.exp2(s * to_log2 - (top if flag is None else jnp.where(flag, top, jnp.inf)))
            summed = summed + jnp.sum(e, axis=0, keepdims=True)
            raised.append(e)
        inverse = 1.0 / summed
        probs = [(e * inverse).astype(BF16) for e in raised]
        delta = jnp.zeros((1, columns), F32)
        for p, t in zip(probs, t_blocks):
            delta = delta + jnp.sum(p.astype(F32) * t, axis=0, keepdims=True)
        gscores = [(p.astype(F32) * (t - delta)).astype(BF16) for p, t in zip(probs, t_blocks)]
        zero = jnp.zeros((), BF16)
        p_all = jnp.concatenate(
            [jnp.where(causal, probs[0], zero)] + probs[1:] + [jnp.where(causal, zero, probs[0])], axis=0
        )
        d_all = jnp.concatenate(
            [jnp.where(causal, gscores[0], zero)] + gscores[1:] + [jnp.where(causal, zero, gscores[0])], axis=0
        )
        dv = dot_nn(p_all, g)
        dk = dot_nn(d_all, q) * scale
        dq = (dot_tn(d_all, keys) * scale).astype(BF16)
        for j, m in enumerate(members):
            dq_ref[:, m] = dq[j * rows:(j + 1) * rows]
        own_ref[:, cut] = block(dk, 0)
        own_ref[:, cut_v] = block(dv, 0)
        zown_ref[:, cut] = block(dk, reach)
        zown_ref[:, cut_v] = block(dv, reach)
        for i, ref in enumerate(message_refs):
            ref[:, cut] = block(dk, i + 1).astype(BF16)
            ref[:, cut_v] = block(dv, i + 1).astype(BF16)
        sink_terms = sink_weight * inverse * delta
        for j in range(group):
            term = jnp.sum(sink_terms[:, j * rows:(j + 1) * rows], axis=1, keepdims=True)
            at = (part * kv_heads + head) * group + j
            sink_row = jnp.where(lane == at, -term, sink_row)
    dsink_ref[...] = sink_row


def attention(part, reach, place, docs, sinks, queries, grad_out, keys, values, received, earlier):
    rows, q_width = queries.shape
    size = q_width // sinks.shape[0]
    kv_width = keys.shape[1] // PARTS
    kv_heads = kv_width // size
    group = sinks.shape[0] * size // keys.shape[1]
    smem = pl.BlockSpec(memory_space=pltpu.SMEM)

    def columns(width, at):
        return pl.BlockSpec((rows, width), lambda i: (0, at))

    q_spec = columns(q_width // PARTS, part)
    kv_spec = columns(kv_width, part)
    pair_spec = columns(2 * kv_width, 0)
    in_specs = [smem] * 3 + [q_spec] * 2 + [kv_spec] * 2 + [pair_spec] * reach
    operands = [place, docs, sinks, queries, grad_out, keys, values, *received]
    aliases = {}
    if part:
        aliases = {len(operands): 0}
        in_specs.append(pl.BlockSpec(memory_space=pl.ANY))
        operands.append(earlier)
    wide = jax.ShapeDtypeStruct((rows, 2 * kv_width), F32)
    narrow = jax.ShapeDtypeStruct((rows, 2 * kv_width), BF16)
    return pl.pallas_call(
        functools.partial(attention_kernel, part, kv_heads, group, reach, rows, size),
        grid=(1,),
        out_shape=[
            jax.ShapeDtypeStruct(queries.shape, BF16), jax.ShapeDtypeStruct((1, 128), F32), wide, wide,
        ] + [narrow] * (reach - 1),
        in_specs=in_specs,
        out_specs=[q_spec, pl.BlockSpec((1, 128), lambda i: (0, 0)), pair_spec, pair_spec]
        + [pair_spec] * (reach - 1),
        input_output_aliases=aliases,
        compiler_params=pltpu.CompilerParams(vmem_limit_bytes=48 * 1024 * 1024),
        cost_estimate=pl.CostEstimate(
            flops=10 * rows * group * rows * (reach + 1) * size * kv_heads,
            bytes_accessed=6 * rows * q_width // PARTS + 20 * rows * reach * kv_width,
            transcendentals=rows * group * rows * reach * kv_heads,
        ),
    )(*operands)


def local(queries, keys, values, grad_out, sinks, doc_ids):
    rows = queries.shape[1]
    reach = WINDOW // rows
    count = lax.axis_size("ctx")
    place = lax.axis_index("ctx")
    slot = lax.rem(place, reach)
    queries, keys, values, grad_out = queries[0], keys[0], values[0], grad_out[0]
    kv_width = keys.shape[1] // PARTS

    def along(x, distance):
        first, last = max(0, -distance), min(count, count - distance)
        return lax.ppermute(x, "ctx", [(i, i + distance) for i in range(first, last)])

    def exchanged(x, step, axis="ctx"):
        return lax.ppermute(x, axis, [(i, i ^ step) for i in range(lax.axis_size(axis))])

    own = [
        jnp.concatenate([x[:, p * kv_width:(p + 1) * kv_width] for x in (keys, values)], axis=1) for p in range(PARTS)
    ]
    received = []
    for p in range(PARTS):
        before = along(own[p], reach)
        arrived = []
        for step in range(1, reach):
            send_own = lax.bitwise_xor(slot, step) > slot
            arrived.append(exchanged(jnp.where(send_own, own[p], before), step))
        received.append(arrived + [before])
    place_row = jnp.full((1,), place, jnp.int32)
    grad_queries = None
    sink_row = jnp.zeros((1, 128), F32)
    shares = []
    for p in range(PARTS):
        grad_queries, sink_part, *share = attention(
            p, reach, place_row, doc_ids, sinks, queries, grad_out, keys, values, received[p], grad_queries
        )
        sink_row = sink_row + sink_part
        shares.append(share)
    totals = []
    for own_sum, before_sum, *messages in shares:
        for step, message in enumerate(messages, 1):
            back = exchanged(message, step).astype(F32)
            mine = lax.bitwise_xor(slot, step) > slot
            own_sum = own_sum + jnp.where(mine, back, 0.0)
            before_sum = before_sum + jnp.where(mine, 0.0, back)
        totals.append((own_sum, along(before_sum.astype(BF16), -reach)))
    sink_row = sink_row + exchanged(sink_row, 1, "dp") if lax.axis_size("dp") == 2 else lax.psum(sink_row, "dp")
    step = 1
    while step < count:
        sink_row = sink_row + exchanged(sink_row, step)
        step *= 2
    whole = [own_sum + last.astype(F32) for own_sum, last in totals]
    grad_keys = jnp.concatenate([w[:, :kv_width] for w in whole], axis=1).astype(BF16)
    grad_values = jnp.concatenate([w[:, kv_width:] for w in whole], axis=1).astype(BF16)
    return grad_queries[None], grad_keys[None], grad_values[None], sink_row[0, : sinks.shape[0]]


def solution(mesh):
    blocks = P("dp", "ctx", None)
    in_specs = (blocks, blocks, blocks, blocks, P(), P("dp", None))
    out_specs = (blocks, blocks, blocks, P())
    return jax.shard_map(local, mesh=mesh, in_specs=in_specs, out_specs=out_specs, check_vma=False)
```

time: 153 us -> 69 us (0.45)
  the two profiles are of different devices: /device:TPU:2 before, /device:TPU:0 now
where the time goes in v1:
time: 69 us; the launch traced here: 68.8 us
  waiting for transfers between devices  37.6 us (54%)
  starting transfers between devices  20.8 us (30%)
  Pallas kernels  6.17 us (9%)
  local copies, waits for them, and re-layouts  1.91 us (3%)
  other arithmetic  1.6 us (2%)
  between operations  0.75 us (1%)
    ppermute x11, waiting for transfers between devices, exchanged(): lax.ppermute(x, axis, [(i, i ^ step) for i in range(lax.axis_size(axis))])  32.1 us
    ppermute x11, starting transfers between devices, exchanged(): lax.ppermute(x, axis, [(i, i ^ step) for i in range(lax.axis_size(axis))])  14.6 us
    ppermute x2, starting transfers between devices, along(): lax.ppermute(x, 'ctx', [(i, i + distance) for i in range(first, last)])  6.24 us
    pallas_call x1, Pallas kernels, attention(): pl.pallas_call(functools.partial(attention_kernel, part, kv_heads, group,...  6.17 us
    ppermute x2, waiting for transfers between devices, along(): lax.ppermute(x, 'ctx', [(i, i + distance) for i in range(first, last)])  5.5 us
  transfers between devices with their start and end apart: 13, of which 11 were waited for; matrix products, arithmetic and copies ran while one was open for 1% of the time, Pallas kernels for 0%

profile of v1, /device:TPU:0, one launch (start us, length us, event | category | flops | bytes accessed | tf_op | source)
XLA Modules:
  0.0 68.8 jit_solution(18046302767011081818)
XLA Ops:
  0.7 1.0 %pad_maximum_fusion = bf16[128,1024]{1,0:T(8,128)(2,1)S(1)} fusion(bf16[128,512]{1,0:T(8,128)(2,1)} %bitcast.15, bf16[128,512]{1,0:T(8,128)(2,1)} %bitcast.12), kind=kLoop, calls=%fused_computation.15 | loop fusion | flops 524288 | bytes 524288 | tf_op jit(solution)/shard_map/concatenate | solution.py:189
  1.7 4.9 %collective-permute-start = (bf16[128,1024]{1,0:T(8,128)(2,1)S(1)}, bf16[128,1024]{1,0:T(8,128)(2,1)S(1)}, u32[]{:S(2)}, u32[]{:S(2)}) collective-permute-start(bf16[128,1024]{1,0:T(8,128)(2,1)S(1)} %pad_maximum_fusion), channel_id=1, source_target_pairs={{0,8},{2,10},{4,12},{6,14},{8,16},{10,18},{12,20},{14,22},{16,24},... | collective-permute-start | bytes 786440 | tf_op jit(solution)/shard_map/ppermute | solution.py:183
  6.7 5.5 %collective-permute-done.refs_3_ = bf16[128,1024]{1,0:T(8,128)(2,1)S(1)} collective-permute-done((bf16[128,1024]{1,0:T(8,128)(2,1)S(1)}, bf16[128,1024]{1,0:T(8,128)(2,1)S(1)}, u32[]{:S(2)}, u32[]{:S(2)}) %collective-permute-start) | collective-permute-done | bytes 262176 | tf_op jit(solution)/shard_map/ppermute | solution.py:183
  12.2 0.2 broadcast_select_fusion
  12.3 2.5 %collective-permute-start.3 = (bf16[128,1024]{1,0:T(8,128)(2,1)S(1)}, bf16[128,1024]{1,0:T(8,128)(2,1)S(1)}, u32[]{:S(2)}, u32[]{:S(2)}) collective-permute-start(bf16[128,1024]{1,0:T(8,128)(2,1)S(1)} %get-tuple-element.18), channel_id=1, source_target_pairs={{0,6},{2,4},{4,2},{6,0},{8,14},{10,12},{12,10},{14,8},{16,22},{18,... | collective-permute-start | bytes 786440 | tf_op jit(solution)/shard_map/ppermute | solution.py:186
  14.8 0.5 collective-permute-start.2
  15.4 0.5 collective-permute-start.1
  15.9 6.7 %collective-permute-done.3.refs_2_ = bf16[128,1024]{1,0:T(8,128)(2,1)S(1)} collective-permute-done((bf16[128,1024]{1,0:T(8,128)(2,1)S(1)}, bf16[128,1024]{1,0:T(8,128)(2,1)S(1)}, u32[]{:S(2)}, u32[]{:S(2)}) %collective-permute-start.3) | collective-permute-done | bytes 262176 | tf_op jit(solution)/shard_map/ppermute | solution.py:186
  22.6 3.5 %collective-permute-done.2.refs_1_ = bf16[128,1024]{1,0:T(8,128)(2,1)S(1)} collective-permute-done((bf16[128,1024]{1,0:T(8,128)(2,1)S(1)}, bf16[128,1024]{1,0:T(8,128)(2,1)S(1)}, u32[]{:S(2)}, u32[]{:S(2)}) %collective-permute-start.2) | collective-permute-done | bytes 262176 | tf_op jit(solution)/shard_map/ppermute | solution.py:186
  26.1 0.1 collective-permute-done.1.refs_0_
  26.2 0.6 copy-done.4
  26.9 6.2 %shard_map.93 = (bf16[128,2048]{1,0:T(8,128)(2,1)}, f32[1,128]{1,0:T(1,128)S(1)}, f32[128,1024]{1,0:T(8,128)S(1)}, f32[128,1024]{1,0:T(8,128)S(1)}, bf16[128,102...) custom-call(s32[1]{0:T(128)} %bitcast.place_ref, s32[1,16]{1,0:T(1,128)S(1)} %copy-done.4, ...), custom_call_target="tpu_custom_call" | custom-call | flops 1677721600 | bytes 6815744 | tf_op jit(solution)/shard_map/pallas_call | solution.py:153
  33.0 1.5 %collective-permute-start.4 = (bf16[128,1024]{1,0:T(8,128)(2,1)S(1)}, bf16[128,1024]{1,0:T(8,128)(2,1)S(1)}, u32[]{:S(2)}, u32[]{:S(2)}) collective-permute-start(bf16[128,1024]{1,0:T(8,128)(2,1)S(1)} %get-tuple-element.13), channel_id=1, source_target_pairs={{0,2},{2,0},{4,6},{6,4},{8,10},{10,8},{12,14},{14,12},{16,18},{18,... | collective-permute-start | bytes 786440 | tf_op jit(solution)/shard_map/ppermute | solution.py:186
  34.5 0.7 %collective-permute-start.5 = (bf16[128,1024]{1,0:T(8,128)(2,1)S(1)}, bf16[128,1024]{1,0:T(8,128)(2,1)S(1)}, u32[]{:S(2)}, u32[]{:S(2)}) collective-permute-start(bf16[128,1024]{1,0:T(8,128)(2,1)S(1)} %get-tuple-element.14), channel_id=1, source_target_pairs={{0,4},{2,6},{4,0},{6,2},{8,12},{10,14},{12,8},{14,10},{16,20},{18,... | collective-permute-start | bytes 786440 | tf_op jit(solution)/shard_map/ppermute | solution.py:186
  35.2 1.3 %collective-permute-start.6 = (bf16[128,1024]{1,0:T(8,128)(2,1)S(1)}, bf16[128,1024]{1,0:T(8,128)(2,1)S(1)}, u32[]{:S(2)}, u32[]{:S(2)}) collective-permute-start(bf16[128,1024]{1,0:T(8,128)(2,1)S(1)} %get-tuple-element.15), channel_id=1, source_target_pairs={{0,6},{2,4},{4,2},{6,0},{8,14},{10,12},{12,10},{14,8},{16,22},{18,... | collective-permute-start | bytes 786440 | tf_op jit(solution)/shard_map/ppermute | solution.py:186
  36.5 5.7 %collective-permute-done.4 = bf16[128,1024]{1,0:T(8,128)(2,1)S(1)} collective-permute-done((bf16[128,1024]{1,0:T(8,128)(2,1)S(1)}, bf16[128,1024]{1,0:T(8,128)(2,1)S(1)}, u32[]{:S(2)}, u32[]{:S(2)}) %collective-permute-start.4) | collective-permute-done | bytes 262176 | tf_op jit(solution)/shard_map/ppermute | solution.py:186
  42.2 5.8 %collective-permute-done.5 = bf16[128,1024]{1,0:T(8,128)(2,1)S(1)} collective-permute-done((bf16[128,1024]{1,0:T(8,128)(2,1)S(1)}, bf16[128,1024]{1,0:T(8,128)(2,1)S(1)}, u32[]{:S(2)}, u32[]{:S(2)}) %collective-permute-start.5) | collective-permute-done | bytes 262176 | tf_op jit(solution)/shard_map/ppermute | solution.py:186
  48.0 0.2 fusion.8
  48.2 1.3 %collective-permute-start.7 = (bf16[128,1024]{1,0:T(8,128)(2,1)S(1)}, bf16[128,1024]{1,0:T(8,128)(2,1)S(1)}, u32[]{:S(2)}, u32[]{:S(2)}) collective-permute-start(bf16[128,1024]{1,0:T(8,128)(2,1)S(1)} %fusion.8), channel_id=1, source_target_pairs={{8,0},{10,2},{12,4},{14,6},{16,8},{18,10},{20,12},{22,14},{24,16},... | collective-permute-start | bytes 786440 | tf_op jit(solution)/shard_map/ppermute | solution.py:183
  49.5 0.1 collective-permute-start.8
  49.5 1.1 %collective-permute-done.8 = f32[1,128]{1,0:T(1,128)S(1)} collective-permute-done((f32[1,128]{1,0:T(1,128)S(1)}, f32[1,128]{1,0:T(1,128)S(1)}, u32[]{:S(2)}, u32[]{:S(2)}) %collective-permute-start.8) | collective-permute-done | bytes 544 | tf_op jit(solution)/shard_map/ppermute | solution.py:186
  50.7 0.5 collective-permute-start.9
  51.2 3.0 %collective-permute-done.9 = f32[1,128]{1,0:T(1,128)S(1)} collective-permute-done((f32[1,128]{1,0:T(1,128)S(1)}, f32[1,128]{1,0:T(1,128)S(1)}, u32[]{:S(2)}, u32[]{:S(2)}) %collective-permute-start.9) | collective-permute-done | bytes 544 | tf_op jit(solution)/shard_map/ppermute | solution.py:186
  54.2 0.3 collective-permute-start.10
  54.5 3.2 %collective-permute-done.10 = f32[1,128]{1,0:T(1,128)S(1)} collective-permute-done((f32[1,128]{1,0:T(1,128)S(1)}, f32[1,128]{1,0:T(1,128)S(1)}, u32[]{:S(2)}, u32[]{:S(2)}) %collective-permute-start.10) | collective-permute-done | bytes 544 | tf_op jit(solution)/shard_map/ppermute | solution.py:186
  57.8 3.1 %collective-permute-start.11 = (f32[1,128]{1,0:T(1,128)S(1)}, f32[1,128]{1,0:T(1,128)S(1)}, u32[]{:S(2)}, u32[]{:S(2)}) collective-permute-start(f32[1,128]{1,0:T(1,128)S(1)} %add.45), channel_id=1, source_target_pairs={{0,8},{2,10},{4,12},{6,14},{8,0},{10,2},{12,4},{14,6},{16,24},{18,... | collective-permute-start | bytes 1544 | tf_op jit(solution)/shard_map/ppermute | solution.py:186
  60.9 1.5 %collective-permute-done.11 = f32[1,128]{1,0:T(1,128)S(1)} collective-permute-done((f32[1,128]{1,0:T(1,128)S(1)}, f32[1,128]{1,0:T(1,128)S(1)}, u32[]{:S(2)}, u32[]{:S(2)}) %collective-permute-start.11) | collective-permute-done | bytes 544 | tf_op jit(solution)/shard_map/ppermute | solution.py:186
  62.4 3.5 %collective-permute-start.12 = (f32[1,128]{1,0:T(1,128)S(1)}, f32[1,128]{1,0:T(1,128)S(1)}, u32[]{:S(2)}, u32[]{:S(2)}) collective-permute-start(f32[1,128]{1,0:T(1,128)S(1)} %add.46), channel_id=1, source_target_pairs={{0,16},{2,18},{4,20},{6,22},{8,24},{10,26},{12,28},{14,30},{16,0},... | collective-permute-start | bytes 1544 | tf_op jit(solution)/shard_map/ppermute | solution.py:186
  65.9 1.5 %collective-permute-done.12 = f32[1,128]{1,0:T(1,128)S(1)} collective-permute-done((f32[1,128]{1,0:T(1,128)S(1)}, f32[1,128]{1,0:T(1,128)S(1)}, u32[]{:S(2)}, u32[]{:S(2)}) %collective-permute-start.12) | collective-permute-done | bytes 544 | tf_op jit(solution)/shard_map/ppermute | solution.py:186
  67.4 0.5 slice_bitcast_fusion.2
  67.9 0.2 fusion.4
  68.1 0.7 %slice_bitcast_fusion = (bf16[1,128,512]{2,1,0:T(8,128)(2,1)}, bf16[1,128,512]{2,1,0:T(8,128)(2,1)}) fusion(bf16[128,1024]{1,0:T(8,128)(2,1)S(1)} %fusion.4), kind=kLoop, calls=%fused_computation.19 | loop fusion | bytes 524288 | tf_op jit(solution)/shard_map/broadcast_in_dim | solution.py:225
  (18 shorter events, 0.1 us)
Async XLA Ops:
  0.6 11.5 %copy-start = (bf16[1,128,512]{2,1,0:T(8,128)(2,1)S(1)}, bf16[1,128,512]{2,1,0:T(8,128)(2,1)}, u32[]{:S(2)}) copy-start(bf16[1,128,512]{2,1,0:T(8,128)(2,1)} %param.7) | copy-start | bytes 393220
  0.6 11.5 %copy-start.1 = (bf16[1,128,512]{2,1,0:T(8,128)(2,1)S(1)}, bf16[1,128,512]{2,1,0:T(8,128)(2,1)}, u32[]{:S(2)}) copy-start(bf16[1,128,512]{2,1,0:T(8,128)(2,1)} %param.8) | copy-start | bytes 393220
  1.7 10.5 %collective-permute-start = (bf16[128,1024]{1,0:T(8,128)(2,1)S(1)}, bf16[128,1024]{1,0:T(8,128)(2,1)S(1)}, u32[]{:S(2)}, u32[]{:S(2)}) collective-permute-start(bf16[128,1024]{1,0:T(8,128)(2,1)S(1)} %pad_maximum_fusion), channel_id=1, source_target_pairs={{0,8},{2,10},{4,12},{6,14},{8,16},{10,18},{12,20},{14,22},{16,24},... | collective-permute-start | bytes 786440 | tf_op jit(solution)/shard_map/ppermute | solution.py:183
  6.7 19.5 %copy-start.2 = (bf16[1,128,2048]{2,1,0:T(8,128)(2,1)S(1)}, bf16[1,128,2048]{2,1,0:T(8,128)(2,1)}, u32[]{:S(2)}) copy-start(bf16[1,128,2048]{2,1,0:T(8,128)(2,1)} %param.6) | copy-start | bytes 1572868
  6.7 19.5 %copy-start.3 = (bf16[1,128,2048]{2,1,0:T(8,128)(2,1)S(1)}, bf16[1,128,2048]{2,1,0:T(8,128)(2,1)}, u32[]{:S(2)}) copy-start(bf16[1,128,2048]{2,1,0:T(8,128)(2,1)} %param.9) | copy-start | bytes 1572868
  12.3 10.3 %collective-permute-start.3 = (bf16[128,1024]{1,0:T(8,128)(2,1)S(1)}, bf16[128,1024]{1,0:T(8,128)(2,1)S(1)}, u32[]{:S(2)}, u32[]{:S(2)}) collective-permute-start(bf16[128,1024]{1,0:T(8,128)(2,1)S(1)} %get-tuple-element.18), channel_id=1, source_target_pairs={{0,6},{2,4},{4,2},{6,0},{8,14},{10,12},{12,10},{14,8},{16,22},{18,... | collective-permute-start | bytes 786440 | tf_op jit(solution)/shard_map/ppermute | solution.py:186
  14.8 11.2 %collective-permute-start.2 = (bf16[128,1024]{1,0:T(8,128)(2,1)S(1)}, bf16[128,1024]{1,0:T(8,128)(2,1)S(1)}, u32[]{:S(2)}, u32[]{:S(2)}) collective-permute-start(bf16[128,1024]{1,0:T(8,128)(2,1)S(1)} %get-tuple-element.19), channel_id=1, source_target_pairs={{0,4},{2,6},{4,0},{6,2},{8,12},{10,14},{12,8},{14,10},{16,20},{18,... | collective-permute-start | bytes 786440 | tf_op jit(solution)/shard_map/ppermute | solution.py:186
  15.4 10.8 %collective-permute-start.1 = (bf16[128,1024]{1,0:T(8,128)(2,1)S(1)}, bf16[128,1024]{1,0:T(8,128)(2,1)S(1)}, u32[]{:S(2)}, u32[]{:S(2)}) collective-permute-start(bf16[128,1024]{1,0:T(8,128)(2,1)S(1)} %get-tuple-element.20), channel_id=1, source_target_pairs={{0,2},{2,0},{4,6},{6,4},{8,10},{10,8},{12,14},{14,12},{16,18},{18,... | collective-permute-start | bytes 786440 | tf_op jit(solution)/shard_map/ppermute | solution.py:186
  26.2 0.7 copy-start.4
  26.2 0.7 copy-start.5
  33.0 9.2 %collective-permute-start.4 = (bf16[128,1024]{1,0:T(8,128)(2,1)S(1)}, bf16[128,1024]{1,0:T(8,128)(2,1)S(1)}, u32[]{:S(2)}, u32[]{:S(2)}) collective-permute-start(bf16[128,1024]{1,0:T(8,128)(2,1)S(1)} %get-tuple-element.13), channel_id=1, source_target_pairs={{0,2},{2,0},{4,6},{6,4},{8,10},{10,8},{12,14},{14,12},{16,18},{18,... | collective-permute-start | bytes 786440 | tf_op jit(solution)/shard_map/ppermute | solution.py:186
  34.5 13.5 %collective-permute-start.5 = (bf16[128,1024]{1,0:T(8,128)(2,1)S(1)}, bf16[128,1024]{1,0:T(8,128)(2,1)S(1)}, u32[]{:S(2)}, u32[]{:S(2)}) collective-permute-start(bf16[128,1024]{1,0:T(8,128)(2,1)S(1)} %get-tuple-element.14), channel_id=1, source_target_pairs={{0,4},{2,6},{4,0},{6,2},{8,12},{10,14},{12,8},{14,10},{16,20},{18,... | collective-permute-start | bytes 786440 | tf_op jit(solution)/shard_map/ppermute | solution.py:186
  35.2 12.7 %collective-permute-start.6 = (bf16[128,1024]{1,0:T(8,128)(2,1)S(1)}, bf16[128,1024]{1,0:T(8,128)(2,1)S(1)}, u32[]{:S(2)}, u32[]{:S(2)}) collective-permute-start(bf16[128,1024]{1,0:T(8,128)(2,1)S(1)} %get-tuple-element.15), channel_id=1, source_target_pairs={{0,6},{2,4},{4,2},{6,0},{8,14},{10,12},{12,10},{14,8},{16,22},{18,... | collective-permute-start | bytes 786440 | tf_op jit(solution)/shard_map/ppermute | solution.py:186
  48.2 19.7 %collective-permute-start.7 = (bf16[128,1024]{1,0:T(8,128)(2,1)S(1)}, bf16[128,1024]{1,0:T(8,128)(2,1)S(1)}, u32[]{:S(2)}, u32[]{:S(2)}) collective-permute-start(bf16[128,1024]{1,0:T(8,128)(2,1)S(1)} %fusion.8), channel_id=1, source_target_pairs={{8,0},{10,2},{12,4},{14,6},{16,8},{18,10},{20,12},{22,14},{24,16},... | collective-permute-start | bytes 786440 | tf_op jit(solution)/shard_map/ppermute | solution.py:183
  49.5 1.2 %collective-permute-start.8 = (f32[1,128]{1,0:T(1,128)S(1)}, f32[1,128]{1,0:T(1,128)S(1)}, u32[]{:S(2)}, u32[]{:S(2)}) collective-permute-start(f32[1,128]{1,0:T(1,128)S(1)} %get-tuple-element.17), channel_id=1, source_target_pairs={{0,1},{1,0},{2,3},{3,2},{4,5},{5,4},{6,7},{7,6},{8,9},{9,8},{10,11... | collective-permute-start | bytes 1544 | tf_op jit(solution)/shard_map/ppermute | solution.py:186
  50.7 3.5 %collective-permute-start.9 = (f32[1,128]{1,0:T(1,128)S(1)}, f32[1,128]{1,0:T(1,128)S(1)}, u32[]{:S(2)}, u32[]{:S(2)}) collective-permute-start(f32[1,128]{1,0:T(1,128)S(1)} %add.43), channel_id=1, source_target_pairs={{0,2},{2,0},{4,6},{6,4},{8,10},{10,8},{12,14},{14,12},{16,18},{18,... | collective-permute-start | bytes 1544 | tf_op jit(solution)/shard_map/ppermute | solution.py:186
  54.2 3.5 %collective-permute-start.10 = (f32[1,128]{1,0:T(1,128)S(1)}, f32[1,128]{1,0:T(1,128)S(1)}, u32[]{:S(2)}, u32[]{:S(2)}) collective-permute-start(f32[1,128]{1,0:T(1,128)S(1)} %add.44), channel_id=1, source_target_pairs={{0,4},{2,6},{4,0},{6,2},{8,12},{10,14},{12,8},{14,10},{16,20},{18,... | collective-permute-start | bytes 1544 | tf_op jit(solution)/shard_map/ppermute | solution.py:186
  57.8 4.6 %collective-permute-start.11 = (f32[1,128]{1,0:T(1,128)S(1)}, f32[1,128]{1,0:T(1,128)S(1)}, u32[]{:S(2)}, u32[]{:S(2)}) collective-permute-start(f32[1,128]{1,0:T(1,128)S(1)} %add.45), channel_id=1, source_target_pairs={{0,8},{2,10},{4,12},{6,14},{8,0},{10,2},{12,4},{14,6},{16,24},{18,... | collective-permute-start | bytes 1544 | tf_op jit(solution)/shard_map/ppermute | solution.py:186
  62.4 5.0 %collective-permute-start.12 = (f32[1,128]{1,0:T(1,128)S(1)}, f32[1,128]{1,0:T(1,128)S(1)}, u32[]{:S(2)}, u32[]{:S(2)}) collective-permute-start(f32[1,128]{1,0:T(1,128)S(1)} %add.46), channel_id=1, source_target_pairs={{0,16},{2,18},{4,20},{6,22},{8,24},{10,26},{12,28},{14,30},{16,0},... | collective-permute-start | bytes 1544 | tf_op jit(solution)/shard_map/ppermute | solution.py:186

commit v2 on v1

v2 whole, which is shorter than its diff:
```python
import functools

import jax
import jax.numpy as jnp
from jax import lax
from jax.experimental import pallas as pl
from jax.experimental.pallas import tpu as pltpu
from jax.sharding import PartitionSpec as P

WINDOW = 512
LOG2E = 1.4426950408889634
PARTS = 2

F32 = jnp.float32
BF16 = jnp.bfloat16
SMEM = pl.BlockSpec(memory_space=pltpu.SMEM)
VMEM = pl.BlockSpec(memory_space=pltpu.VMEM)


def dot_nt(a, b):
    return lax.dot_general(a, b, (((1,), (1,)), ((), ())), preferred_element_type=F32)


def dot_nn(a, b):
    return lax.dot_general(a, b, (((1,), (0,)), ((), ())), preferred_element_type=F32)


def dot_tn(a, b):
    return lax.dot_general(a, b, (((0,), (0,)), ((), ())), preferred_element_type=F32)


def kernel_call(body, out_shape, in_specs, operands, flops=0, bytes_accessed=0, transcendentals=0, **options):
    return pl.pallas_call(
        body,
        out_shape=out_shape,
        in_specs=in_specs,
        compiler_params=pltpu.CompilerParams(vmem_limit_bytes=24 * 1024 * 1024),
        cost_estimate=pl.CostEstimate(
            flops=flops, bytes_accessed=bytes_accessed, transcendentals=transcendentals
        ),
        **options,
    )(*operands)


def later(slot, step):
    return lax.bitwise_xor(slot, step) > slot


def prepare_kernel(reach, rows, group, place_ref, docs_ref, sinks_ref, k_ref, v_ref, caps_ref, tops_ref, *own_refs):
    place = place_ref[0]
    slot = lax.rem(place, reach)
    doc = docs_ref[0, place]
    width = k_ref.shape[1] // len(own_refs)
    for part, ref in enumerate(own_refs):
        ref[:, :width] = k_ref[:, part * width:(part + 1) * width]
        ref[:, width:] = v_ref[:, part * width:(part + 1) * width]
    columns = caps_ref.shape[1]
    for step in range(1, reach + 1):
        distance = reach
        if step < reach:
            distance = lax.rem(slot - lax.bitwise_xor(slot, step) + reach, reach)
        other = docs_ref[0, jnp.maximum(place - distance, 0)]
        same = jnp.logical_and(place >= distance, other == doc)
        caps_ref[step:step + 1, :] = jnp.full((1, columns), jnp.where(same, jnp.inf, -jnp.inf), F32)
    for head in range(sinks_ref.shape[0] // group):
        for j in range(group):
            tops_ref[head:head + 1, j * rows:(j + 1) * rows] = jnp.full(
                (1, rows), sinks_ref[head * group + j] * LOG2E, F32
            )


def choose_kernel(reach, place_ref, own_ref, before_ref, *out_refs):
    slot = lax.rem(place_ref[0], reach)
    for bit, ref in enumerate(out_refs):
        @pl.when(later(slot, 1 << bit))
        def _():
            ref[...] = own_ref[...]

        @pl.when(jnp.logical_not(later(slot, 1 << bit)))
        def _():
            ref[...] = before_ref[...]


def attention_kernel(part, kv_heads, group, reach, rows, size, caps_ref, tops_ref, q_ref, g_ref, *refs):
    blocks, outs = refs[:reach + 1], refs[reach + 1:]
    if part:
        sink_before, outs = outs[0], outs[1:]
    sink_ref, own_ref, before_ref, gscores_ref = outs[:4]
    message_refs = outs[4:]
    scale = size ** (-0.5)
    to_log2 = scale * LOG2E
    columns = group * rows
    key_at = lax.broadcasted_iota(jnp.int32, (rows, columns), 0)
    query_at = lax.rem(lax.broadcasted_iota(jnp.int32, (rows, columns), 1), rows)
    causal = key_at <= query_at
    lane = lax.broadcasted_iota(jnp.int32, (1, 128), 1)
    sink_row = sink_before[...] if part else jnp.zeros((1, 128), F32)
    width = kv_heads * size
    zero = jnp.zeros((), BF16)

    def block(x, i):
        return x[i * rows:(i + 1) * rows]

    caps = [caps_ref[i:i + 1, :] for i in range(reach + 1)]
    for head in range(kv_heads):
        cut = slice(head * size, (head + 1) * size)
        cut_v = slice(width + head * size, width + (head + 1) * size)
        first = (part * kv_heads + head) * group
        members = [slice((first + j) * size, (first + j + 1) * size) for j in range(group)]
        q = jnp.concatenate([q_ref[:, m] for m in members], axis=0)
        g = jnp.concatenate([g_ref[:, m] for m in members], axis=0)
        keys = jnp.concatenate([r[:, cut] for r in blocks], axis=0)
        values = jnp.concatenate([r[:, cut_v] for r in blocks], axis=0)
        scores = dot_nt(keys, q)
        gprobs = dot_nt(values, g)
        s_blocks = [jnp.where(causal, block(scores, 0), jnp.minimum(block(scores, reach), caps[reach]))]
        t_blocks = [jnp.where(causal, block(gprobs, 0), block(gprobs, reach))]
        for i in range(1, reach):
            s_blocks.append(block(scores, i))
            t_blocks.append(block(gprobs, i))
        top = tops_ref[part * kv_heads + head:part * kv_heads + head + 1, :]
        sink_log = top
        for i, s in enumerate(s_blocks):
            high = jnp.max(s, axis=0, keepdims=True) * to_log2
            top = jnp.maximum(top, jnp.minimum(high, caps[i]) if i else high)
        sink_weight = jnp.exp2(sink_log - top)
        summed = sink_weight
        raised = []
        for i, s in enumerate(s_blocks):
            e = jnp.exp2(s * to_log2 - (jnp.maximum(top, -caps[i]) if i else top))
            summed = summed + jnp.sum(e, axis=0, keepdims=True)
            raised.append(e)
        inverse = 1.0 / summed
        probs = [(e * inverse).astype(BF16) for e in raised]
        delta = jnp.zeros((1, columns), F32)
        for p, t in zip(probs, t_blocks):
            delta = delta + jnp.sum(p.astype(F32) * t, axis=0, keepdims=True)
        gscores = [(p.astype(F32) * (t - delta)).astype(BF16) for p, t in zip(probs, t_blocks)]
        p_all = jnp.concatenate(
            [jnp.where(causal, probs[0], zero)] + probs[1:] + [jnp.where(causal, zero, probs[0])], axis=0
        )
        d_all = jnp.concatenate(
            [jnp.where(causal, gscores[0], zero)] + gscores[1:] + [jnp.where(causal, zero, gscores[0])], axis=0
        )
        dv = dot_nn(p_all, g)
        dk = dot_nn(d_all, q) * scale
        gscores_ref[head * (reach + 1) * rows:(head + 1) * (reach + 1) * rows, :] = d_all
        own_ref[:, cut] = block(dk, 0)
        own_ref[:, cut_v] = block(dv, 0)
        before_ref[:, cut] = block(dk, reach)
        before_ref[:, cut_v] = block(dv, reach)
        for i, ref in enumerate(message_refs):
            ref[:, cut] = block(dk, i + 1).astype(BF16)
            ref[:, cut_v] = block(dv, i + 1).astype(BF16)
        sink_terms = sink_weight * inverse * delta
        for j in range(group):
            term = jnp.sum(sink_terms[:, j * rows:(j + 1) * rows], axis=1, keepdims=True)
            sink_row = jnp.where(lane == first + j, -term, sink_row)
    sink_ref[...] = sink_row


def queries_kernel(kv_heads, group, reach, rows, size, *refs):
    parts = len(refs) // (reach + 2)
    *ins, dq_ref, done_ref = refs
    scale = size ** (-0.5)
    span = (reach + 1) * rows
    for part in range(parts):
        gscores_ref, *blocks = ins[part * (reach + 2):(part + 1) * (reach + 2)]
        for head in range(kv_heads):
            cut = slice(head * size, (head + 1) * size)
            keys = jnp.concatenate([r[:, cut] for r in blocks], axis=0)
            dq = (dot_tn(gscores_ref[head * span:(head + 1) * span, :], keys) * scale).astype(BF16)
            for j in range(group):
                at = ((part * kv_heads + head) * group + j) * size
                dq_ref[:, at:at + size] = dq[j * rows:(j + 1) * rows]
    done_ref[...] = jnp.zeros_like(done_ref)


def combine_kernel(reach, place_ref, pass_ref, own_ref, before_ref, *refs):
    *messages, own_out, before_out, pass_out = refs
    slot = lax.rem(place_ref[0], reach)
    own, before = own_ref[...], before_ref[...]
    for step, message in enumerate(messages, 1):
        mine = later(slot, step)
        back = message[...].astype(F32)
        own = own + jnp.where(mine, back, 0.0)
        before = before + jnp.where(mine, 0.0, back)
    own_out[...] = own
    before_out[...] = before.astype(BF16)
    pass_out[...] = pass_ref[...]


def finish_kernel(parts, sink_ref, *refs):
    owns, lasts = refs[:parts], refs[parts:2 * parts]
    dk_ref, dv_ref, dsink_ref = refs[2 * parts:]
    width = dk_ref.shape[1] // parts
    for part in range(parts):
        total = owns[part][...] + lasts[part][...].astype(F32)
        cut = slice(part * width, (part + 1) * width)
        dk_ref[:, cut] = total[:, :width].astype(BF16)
        dv_ref[:, cut] = total[:, width:].astype(BF16)
    dsink_ref[...] = sink_ref[0, :dsink_ref.shape[0]]


def local(queries, keys, values, grad_out, sinks, doc_ids):
    rows, q_width = queries.shape[1:]
    kv_width = keys.shape[2]
    heads = sinks.shape[0]
    size = q_width // heads
    group = q_width // kv_width
    kv_heads = kv_width // size // PARTS
    reach = WINDOW // rows
    count = lax.axis_size("ctx")
    place = jnp.full((1,), lax.axis_index("ctx"), jnp.int32)
    queries, keys, values, grad_out = queries[0], keys[0], values[0], grad_out[0]
    wide = jax.ShapeDtypeStruct((rows, 2 * kv_width // PARTS), F32)
    narrow = jax.ShapeDtypeStruct(wide.shape, BF16)
    row = jax.ShapeDtypeStruct((1, 128), F32)
    table = jax.ShapeDtypeStruct((8 * (-(-max(reach + 1, heads // group) // 8)), group * rows), F32)
    span = (reach + 1) * rows

    def along(x, distance):
        first, last = max(0, -distance), min(count, count - distance)
        return lax.ppermute(x, "ctx", [(i, i + distance) for i in range(first, last)])

    def exchanged(x, step, axis="ctx"):
        return lax.ppermute(x, axis, [(i, i ^ step) for i in range(lax.axis_size(axis))])

    caps, tops, *own = kernel_call(
        functools.partial(prepare_kernel, reach, rows, group),
        [table, table] + [narrow] * PARTS,
        [SMEM] * 3 + [VMEM] * 2,
        (place, doc_ids, sinks, keys, values),
        bytes_accessed=8 * rows * kv_width,
    )
    bits = reach.bit_length() - 1
    before = [along(x, reach) for x in own]
    blocks = []
    for p in range(PARTS):
        chosen = kernel_call(
            functools.partial(choose_kernel, reach),
            [narrow] * bits,
            [SMEM] + [VMEM] * 2,
            (place, own[p], before[p]),
            bytes_accessed=bits * 8 * rows * kv_width // PARTS,
        )
        arrived = [exchanged(chosen[step.bit_length() - 1], step) for step in range(1, reach)]
        blocks.append([own[p], *arrived, before[p]])
    sink_row = None
    shares, gscores = [], []
    for p in range(PARTS):
        sink_row, own_sum, before_sum, part_gscores, *messages = kernel_call(
            functools.partial(attention_kernel, p, kv_heads, group, reach, rows, size),
            [row, wide, wide, jax.ShapeDtypeStruct((kv_heads * span, group * rows), BF16)] + [narrow] * (reach - 1),
            [VMEM] * (5 + reach + (p > 0)),
            (caps, tops, queries, grad_out, *blocks[p]) + ((sink_row,) if p else ()),
            flops=8 * rows * group * span * size * kv_heads,
            bytes_accessed=8 * rows * q_width // PARTS + 20 * span * kv_width // PARTS,
            transcendentals=group * rows * span * kv_heads,
        )
        gscores.append(part_gscores)
        shares.append((own_sum, before_sum, [exchanged(m, step) for step, m in enumerate(messages, 1)]))
    grad_queries, done = kernel_call(
        functools.partial(queries_kernel, kv_heads, group, reach, rows, size),
        [jax.ShapeDtypeStruct(queries.shape, BF16), row],
        [VMEM] * (PARTS * (reach + 2)),
        [x for p in range(PARTS) for x in (gscores[p], *blocks[p])],
        flops=2 * rows * group * span * size * kv_heads * PARTS,
        bytes_accessed=2 * rows * q_width + 2 * group * rows * span * kv_heads * PARTS,
    )
    if lax.axis_size("dp") == 2:
        sink_row = sink_row + exchanged(sink_row, 1, "dp")
    else:
        sink_row = lax.psum(sink_row, "dp")
    step = reach
    while step < count:
        sink_row = sink_row + exchanged(sink_row, step)
        step *= 2
    passing = [done] * (PARTS - 1) + [sink_row + done]
    owns, lasts = [], []
    for p in range(PARTS):
        own_sum, before_sum, back = shares[p]
        own_sum, before_sum, sink_row = kernel_call(
            functools.partial(combine_kernel, reach),
            [wide, narrow, row],
            [SMEM] + [VMEM] * (reach + 2),
            (place, passing[p], own_sum, before_sum, *back),
            bytes_accessed=24 * rows * kv_width // PARTS,
        )
        owns.append(own_sum)
        lasts.append(along(before_sum, -reach))
    step = 1
    while step < reach:
        sink_row = sink_row + exchanged(sink_row, step)
        step *= 2
    grad_keys, grad_values, grad_sinks = kernel_call(
        functools.partial(finish_kernel, PARTS),
        [jax.ShapeDtypeStruct(keys.shape, BF16)] * 2 + [jax.ShapeDtypeStruct(sinks.shape, F32)],
        [VMEM] * (1 + 2 * PARTS),
        (sink_row, *owns, *lasts),
        bytes_accessed=16 * rows * kv_width,
    )
    return grad_queries[None], grad_keys[None], grad_values[None], grad_sinks


def solution(mesh):
    blocks = P("dp", "ctx", None)
    in_specs = (blocks, blocks, blocks, blocks, P(), P("dp", None))
    out_specs = (blocks, blocks, blocks, P())
    return jax.shard_map(local, mesh=mesh, in_specs=in_specs, out_specs=out_specs, check_vma=False)
```

time: 69 us -> 62.9 us (0.912)
  waiting for transfers between devices: 37.6 us -> 13.9 us
  starting transfers between devices: 20.8 us -> 34 us
  local copies, waits for them, and re-layouts: 1.91 us -> 5.19 us
  Pallas kernels: 6.17 us -> 8.63 us
  other arithmetic: 1.6 us -> 0.02 us
    ppermute x11 -> x17, waiting for transfers between devices: 32.1 us -> 13.9 us  [exchanged(): lax.ppermute(x, axis, [(i, i ^ step) for i in range(lax.axis_size(axis))])]
    ppermute x11 -> x17, starting transfers between devices: 14.6 us -> 23 us  [exchanged(): lax.ppermute(x, axis, [(i, i ^ step) for i in range(lax.axis_size(axis))])]
    ppermute x2 -> x4, waiting for transfers between devices: 5.5 us -> 0.01 us  [along(): lax.ppermute(x, 'ctx', [(i, i + distance) for i in range(first, last)])]
    ppermute x2 -> x4, starting transfers between devices: 6.24 us -> 11 us  [along(): lax.ppermute(x, 'ctx', [(i, i + distance) for i in range(first, last)])]
    unnamed x12, local copies, waits for them, and re-layouts: 0.68 us -> 5.19 us
    pallas_call x1 -> x9, Pallas kernels: 6.17 us -> 8.63 us  [kernel_call(): pl.pallas_call(body, out_shape=out_shape, in_specs=in_specs, compiler_par...]
    concatenate x1 -> x0, other arithmetic: 1.03 us -> none  [local(): jnp.concatenate([x[:, p * kv_width:(p + 1) * kv_width] for x in (keys, va...]
    broadcast_in_dim x1 -> x0, local copies, waits for them, and re-layouts: 0.72 us -> none  [local(): grad_values[None]]
  transfers between devices with their start and end apart: 13 -> 21, of which waited for: 11 -> 6; matrix products, arithmetic and copies ran while one was open for 1% -> 0% of each run, Pallas kernels for 0% -> 12%
where the time goes in v2:
time: 62.9 us; the launch traced here: 62.5 us
  starting transfers between devices  34 us (54%)
  waiting for transfers between devices  13.9 us (22%)
  Pallas kernels  8.63 us (14%)
  local copies, waits for them, and re-layouts  5.19 us (8%)
  between operations  0.77 us (1%)
    ppermute x17, starting transfers between devices, exchanged(): lax.ppermute(x, axis, [(i, i ^ step) for i in range(lax.axis_size(axis))])  23 us
    ppermute x17, waiting for transfers between devices, exchanged(): lax.ppermute(x, axis, [(i, i ^ step) for i in range(lax.axis_size(axis))])  13.9 us
    ppermute x4, starting transfers between devices, along(): lax.ppermute(x, 'ctx', [(i, i + distance) for i in range(first, last)])  11 us
    pallas_call x9, Pallas kernels, kernel_call(): pl.pallas_call(body, out_shape=out_shape, in_specs=in_specs, compiler_par...  8.63 us
    unnamed x12, local copies, waits for them, and re-layouts  5.19 us
  transfers between devices with their start and end apart: 21, of which 6 were waited for; matrix products, arithmetic and copies ran while one was open for 0% of the time, Pallas kernels for 12%

profile of v2, /device:TPU:0, one launch (start us, length us, event | category | flops | bytes accessed | tf_op | source)
XLA Modules:
  0.0 62.5 jit_solution(6886719259398681756)
XLA Ops:
  0.6 0.9 %copy-done = bf16[1,128,512]{2,1,0:T(8,128)(2,1)S(1)} copy-done((bf16[1,128,512]{2,1,0:T(8,128)(2,1)S(1)}, bf16[1,128,512]{2,1,0:T(8,128)(2,1)}, u32[]{:S(2)}) %copy-start) | copy-done | bytes 131096
  1.5 0.9 %copy-done.1 = bf16[1,128,512]{2,1,0:T(8,128)(2,1)S(1)} copy-done((bf16[1,128,512]{2,1,0:T(8,128)(2,1)S(1)}, bf16[1,128,512]{2,1,0:T(8,128)(2,1)}, u32[]{:S(2)}) %copy-start.1) | copy-done | bytes 131096
  2.4 0.7 %copy-done.2 = s32[1,16]{1,0:T(1,128)S(1)} copy-done((s32[1,16]{1,0:T(1,128)S(1)}, s32[1,16]{1,0:T(1,128)}, u32[]{:S(2)}) %copy-start.2) | copy-done | bytes 88
  3.1 0.7 %copy-done.3 = f32[16]{0:T(128)S(1)} copy-done((f32[16]{0:T(128)S(1)}, f32[16]{0:T(128)}, u32[]{:S(2)}) %copy-start.3) | copy-done | bytes 88
  4.3 4.9 %collective-permute-start = (bf16[128,512]{1,0:T(8,128)(2,1)S(1)}, bf16[128,512]{1,0:T(8,128)(2,1)S(1)}, u32[]{:S(2)}, u32[]{:S(2)}) collective-permute-start(bf16[128,512]{1,0:T(8,128)(2,1)S(1)} %get-tuple-element.38.own_ref.refs_0_.refs_1_), channel_id=1, source_target_pairs={{0,8},{2,10},{4,12},{6,14},{8,16},{10,18},{12,20},{14,22},{16,24},... | collective-permute-start | bytes 393224 | tf_op jit(solution)/shard_map/ppermute | solution.py:224
  9.3 3.5 %collective-permute-start.4 = (bf16[128,512]{1,0:T(8,128)(2,1)S(1)}, bf16[128,512]{1,0:T(8,128)(2,1)S(1)}, u32[]{:S(2)}, u32[]{:S(2)}) collective-permute-start(bf16[128,512]{1,0:T(8,128)(2,1)S(1)} %get-tuple-element.42.own_ref.refs_0_.refs_7_), channel_id=1, source_target_pairs={{0,8},{2,10},{4,12},{6,14},{8,16},{10,18},{12,20},{14,22},{16,24},... | collective-permute-start | bytes 393224 | tf_op jit(solution)/shard_map/ppermute | solution.py:224
  12.8 1.6 %collective-permute-start.1 = (bf16[128,512]{1,0:T(8,128)(2,1)S(1)}, bf16[128,512]{1,0:T(8,128)(2,1)S(1)}, u32[]{:S(2)}, u32[]{:S(2)}) collective-permute-start(bf16[128,512]{1,0:T(8,128)(2,1)S(1)} %get-tuple-element.39), channel_id=1, source_target_pairs={{0,2},{2,0},{4,6},{6,4},{8,10},{10,8},{12,14},{14,12},{16,18},{18,... | collective-permute-start | bytes 393224 | tf_op jit(solution)/shard_map/ppermute | solution.py:227
  14.4 1.5 %collective-permute-start.3 = (bf16[128,512]{1,0:T(8,128)(2,1)S(1)}, bf16[128,512]{1,0:T(8,128)(2,1)S(1)}, u32[]{:S(2)}, u32[]{:S(2)}) collective-permute-start(bf16[128,512]{1,0:T(8,128)(2,1)S(1)} %get-tuple-element.40), channel_id=1, source_target_pairs={{0,6},{2,4},{4,2},{6,0},{8,14},{10,12},{12,10},{14,8},{16,22},{18,... | collective-permute-start | bytes 393224 | tf_op jit(solution)/shard_map/ppermute | solution.py:227
  16.4 1.6 %collective-permute-start.5 = (bf16[128,512]{1,0:T(8,128)(2,1)S(1)}, bf16[128,512]{1,0:T(8,128)(2,1)S(1)}, u32[]{:S(2)}, u32[]{:S(2)}) collective-permute-start(bf16[128,512]{1,0:T(8,128)(2,1)S(1)} %get-tuple-element.43), channel_id=1, source_target_pairs={{0,2},{2,0},{4,6},{6,4},{8,10},{10,8},{12,14},{14,12},{16,18},{18,... | collective-permute-start | bytes 393224 | tf_op jit(solution)/shard_map/ppermute | solution.py:227
  18.0 1.5 %collective-permute-start.7 = (bf16[128,512]{1,0:T(8,128)(2,1)S(1)}, bf16[128,512]{1,0:T(8,128)(2,1)S(1)}, u32[]{:S(2)}, u32[]{:S(2)}) collective-permute-start(bf16[128,512]{1,0:T(8,128)(2,1)S(1)} %get-tuple-element.44), channel_id=1, source_target_pairs={{0,6},{2,4},{4,2},{6,0},{8,14},{10,12},{12,10},{14,8},{16,22},{18,... | collective-permute-start | bytes 393224 | tf_op jit(solution)/shard_map/ppermute | solution.py:227
  19.5 1.4 %collective-permute-start.6 = (bf16[128,512]{1,0:T(8,128)(2,1)S(1)}, bf16[128,512]{1,0:T(8,128)(2,1)S(1)}, u32[]{:S(2)}, u32[]{:S(2)}) collective-permute-start(bf16[128,512]{1,0:T(8,128)(2,1)S(1)} %get-tuple-element.44), channel_id=1, source_target_pairs={{0,4},{2,6},{4,0},{6,2},{8,12},{10,14},{12,8},{14,10},{16,20},{18,... | collective-permute-start | bytes 393224 | tf_op jit(solution)/shard_map/ppermute | solution.py:227
  20.9 2.3 %collective-permute-done.3.refs_3_.refs_4_ = bf16[128,512]{1,0:T(8,128)(2,1)S(1)} collective-permute-done((bf16[128,512]{1,0:T(8,128)(2,1)S(1)}, bf16[128,512]{1,0:T(8,128)(2,1)S(1)}, u32[]{:S(2)}, u32[]{:S(2)}) %collective-permute-start.3) | collective-permute-done | bytes 131104 | tf_op jit(solution)/shard_map/ppermute | solution.py:227
  23.2 2.0 %collective-permute-done.2.refs_2_.refs_3_ = bf16[128,512]{1,0:T(8,128)(2,1)S(1)} collective-permute-done((bf16[128,512]{1,0:T(8,128)(2,1)S(1)}, bf16[128,512]{1,0:T(8,128)(2,1)S(1)}, u32[]{:S(2)}, u32[]{:S(2)}) %collective-permute-start.2) | collective-permute-done | bytes 131104 | tf_op jit(solution)/shard_map/ppermute | solution.py:227
  25.2 1.0 %copy-done.4 = bf16[1,128,2048]{2,1,0:T(8,128)(2,1)S(1)} copy-done((bf16[1,128,2048]{2,1,0:T(8,128)(2,1)S(1)}, bf16[1,128,2048]{2,1,0:T(8,128)(2,1)}, u32[]{:S(2)}) %copy-start.4) | copy-done | bytes 524312
  26.2 1.0 %copy-done.5 = bf16[1,128,2048]{2,1,0:T(8,128)(2,1)S(1)} copy-done((bf16[1,128,2048]{2,1,0:T(8,128)(2,1)S(1)}, bf16[1,128,2048]{2,1,0:T(8,128)(2,1)}, u32[]{:S(2)}) %copy-start.5) | copy-done | bytes 524312
  27.3 2.4 %shard_map.95 = (f32[1,128]{1,0:T(1,128)S(1)}, f32[128,512]{1,0:T(8,128)S(1)}, f32[128,512]{1,0:T(8,128)S(1)}, bf16[1280,512]{1,0:T(8,128)(2,1)S(1)}, bf16[128,5...) custom-call(f32[8,512]{1,0:T(8,128)S(1)} %get-tuple-element.36.caps_ref, ...), custom_call_target="tpu_custom_call" | custom-call | flops 671088640 | bytes 4325376 | tf_op jit(solution)/shard_map/pallas_call | solution.py:33
  29.7 1.6 %collective-permute-start.16 = (bf16[128,512]{1,0:T(8,128)(2,1)S(1)}, bf16[128,512]{1,0:T(8,128)(2,1)S(1)}, u32[]{:S(2)}, u32[]{:S(2)}) collective-permute-start(bf16[128,512]{1,0:T(8,128)(2,1)S(1)} %get-tuple-element.58), channel_id=1, source_target_pairs={{0,2},{2,0},{4,6},{6,4},{8,10},{10,8},{12,14},{14,12},{16,18},{18,... | collective-permute-start | bytes 393224 | tf_op jit(solution)/shard_map/ppermute | solution.py:227
  31.3 2.4 %shard_map.97 = (f32[1,128]{1,0:T(1,128)S(1)}, f32[128,512]{1,0:T(8,128)S(1)}, f32[128,512]{1,0:T(8,128)S(1)}, bf16[1280,512]{1,0:T(8,128)(2,1)S(1)}, bf16[128,5...) custom-call(f32[8,512]{1,0:T(8,128)S(1)} %get-tuple-element.36.caps_ref, ...), custom_call_target="tpu_custom_call" | custom-call | flops 671088640 | bytes 4325376 | tf_op jit(solution)/shard_map/pallas_call | solution.py:33
  33.8 1.1 %collective-permute-done.8 = f32[1,128]{1,0:T(1,128)S(1)} collective-permute-done((f32[1,128]{1,0:T(1,128)S(1)}, f32[1,128]{1,0:T(1,128)S(1)}, u32[]{:S(2)}, u32[]{:S(2)}) %collective-permute-start.8) | collective-permute-done | bytes 544 | tf_op jit(solution)/shard_map/ppermute | solution.py:227
  34.9 1.6 %collective-permute-start.9 = (f32[1,128]{1,0:T(1,128)S(1)}, f32[1,128]{1,0:T(1,128)S(1)}, u32[]{:S(2)}, u32[]{:S(2)}) collective-permute-start(f32[1,128]{1,0:T(1,128)S(1)} %add.18), channel_id=1, source_target_pairs={{0,8},{2,10},{4,12},{6,14},{8,0},{10,2},{12,4},{14,6},{16,24},{18,... | collective-permute-start | bytes 1544 | tf_op jit(solution)/shard_map/ppermute | solution.py:227
  37.0 1.5 %collective-permute-start.18 = (bf16[128,512]{1,0:T(8,128)(2,1)S(1)}, bf16[128,512]{1,0:T(8,128)(2,1)S(1)}, u32[]{:S(2)}, u32[]{:S(2)}) collective-permute-start(bf16[128,512]{1,0:T(8,128)(2,1)S(1)} %get-tuple-element.60), channel_id=1, source_target_pairs={{0,6},{2,4},{4,2},{6,0},{8,14},{10,12},{12,10},{14,8},{16,22},{18,... | collective-permute-start | bytes 393224 | tf_op jit(solution)/shard_map/ppermute | solution.py:227
  38.5 1.5 %collective-permute-start.11 = (bf16[128,512]{1,0:T(8,128)(2,1)S(1)}, bf16[128,512]{1,0:T(8,128)(2,1)S(1)}, u32[]{:S(2)}, u32[]{:S(2)}) collective-permute-start(bf16[128,512]{1,0:T(8,128)(2,1)S(1)} %get-tuple-element.52), channel_id=1, source_target_pairs={{0,2},{2,0},{4,6},{6,4},{8,10},{10,8},{12,14},{14,12},{16,18},{18,... | collective-permute-start | bytes 393224 | tf_op jit(solution)/shard_map/ppermute | solution.py:227
  40.0 4.4 %collective-permute-start.10 = (f32[1,128]{1,0:T(1,128)S(1)}, f32[1,128]{1,0:T(1,128)S(1)}, u32[]{:S(2)}, u32[]{:S(2)}) collective-permute-start(f32[1,128]{1,0:T(1,128)S(1)} %add.19), channel_id=1, source_target_pairs={{0,16},{2,18},{4,20},{6,22},{8,24},{10,26},{12,28},{14,30},{16,0},... | collective-permute-start | bytes 1544 | tf_op jit(solution)/shard_map/ppermute | solution.py:227
  44.4 1.7 %shard_map.98 = (bf16[128,2048]{1,0:T(8,128)(2,1)}, f32[1,128]{1,0:T(1,128)S(1)}) custom-call(bf16[1280,512]{1,0:T(8,128)(2,1)S(1)} %get-tuple-element.41.refs_0_, bf16[128,512]{1,0:T(8,128)(2,1)S(1)} %get-tuple-element.38.own_ref.refs_0_.refs_1_, bf16[128,512]{1,0:T(8,128)(2,1)S(1)} %collective-permute-done.1.refs_1_.refs_2_, ...), custom_call_target="tpu_custom_call" | custom-call | flops 335544320 | bytes 3145728 | tf_op jit(solution)/shard_map/pallas_call | solution.py:33
  46.6 1.5 %collective-permute-start.13 = (bf16[128,512]{1,0:T(8,128)(2,1)S(1)}, bf16[128,512]{1,0:T(8,128)(2,1)S(1)}, u32[]{:S(2)}, u32[]{:S(2)}) collective-permute-start(bf16[128,512]{1,0:T(8,128)(2,1)S(1)} %get-tuple-element.54), channel_id=1, source_target_pairs={{0,6},{2,4},{4,2},{6,0},{8,14},{10,12},{12,10},{14,8},{16,22},{18,... | collective-permute-start | bytes 393224 | tf_op jit(solution)/shard_map/ppermute | solution.py:227
  48.7 1.3 %collective-permute-start.19 = (bf16[128,512]{1,0:T(8,128)(2,1)S(1)}, bf16[128,512]{1,0:T(8,128)(2,1)S(1)}, u32[]{:S(2)}, u32[]{:S(2)}) collective-permute-start(bf16[128,512]{1,0:T(8,128)(2,1)S(1)} %get-tuple-element.63), channel_id=1, source_target_pairs={{8,0},{10,2},{12,4},{14,6},{16,8},{18,10},{20,12},{22,14},{24,16},... | collective-permute-start | bytes 393224 | tf_op jit(solution)/shard_map/ppermute | solution.py:224
  50.0 3.1 %collective-permute-done.12.refs_1_ = bf16[128,512]{1,0:T(8,128)(2,1)S(1)} collective-permute-done((bf16[128,512]{1,0:T(8,128)(2,1)S(1)}, bf16[128,512]{1,0:T(8,128)(2,1)S(1)}, u32[]{:S(2)}, u32[]{:S(2)}) %collective-permute-start.12) | collective-permute-done | bytes 131104 | tf_op jit(solution)/shard_map/ppermute | solution.py:227
  53.3 1.3 %collective-permute-start.20 = (bf16[128,512]{1,0:T(8,128)(2,1)S(1)}, bf16[128,512]{1,0:T(8,128)(2,1)S(1)}, u32[]{:S(2)}, u32[]{:S(2)}) collective-permute-start(bf16[128,512]{1,0:T(8,128)(2,1)S(1)} %get-tuple-element.64), channel_id=1, source_target_pairs={{8,0},{10,2},{12,4},{14,6},{16,8},{18,10},{20,12},{22,14},{24,16},... | collective-permute-start | bytes 393224 | tf_op jit(solution)/shard_map/ppermute | solution.py:224
  55.2 3.0 %collective-permute-done.14 = f32[1,128]{1,0:T(1,128)S(1)} collective-permute-done((f32[1,128]{1,0:T(1,128)S(1)}, f32[1,128]{1,0:T(1,128)S(1)}, u32[]{:S(2)}, u32[]{:S(2)}) %collective-permute-start.14) | collective-permute-done | bytes 544 | tf_op jit(solution)/shard_map/ppermute | solution.py:227
  58.2 1.2 %collective-permute-start.15 = (f32[1,128]{1,0:T(1,128)S(1)}, f32[1,128]{1,0:T(1,128)S(1)}, u32[]{:S(2)}, u32[]{:S(2)}) collective-permute-start(f32[1,128]{1,0:T(1,128)S(1)} %add.22), channel_id=1, source_target_pairs={{0,4},{2,6},{4,0},{6,2},{8,12},{10,14},{12,8},{14,10},{16,20},{18,... | collective-permute-start | bytes 1544 | tf_op jit(solution)/shard_map/ppermute | solution.py:227
  59.4 2.3 %collective-permute-done.15 = f32[1,128]{1,0:T(1,128)S(1)} collective-permute-done((f32[1,128]{1,0:T(1,128)S(1)}, f32[1,128]{1,0:T(1,128)S(1)}, u32[]{:S(2)}, u32[]{:S(2)}) %collective-permute-start.15) | collective-permute-done | bytes 544 | tf_op jit(solution)/shard_map/ppermute | solution.py:227
  61.7 0.8 %shard_map.101 = (bf16[128,512]{1,0:T(8,128)(2,1)}, bf16[128,512]{1,0:T(8,128)(2,1)}, f32[16]{0:T(128)}) custom-call(f32[1,128]{1,0:T(1,128)S(1)} %add.23.sink_ref, f32[128,512]{1,0:T(8,128)S(1)} %get-tuple-element.61.refs_0_, f32[128,512]{1,0:T(8,128)S(1)} %get-tuple-element.62.refs_1_, bf16[128,512]{1,0:T(8,128)(2,1)S(1)} %collective-permute-done.19.refs_2_, ...), custom_call_target="tpu_custom_call" | custom-call | bytes 1048576 | tf_op jit(solution)/shard_map/pallas_call | solution.py:33
  (36 shorter events, 3.6 us)
Async XLA Ops:
  0.6 0.9 %copy-start = (bf16[1,128,512]{2,1,0:T(8,128)(2,1)S(1)}, bf16[1,128,512]{2,1,0:T(8,128)(2,1)}, u32[]{:S(2)}) copy-start(bf16[1,128,512]{2,1,0:T(8,128)(2,1)} %param.7) | copy-start | bytes 393220
  1.5 0.9 %copy-start.1 = (bf16[1,128,512]{2,1,0:T(8,128)(2,1)S(1)}, bf16[1,128,512]{2,1,0:T(8,128)(2,1)}, u32[]{:S(2)}) copy-start(bf16[1,128,512]{2,1,0:T(8,128)(2,1)} %param.8) | copy-start | bytes 393220
  2.4 0.7 %copy-start.2 = (s32[1,16]{1,0:T(1,128)S(1)}, s32[1,16]{1,0:T(1,128)}, u32[]{:S(2)}) copy-start(s32[1,16]{1,0:T(1,128)} %docs_ref.1) | copy-start | bytes 196
  3.1 0.7 %copy-start.3 = (f32[16]{0:T(128)S(1)}, f32[16]{0:T(128)}, u32[]{:S(2)}) copy-start(f32[16]{0:T(128)} %sinks_ref.1) | copy-start | bytes 196
  4.3 8.4 %collective-permute-start = (bf16[128,512]{1,0:T(8,128)(2,1)S(1)}, bf16[128,512]{1,0:T(8,128)(2,1)S(1)}, u32[]{:S(2)}, u32[]{:S(2)}) collective-permute-start(bf16[128,512]{1,0:T(8,128)(2,1)S(1)} %get-tuple-element.38.own_ref.refs_0_.refs_1_), channel_id=1, source_target_pairs={{0,8},{2,10},{4,12},{6,14},{8,16},{10,18},{12,20},{14,22},{16,24},... | collective-permute-start | bytes 393224 | tf_op jit(solution)/shard_map/ppermute | solution.py:224
  9.3 7.1 %collective-permute-start.4 = (bf16[128,512]{1,0:T(8,128)(2,1)S(1)}, bf16[128,512]{1,0:T(8,128)(2,1)S(1)}, u32[]{:S(2)}, u32[]{:S(2)}) collective-permute-start(bf16[128,512]{1,0:T(8,128)(2,1)S(1)} %get-tuple-element.42.own_ref.refs_0_.refs_7_), channel_id=1, source_target_pairs={{0,8},{2,10},{4,12},{6,14},{8,16},{10,18},{12,20},{14,22},{16,24},... | collective-permute-start | bytes 393224 | tf_op jit(solution)/shard_map/ppermute | solution.py:224
  12.8 6.6 %collective-permute-start.1 = (bf16[128,512]{1,0:T(8,128)(2,1)S(1)}, bf16[128,512]{1,0:T(8,128)(2,1)S(1)}, u32[]{:S(2)}, u32[]{:S(2)}) collective-permute-start(bf16[128,512]{1,0:T(8,128)(2,1)S(1)} %get-tuple-element.39), channel_id=1, source_target_pairs={{0,2},{2,0},{4,6},{6,4},{8,10},{10,8},{12,14},{14,12},{16,18},{18,... | collective-permute-start | bytes 393224 | tf_op jit(solution)/shard_map/ppermute | solution.py:227
  14.4 8.8 %collective-permute-start.3 = (bf16[128,512]{1,0:T(8,128)(2,1)S(1)}, bf16[128,512]{1,0:T(8,128)(2,1)S(1)}, u32[]{:S(2)}, u32[]{:S(2)}) collective-permute-start(bf16[128,512]{1,0:T(8,128)(2,1)S(1)} %get-tuple-element.40), channel_id=1, source_target_pairs={{0,6},{2,4},{4,2},{6,0},{8,14},{10,12},{12,10},{14,8},{16,22},{18,... | collective-permute-start | bytes 393224 | tf_op jit(solution)/shard_map/ppermute | solution.py:227
  15.9 9.3 %collective-permute-start.2 = (bf16[128,512]{1,0:T(8,128)(2,1)S(1)}, bf16[128,512]{1,0:T(8,128)(2,1)S(1)}, u32[]{:S(2)}, u32[]{:S(2)}) collective-permute-start(bf16[128,512]{1,0:T(8,128)(2,1)S(1)} %get-tuple-element.40), channel_id=1, source_target_pairs={{0,4},{2,6},{4,0},{6,2},{8,12},{10,14},{12,8},{14,10},{16,20},{18,... | collective-permute-start | bytes 393224 | tf_op jit(solution)/shard_map/ppermute | solution.py:227
  16.4 14.8 %collective-permute-start.5 = (bf16[128,512]{1,0:T(8,128)(2,1)S(1)}, bf16[128,512]{1,0:T(8,128)(2,1)S(1)}, u32[]{:S(2)}, u32[]{:S(2)}) collective-permute-start(bf16[128,512]{1,0:T(8,128)(2,1)S(1)} %get-tuple-element.43), channel_id=1, source_target_pairs={{0,2},{2,0},{4,6},{6,4},{8,10},{10,8},{12,14},{14,12},{16,18},{18,... | collective-permute-start | bytes 393224 | tf_op jit(solution)/shard_map/ppermute | solution.py:227
  18.0 13.3 %collective-permute-start.7 = (bf16[128,512]{1,0:T(8,128)(2,1)S(1)}, bf16[128,512]{1,0:T(8,128)(2,1)S(1)}, u32[]{:S(2)}, u32[]{:S(2)}) collective-permute-start(bf16[128,512]{1,0:T(8,128)(2,1)S(1)} %get-tuple-element.44), channel_id=1, source_target_pairs={{0,6},{2,4},{4,2},{6,0},{8,14},{10,12},{12,10},{14,8},{16,22},{18,... | collective-permute-start | bytes 393224 | tf_op jit(solution)/shard_map/ppermute | solution.py:227
  19.5 11.8 %collective-permute-start.6 = (bf16[128,512]{1,0:T(8,128)(2,1)S(1)}, bf16[128,512]{1,0:T(8,128)(2,1)S(1)}, u32[]{:S(2)}, u32[]{:S(2)}) collective-permute-start(bf16[128,512]{1,0:T(8,128)(2,1)S(1)} %get-tuple-element.44), channel_id=1, source_target_pairs={{0,4},{2,6},{4,0},{6,2},{8,12},{10,14},{12,8},{14,10},{16,20},{18,... | collective-permute-start | bytes 393224 | tf_op jit(solution)/shard_map/ppermute | solution.py:227
  25.2 1.0 %copy-start.4 = (bf16[1,128,2048]{2,1,0:T(8,128)(2,1)S(1)}, bf16[1,128,2048]{2,1,0:T(8,128)(2,1)}, u32[]{:S(2)}) copy-start(bf16[1,128,2048]{2,1,0:T(8,128)(2,1)} %param.6) | copy-start | bytes 1572868
  26.2 1.0 %copy-start.5 = (bf16[1,128,2048]{2,1,0:T(8,128)(2,1)S(1)}, bf16[1,128,2048]{2,1,0:T(8,128)(2,1)}, u32[]{:S(2)}) copy-start(bf16[1,128,2048]{2,1,0:T(8,128)(2,1)} %param.9) | copy-start | bytes 1572868
  29.7 16.9 %collective-permute-start.16 = (bf16[128,512]{1,0:T(8,128)(2,1)S(1)}, bf16[128,512]{1,0:T(8,128)(2,1)S(1)}, u32[]{:S(2)}, u32[]{:S(2)}) collective-permute-start(bf16[128,512]{1,0:T(8,128)(2,1)S(1)} %get-tuple-element.58), channel_id=1, source_target_pairs={{0,2},{2,0},{4,6},{6,4},{8,10},{10,8},{12,14},{14,12},{16,18},{18,... | collective-permute-start | bytes 393224 | tf_op jit(solution)/shard_map/ppermute | solution.py:227
  33.7 1.2 %collective-permute-start.8 = (f32[1,128]{1,0:T(1,128)S(1)}, f32[1,128]{1,0:T(1,128)S(1)}, u32[]{:S(2)}, u32[]{:S(2)}) collective-permute-start(f32[1,128]{1,0:T(1,128)S(1)} %get-tuple-element.48), channel_id=1, source_target_pairs={{0,1},{1,0},{2,3},{3,2},{4,5},{5,4},{6,7},{7,6},{8,9},{9,8},{10,11... | collective-permute-start | bytes 1544 | tf_op jit(solution)/shard_map/ppermute | solution.py:227
  34.9 5.1 %collective-permute-start.9 = (f32[1,128]{1,0:T(1,128)S(1)}, f32[1,128]{1,0:T(1,128)S(1)}, u32[]{:S(2)}, u32[]{:S(2)}) collective-permute-start(f32[1,128]{1,0:T(1,128)S(1)} %add.18), channel_id=1, source_target_pairs={{0,8},{2,10},{4,12},{6,14},{8,0},{10,2},{12,4},{14,6},{16,24},{18,... | collective-permute-start | bytes 1544 | tf_op jit(solution)/shard_map/ppermute | solution.py:227
  36.5 11.6 %collective-permute-start.17 = (bf16[128,512]{1,0:T(8,128)(2,1)S(1)}, bf16[128,512]{1,0:T(8,128)(2,1)S(1)}, u32[]{:S(2)}, u32[]{:S(2)}) collective-permute-start(bf16[128,512]{1,0:T(8,128)(2,1)S(1)} %get-tuple-element.59), channel_id=1, source_target_pairs={{0,4},{2,6},{4,0},{6,2},{8,12},{10,14},{12,8},{14,10},{16,20},{18,... | collective-permute-start | bytes 393224 | tf_op jit(solution)/shard_map/ppermute | solution.py:227
  37.0 11.1 %collective-permute-start.18 = (bf16[128,512]{1,0:T(8,128)(2,1)S(1)}, bf16[128,512]{1,0:T(8,128)(2,1)S(1)}, u32[]{:S(2)}, u32[]{:S(2)}) collective-permute-start(bf16[128,512]{1,0:T(8,128)(2,1)S(1)} %get-tuple-element.60), channel_id=1, source_target_pairs={{0,6},{2,4},{4,2},{6,0},{8,14},{10,12},{12,10},{14,8},{16,22},{18,... | collective-permute-start | bytes 393224 | tf_op jit(solution)/shard_map/ppermute | solution.py:227
  38.5 11.5 %collective-permute-start.11 = (bf16[128,512]{1,0:T(8,128)(2,1)S(1)}, bf16[128,512]{1,0:T(8,128)(2,1)S(1)}, u32[]{:S(2)}, u32[]{:S(2)}) collective-permute-start(bf16[128,512]{1,0:T(8,128)(2,1)S(1)} %get-tuple-element.52), channel_id=1, source_target_pairs={{0,2},{2,0},{4,6},{6,4},{8,10},{10,8},{12,14},{14,12},{16,18},{18,... | collective-permute-start | bytes 393224 | tf_op jit(solution)/shard_map/ppermute | solution.py:227
  40.0 6.1 %collective-permute-start.10 = (f32[1,128]{1,0:T(1,128)S(1)}, f32[1,128]{1,0:T(1,128)S(1)}, u32[]{:S(2)}, u32[]{:S(2)}) collective-permute-start(f32[1,128]{1,0:T(1,128)S(1)} %add.19), channel_id=1, source_target_pairs={{0,16},{2,18},{4,20},{6,22},{8,24},{10,26},{12,28},{14,30},{16,0},... | collective-permute-start | bytes 1544 | tf_op jit(solution)/shard_map/ppermute | solution.py:227
  46.1 7.0 %collective-permute-start.12 = (bf16[128,512]{1,0:T(8,128)(2,1)S(1)}, bf16[128,512]{1,0:T(8,128)(2,1)S(1)}, u32[]{:S(2)}, u32[]{:S(2)}) collective-permute-start(bf16[128,512]{1,0:T(8,128)(2,1)S(1)} %get-tuple-element.53), channel_id=1, source_target_pairs={{0,4},{2,6},{4,0},{6,2},{8,12},{10,14},{12,8},{14,10},{16,20},{18,... | collective-permute-start | bytes 393224 | tf_op jit(solution)/shard_map/ppermute | solution.py:227
  46.6 6.5 %collective-permute-start.13 = (bf16[128,512]{1,0:T(8,128)(2,1)S(1)}, bf16[128,512]{1,0:T(8,128)(2,1)S(1)}, u32[]{:S(2)}, u32[]{:S(2)}) collective-permute-start(bf16[128,512]{1,0:T(8,128)(2,1)S(1)} %get-tuple-element.54), channel_id=1, source_target_pairs={{0,6},{2,4},{4,2},{6,0},{8,14},{10,12},{12,10},{14,8},{16,22},{18,... | collective-permute-start | bytes 393224 | tf_op jit(solution)/shard_map/ppermute | solution.py:227
  48.7 13.1 %collective-permute-start.19 = (bf16[128,512]{1,0:T(8,128)(2,1)S(1)}, bf16[128,512]{1,0:T(8,128)(2,1)S(1)}, u32[]{:S(2)}, u32[]{:S(2)}) collective-permute-start(bf16[128,512]{1,0:T(8,128)(2,1)S(1)} %get-tuple-element.63), channel_id=1, source_target_pairs={{8,0},{10,2},{12,4},{14,6},{16,8},{18,10},{20,12},{22,14},{24,16},... | collective-permute-start | bytes 393224 | tf_op jit(solution)/shard_map/ppermute | solution.py:224
  53.3 8.5 %collective-permute-start.20 = (bf16[128,512]{1,0:T(8,128)(2,1)S(1)}, bf16[128,512]{1,0:T(8,128)(2,1)S(1)}, u32[]{:S(2)}, u32[]{:S(2)}) collective-permute-start(bf16[128,512]{1,0:T(8,128)(2,1)S(1)} %get-tuple-element.64), channel_id=1, source_target_pairs={{8,0},{10,2},{12,4},{14,6},{16,8},{18,10},{20,12},{22,14},{24,16},... | collective-permute-start | bytes 393224 | tf_op jit(solution)/shard_map/ppermute | solution.py:224
  54.6 3.6 %collective-permute-start.14 = (f32[1,128]{1,0:T(1,128)S(1)}, f32[1,128]{1,0:T(1,128)S(1)}, u32[]{:S(2)}, u32[]{:S(2)}) collective-permute-start(f32[1,128]{1,0:T(1,128)S(1)} %get-tuple-element.55), channel_id=1, source_target_pairs={{0,2},{2,0},{4,6},{6,4},{8,10},{10,8},{12,14},{14,12},{16,18},{18,... | collective-permute-start | bytes 1544 | tf_op jit(solution)/shard_map/ppermute | solution.py:227
  58.2 3.5 %collective-permute-start.15 = (f32[1,128]{1,0:T(1,128)S(1)}, f32[1,128]{1,0:T(1,128)S(1)}, u32[]{:S(2)}, u32[]{:S(2)}) collective-permute-start(f32[1,128]{1,0:T(1,128)S(1)} %add.22), channel_id=1, source_target_pairs={{0,4},{2,6},{4,0},{6,2},{8,12},{10,14},{12,8},{14,10},{16,20},{18,... | collective-permute-start | bytes 1544 | tf_op jit(solution)/shard_map/ppermute | solution.py:227

commit v3 on v2

v3 whole, which is shorter than its diff:
```python
import functools

import jax
import jax.numpy as jnp
from jax import lax
from jax.experimental import pallas as pl
from jax.experimental.pallas import tpu as pltpu
from jax.sharding import PartitionSpec as P

WINDOW = 512
LOG2E = 1.4426950408889634

F32 = jnp.float32
BF16 = jnp.bfloat16
SMEM = pl.BlockSpec(memory_space=pltpu.SMEM)
VMEM = pl.BlockSpec(memory_space=pltpu.VMEM)


def dot_nt(a, b):
    return lax.dot_general(a, b, (((1,), (1,)), ((), ())), preferred_element_type=F32)


def dot_nn(a, b):
    return lax.dot_general(a, b, (((1,), (0,)), ((), ())), preferred_element_type=F32)


def dot_tn(a, b):
    return lax.dot_general(a, b, (((0,), (0,)), ((), ())), preferred_element_type=F32)


def kernel_call(body, out_shape, in_specs, operands):
    return pl.pallas_call(
        body,
        out_shape=out_shape,
        in_specs=in_specs,
        out_specs=[VMEM] * len(out_shape),
        compiler_params=pltpu.CompilerParams(vmem_limit_bytes=24 * 1024 * 1024),
        cost_estimate=pl.CostEstimate(flops=0, bytes_accessed=0, transcendentals=0),
    )(*operands)


def later(slot, step):
    return lax.bitwise_xor(slot, step) > slot


def choose(slot, own, before_ref, out_refs):
    for bit, ref in enumerate(out_refs):
        @pl.when(later(slot, 1 << bit))
        def _():
            ref[...] = own

        @pl.when(jnp.logical_not(later(slot, 1 << bit)))
        def _():
            ref[...] = before_ref[...]


def keys_kernel(reach, place_ref, own_ref, before_ref, *out_refs):
    choose(lax.rem(place_ref[0], reach), own_ref[:, :before_ref.shape[1]], before_ref, out_refs)


def tables_kernel(reach, rows, group, place_ref, docs_ref, sinks_ref, own_ref, before_ref, pair_ref, *refs):
    caps_ref, tops_ref, *out_refs = refs
    place = place_ref[0]
    slot = lax.rem(place, reach)
    choose(slot, own_ref[:, before_ref.shape[1]:], before_ref, out_refs)
    doc = docs_ref[0, place]
    columns = caps_ref.shape[1]
    for step in range(1, reach + 1):
        distance = reach
        if step < reach:
            distance = lax.rem(slot - lax.bitwise_xor(slot, step) + reach, reach)
        other = docs_ref[0, jnp.maximum(place - distance, 0)]
        same = jnp.logical_and(place >= distance, other == doc)
        caps_ref[step:step + 1, :] = jnp.full((1, columns), jnp.where(same, jnp.inf, -jnp.inf), F32)
    for head in range(sinks_ref.shape[0] // group):
        for j in range(group):
            tops_ref[head:head + 1, j * rows:(j + 1) * rows] = jnp.full(
                (1, rows), sinks_ref[head * group + j] * LOG2E, F32
            )


def block(x, i, rows):
    return x[i * rows:(i + 1) * rows]


def causal_mask(rows, group):
    shape = (rows, group * rows)
    key_at = lax.broadcasted_iota(jnp.int32, shape, 0)
    return key_at <= lax.rem(lax.broadcasted_iota(jnp.int32, shape, 1), rows)


def parted(x, causal):
    zero = jnp.zeros((), x.dtype)
    return jnp.where(causal, x, zero), jnp.where(causal, zero, x)


def stacked(ref, first, group, size):
    return jnp.concatenate([ref[:, (first + j) * size:(first + j + 1) * size] for j in range(group)], axis=0)


def store_shares(x, cut, rows, reach, own_ref, before_ref, message_refs):
    own_ref[:, cut] = block(x, 0, rows)
    before_ref[:, cut] = block(x, reach, rows)
    for i, ref in enumerate(message_refs, 1):
        ref[:, cut] = block(x, i, rows).astype(BF16)


def probs_kernel(kv_heads, group, reach, rows, size, caps_ref, tops_ref, pair_ref, *refs):
    blocks = refs[:reach + 1]
    probs_ref, sink_ref, own_ref, before_ref, *message_refs = refs[reach + 1:]
    to_log2 = size ** (-0.5) * LOG2E
    causal = causal_mask(rows, group)
    caps = [caps_ref[i:i + 1, :] for i in range(reach + 1)]
    for head in range(kv_heads):
        cut = slice(head * size, (head + 1) * size)
        q = stacked(pair_ref, head * group, group, size)
        g = stacked(pair_ref, (kv_heads + head) * group, group, size)
        keys = jnp.concatenate([r[:, cut] for r in blocks], axis=0)
        scores = dot_nt(keys, q)
        s_blocks = [
            jnp.where(causal, block(scores, 0, rows), jnp.minimum(block(scores, reach, rows), caps[reach]))
        ] + [block(scores, i, rows) for i in range(1, reach)]
        top = tops_ref[head:head + 1, :]
        sink_log = top
        for i, s in enumerate(s_blocks):
            high = jnp.max(s, axis=0, keepdims=True) * to_log2
            top = jnp.maximum(top, jnp.minimum(high, caps[i]) if i else high)
        sink_weight = jnp.exp2(sink_log - top)
        summed = sink_weight
        raised = []
        for i, s in enumerate(s_blocks):
            e = jnp.exp2(s * to_log2 - (jnp.maximum(top, -caps[i]) if i else top))
            summed = summed + jnp.sum(e, axis=0, keepdims=True)
            raised.append(e)
        inverse = 1.0 / summed
        probs = [(e * inverse).astype(BF16) for e in raised]
        for i, p in enumerate(probs):
            at = (head * reach + i) * rows
            probs_ref[at:at + rows, :] = p
        sink_ref[head:head + 1, :] = sink_weight * inverse
        first, last = parted(probs[0], causal)
        dv = dot_nn(jnp.concatenate([first] + probs[1:] + [last], axis=0), g)
        store_shares(dv, cut, rows, reach, own_ref, before_ref, message_refs)


def scores_kernel(kv_heads, group, reach, rows, size, probs_ref, sinkp_ref, pair_ref, *refs):
    blocks = refs[:reach + 1]
    gscores_ref, sink_ref, own_ref, before_ref, *message_refs = refs[reach + 1:]
    scale = size ** (-0.5)
    columns = group * rows
    causal = causal_mask(rows, group)
    lane = lax.broadcasted_iota(jnp.int32, (1, 128), 1)
    sink_row = jnp.zeros((1, 128), F32)
    for head in range(kv_heads):
        cut = slice(head * size, (head + 1) * size)
        q = stacked(pair_ref, head * group, group, size)
        g = stacked(pair_ref, (kv_heads + head) * group, group, size)
        own_cut = slice((kv_heads + head) * size, (kv_heads + head + 1) * size)
        values = jnp.concatenate([blocks[0][:, own_cut]] + [r[:, cut] for r in blocks[1:]], axis=0)
        gprobs = dot_nt(values, g)
        t_blocks = [jnp.where(causal, block(gprobs, 0, rows), block(gprobs, reach, rows))]
        t_blocks += [block(gprobs, i, rows) for i in range(1, reach)]
        probs = [
            probs_ref[(head * reach + i) * rows:(head * reach + i + 1) * rows, :].astype(F32) for i in range(reach)
        ]
        delta = jnp.zeros((1, columns), F32)
        for p, t in zip(probs, t_blocks):
            delta = delta + jnp.sum(p * t, axis=0, keepdims=True)
        gscores = [(p * (t - delta)).astype(BF16) for p, t in zip(probs, t_blocks)]
        first, last = parted(gscores[0], causal)
        gscores = jnp.concatenate([first] + gscores[1:] + [last], axis=0)
        span = (reach + 1) * rows
        gscores_ref[head * span:(head + 1) * span, :] = gscores
        dk = dot_nn(gscores, q) * scale
        store_shares(dk, cut, rows, reach, own_ref, before_ref, message_refs)
        sink_terms = sinkp_ref[head:head + 1, :] * delta
        for j in range(group):
            term = jnp.sum(sink_terms[:, j * rows:(j + 1) * rows], axis=1, keepdims=True)
            sink_row = jnp.where(lane == head * group + j, -term, sink_row)
    sink_ref[...] = sink_row


def queries_kernel(kv_heads, group, reach, rows, size, gscores_ref, *refs):
    *blocks, dq_ref, done_ref = refs
    scale = size ** (-0.5)
    span = (reach + 1) * rows
    for head in range(kv_heads):
        cut = slice(head * size, (head + 1) * size)
        keys = jnp.concatenate([r[:, cut] for r in blocks], axis=0)
        dq = (dot_tn(gscores_ref[head * span:(head + 1) * span, :], keys) * scale).astype(BF16)
        for j in range(group):
            at = (head * group + j) * size
            dq_ref[:, at:at + size] = dq[j * rows:(j + 1) * rows]
    done_ref[...] = jnp.zeros_like(done_ref)


def combine_kernel(reach, place_ref, own_ref, before_ref, *refs):
    *messages, own_out, before_out, done_ref = refs
    slot = lax.rem(place_ref[0], reach)
    own, before = own_ref[...], before_ref[...]
    for step, message in enumerate(messages, 1):
        mine = later(slot, step)
        back = message[...].astype(F32)
        own = own + jnp.where(mine, back, 0.0)
        before = before + jnp.where(mine, 0.0, back)
    own_out[...] = own
    before_out[...] = before.astype(BF16)
    done_ref[...] = jnp.zeros_like(done_ref)


def joined_kernel(share_ref, sink_ref, done_ref, share_out, sink_out):
    share_out[...] = share_ref[...]
    sink_out[...] = sink_ref[...] + done_ref[...]


def out_kernel(keys_ref, sink_ref, done_ref, keys_out, sink_out):
    keys_out[...] = keys_ref[...]
    sink_out[...] = sink_ref[0, :sink_out.shape[0]]


def total_kernel(own_ref, last_ref, out_ref):
    out_ref[...] = (own_ref[...] + last_ref[...].astype(F32)).astype(BF16)


def end_kernel(own_ref, last_ref, out_ref, done_ref):
    done_ref[...] = jnp.zeros_like(done_ref)
    out_ref[...] = (own_ref[...] + last_ref[...].astype(F32)).astype(BF16)


def local(queries, keys, values, grad_out, sinks, doc_ids):
    rows, q_width = queries.shape[1:]
    kv_width = keys.shape[2]
    heads = sinks.shape[0]
    size = q_width // heads
    group = q_width // kv_width
    kv_heads = kv_width // size
    reach = WINDOW // rows
    count = lax.axis_size("ctx")
    place = jnp.full((1,), lax.axis_index("ctx"), jnp.int32)
    queries, keys, values, grad_out = queries[0], keys[0], values[0], grad_out[0]
    wide = jax.ShapeDtypeStruct(keys.shape, F32)
    narrow = jax.ShapeDtypeStruct(keys.shape, BF16)
    row = jax.ShapeDtypeStruct((1, 128), F32)
    columns = group * rows
    table = jax.ShapeDtypeStruct((8 * (-(-max(reach + 1, kv_heads) // 8)), columns), F32)
    sizes = (kv_heads, group, reach, rows, size)

    def along(x, distance):
        if distance < 0:
            return lax.ppermute(x, "ctx", [(i, (i + distance) % count) for i in range(count)])
        first, last = max(0, -distance), min(count, count - distance)
        return lax.ppermute(x, "ctx", [(i, i + distance) for i in range(first, last)])

    def exchanged(x, step, axis="ctx"):
        return lax.ppermute(x, axis, [(i, i ^ step) for i in range(lax.axis_size(axis))])

    def summed_over(x, first, end):
        while first < end:
            x = x + exchanged(x, first)
            first *= 2
        return x

    keys_before = along(keys, reach)
    values_before = along(values, reach)
    own = jnp.concatenate([keys, values], axis=1)
    pair = jnp.concatenate([queries, grad_out], axis=1)

    def gathered(own, chosen, before):
        return [own, *(exchanged(chosen[step.bit_length() - 1], step) for step in range(1, reach)), before]

    choices = [narrow] * (reach.bit_length() - 1)
    chosen = kernel_call(
        functools.partial(keys_kernel, reach), choices, [SMEM, VMEM, VMEM], (place, own, keys_before)
    )
    key_blocks = gathered(own, chosen, keys_before)
    caps, tops, *chosen = kernel_call(
        functools.partial(tables_kernel, reach, rows, group),
        [table, table] + choices,
        [SMEM] * 3 + [VMEM] * 3,
        (place, doc_ids, sinks, own, values_before, pair),
    )
    value_blocks = gathered(own, chosen, values_before)
    probs, sink_probs, values_own, values_share, *messages = kernel_call(
        functools.partial(probs_kernel, *sizes),
        [jax.ShapeDtypeStruct((kv_heads * reach * rows, columns), BF16), table, wide, wide] + [narrow] * (reach - 1),
        [VMEM] * (4 + reach),
        (caps, tops, pair, *key_blocks),
    )
    values_back = [exchanged(m, step) for step, m in enumerate(messages, 1)]
    gscores, sink_row, keys_own, keys_share, *messages = kernel_call(
        functools.partial(scores_kernel, *sizes),
        [jax.ShapeDtypeStruct((kv_heads * (reach + 1) * rows, columns), BF16), row, wide, wide]
        + [narrow] * (reach - 1),
        [VMEM] * (4 + reach),
        (probs, sink_probs, pair, *value_blocks),
    )
    keys_back = [exchanged(m, step) for step, m in enumerate(messages, 1)]
    grad_queries, dq_done = kernel_call(
        functools.partial(queries_kernel, *sizes),
        [jax.ShapeDtypeStruct(queries.shape, BF16), row],
        [VMEM] * (2 + reach),
        (gscores, *key_blocks),
    )

    def combined(own, share, back):
        return kernel_call(
            functools.partial(combine_kernel, reach),
            [wide, narrow, row],
            [SMEM] + [VMEM] * (reach + 1),
            (place, own, share, *back),
        )

    values_own, values_share, done = combined(values_own, values_share, values_back)
    values_last = along(values_share, -reach)
    sink_row = sink_row + done
    if lax.axis_size("dp") == 2:
        sink_row = sink_row + exchanged(sink_row, 1, "dp")
    else:
        sink_row = lax.psum(sink_row, "dp")
    sink_row = summed_over(sink_row, reach, count)
    keys_own, keys_share, _ = combined(keys_own, keys_share, keys_back)
    keys_share, sink_row = kernel_call(
        joined_kernel, [narrow, row], [VMEM] * 3, (keys_share, sink_row, dq_done)
    )
    keys_last = along(keys_share, -reach)
    grad_values, done = kernel_call(end_kernel, [narrow, row], [VMEM] * 2, (values_own, values_last))
    sink_row = sink_row + exchanged(sink_row, 1) + done
    sink_row = summed_over(sink_row, 2, reach)
    grad_keys, = kernel_call(total_kernel, [narrow], [VMEM] * 2, (keys_own, keys_last))
    grad_keys, grad_sinks = kernel_call(
        out_kernel,
        [narrow, jax.ShapeDtypeStruct(sinks.shape, F32)],
        [VMEM] * 3,
        (grad_keys, sink_row, done),
    )
    return grad_queries[None], grad_keys[None], grad_values[None], grad_sinks


def solution(mesh):
    blocks = P("dp", "ctx", None)
    in_specs = (blocks, blocks, blocks, blocks, P(), P("dp", None))
    out_specs = (blocks, blocks, blocks, P())
    return jax.shard_map(local, mesh=mesh, in_specs=in_specs, out_specs=out_specs, check_vma=False)
```

time: 62.9 us -> 54.4 us (0.86)
  local copies, waits for them, and re-layouts: 5.19 us -> 0.01 us
  starting transfers between devices: 34 us -> 29.7 us
  other arithmetic: 0.02 us -> 2.28 us
  waiting for transfers between devices: 13.9 us -> 11.9 us
  Pallas kernels: 8.63 us -> 9.48 us
    ppermute x17, starting transfers between devices: 23 us -> 16.8 us  [exchanged(): lax.ppermute(x, axis, [(i, i ^ step) for i in range(lax.axis_size(axis))])]
    unnamed x12 -> x4, local copies, waits for them, and re-layouts: 5.19 us -> 0.01 us
    ppermute x0 -> x2, starting transfers between devices: none -> 4.35 us  [along(): lax.ppermute(x, 'ctx', [(i, (i + distance) % count) for i in range(count)])]
    ppermute x4 -> x2, starting transfers between devices: 11 us -> 8.55 us  [along(): lax.ppermute(x, 'ctx', [(i, i + distance) for i in range(first, last)])]
    concatenate x0 -> x2, other arithmetic: none -> 2.26 us  [the longest x1 1.27 us: local(): pair = jnp.concatenate([queries, grad_out], axis=1)]
    ppermute x17, waiting for transfers between devices: 13.9 us -> 11.9 us  [exchanged(): lax.ppermute(x, axis, [(i, i ^ step) for i in range(lax.axis_size(axis))])]
    pallas_call x9 -> x11, Pallas kernels: 8.63 us -> 9.48 us  [kernel_call(): pl.pallas_call(body, out_shape=out_shape, in_specs=in_specs, out_specs=[V...]
  transfers between devices with their start and end apart: 21 -> 21, of which waited for: 6 -> 9; matrix products, arithmetic and copies ran while one was open for 0% -> 4% of each run, Pallas kernels for 12% -> 16%
where the time goes in v3:
time: 54.4 us; the launch traced here: 54.2 us
  starting transfers between devices  29.7 us (55%)
  waiting for transfers between devices  11.9 us (22%)
  Pallas kernels  9.48 us (17%)
  other arithmetic  2.28 us (4%)
  between operations  0.77 us (1%)
    ppermute x17, starting transfers between devices, exchanged(): lax.ppermute(x, axis, [(i, i ^ step) for i in range(lax.axis_size(axis))])  16.8 us
    ppermute x17, waiting for transfers between devices, exchanged(): lax.ppermute(x, axis, [(i, i ^ step) for i in range(lax.axis_size(axis))])  11.9 us
    pallas_call x11, Pallas kernels, kernel_call(): pl.pallas_call(body, out_shape=out_shape, in_specs=in_specs, out_specs=[V...  9.48 us
    ppermute x2, starting transfers between devices, along(): lax.ppermute(x, 'ctx', [(i, i + distance) for i in range(first, last)])  8.55 us
    ppermute x2, starting transfers between devices, along(): lax.ppermute(x, 'ctx', [(i, (i + distance) % count) for i in range(count)])  4.35 us
    concatenate x1, other arithmetic, local(): pair = jnp.concatenate([queries, grad_out], axis=1)  1.27 us
  transfers between devices with their start and end apart: 21, of which 9 were waited for; matrix products, arithmetic and copies ran while one was open for 4% of the time, Pallas kernels for 16%

profile of v3, /device:TPU:0, one launch (start us, length us, event | category | flops | bytes accessed | tf_op | source)
XLA Modules:
  0.0 54.2 jit_solution(2073783544245478342)
XLA Ops:
  0.7 5.1 %collective-permute-start.1 = (bf16[128,512]{1,0:T(8,128)(2,1)}, bf16[128,512]{1,0:T(8,128)(2,1)S(1)}, u32[]{:S(2)}, u32[]{:S(2)}) collective-permute-start(bf16[128,512]{1,0:T(8,128)(2,1)} %bitcast.10), channel_id=1, source_target_pairs={{0,8},{2,10},{4,12},{6,14},{8,16},{10,18},{12,20},{14,22},{16,24},... | collective-permute-start | bytes 393224 | tf_op jit(solution)/shard_map/ppermute | solution.py:252
  5.7 3.5 %collective-permute-start = (bf16[128,512]{1,0:T(8,128)(2,1)}, bf16[128,512]{1,0:T(8,128)(2,1)S(1)}, u32[]{:S(2)}, u32[]{:S(2)}) collective-permute-start(bf16[128,512]{1,0:T(8,128)(2,1)} %bitcast.12), channel_id=1, source_target_pairs={{0,8},{2,10},{4,12},{6,14},{8,16},{10,18},{12,20},{14,22},{16,24},... | collective-permute-start | bytes 393224 | tf_op jit(solution)/shard_map/ppermute | solution.py:252
  9.2 1.0 %pad_maximum_fusion.1.own_ref.refs_0_ = bf16[128,1024]{1,0:T(8,128)(2,1)S(1)} fusion(bf16[128,512]{1,0:T(8,128)(2,1)} %bitcast.13, bf16[128,512]{1,0:T(8,128)(2,1)} %bitcast.11), kind=kLoop, calls=%fused_computation.1 | loop fusion | flops 524288 | bytes 524288 | tf_op jit(solution)/shard_map/concatenate | solution.py:265
  10.3 1.6 %collective-permute-start.3 = (bf16[128,512]{1,0:T(8,128)(2,1)S(1)}, bf16[128,512]{1,0:T(8,128)(2,1)S(1)}, u32[]{:S(2)}, u32[]{:S(2)}) collective-permute-start(bf16[128,512]{1,0:T(8,128)(2,1)S(1)} %get-tuple-element.40), channel_id=1, source_target_pairs={{0,4},{2,6},{4,0},{6,2},{8,12},{10,14},{12,8},{14,10},{16,20},{18,... | collective-permute-start | bytes 393224 | tf_op jit(solution)/shard_map/ppermute | solution.py:255
  11.9 1.4 %collective-permute-start.4 = (bf16[128,512]{1,0:T(8,128)(2,1)S(1)}, bf16[128,512]{1,0:T(8,128)(2,1)S(1)}, u32[]{:S(2)}, u32[]{:S(2)}) collective-permute-start(bf16[128,512]{1,0:T(8,128)(2,1)S(1)} %get-tuple-element.40), channel_id=1, source_target_pairs={{0,6},{2,4},{4,2},{6,0},{8,14},{10,12},{12,10},{14,8},{16,22},{18,... | collective-permute-start | bytes 393224 | tf_op jit(solution)/shard_map/ppermute | solution.py:255
  13.3 0.5 collective-permute-start.2
  13.8 1.3 %pad_maximum_fusion.pair_ref = bf16[128,4096]{1,0:T(8,128)(2,1)S(1)} fusion(bf16[128,2048]{1,0:T(8,128)(2,1)} %bitcast.8, bf16[128,2048]{1,0:T(8,128)(2,1)} %bitcast.9), kind=kLoop, calls=%fused_computation | loop fusion | flops 2097152 | bytes 2097152 | tf_op jit(solution)/shard_map/concatenate | solution.py:266
  15.1 0.6 %shard_map.93 = (f32[8,512]{1,0:T(8,128)S(1)}, f32[8,512]{1,0:T(8,128)S(1)}, bf16[128,512]{1,0:T(8,128)(2,1)S(1)}, bf16[128,512]{1,0:T(8,128)(2,1)S(1)}) custom-call(s32[1]{0:T(128)} %bitcast.place_ref, s32[1,16]{1,0:T(1,128)S(1)} %copy-done, f32[16]{0:T(128)S(1)} %copy-done.1, bf16[128,1024]{1,0:T(8,128)(2,1)S(1)} %pad_maximum_fusion.1.own_ref.refs_0_, ...), custom_call_target="tpu_custom_call" | custom-call | tf_op jit(solution)/shard_map/pallas_call | solution.py:32
  15.7 1.6 %collective-permute-start.6 = (bf16[128,512]{1,0:T(8,128)(2,1)S(1)}, bf16[128,512]{1,0:T(8,128)(2,1)S(1)}, u32[]{:S(2)}, u32[]{:S(2)}) collective-permute-start(bf16[128,512]{1,0:T(8,128)(2,1)S(1)} %get-tuple-element.44), channel_id=1, source_target_pairs={{0,4},{2,6},{4,0},{6,2},{8,12},{10,14},{12,8},{14,10},{16,20},{18,... | collective-permute-start | bytes 393224 | tf_op jit(solution)/shard_map/ppermute | solution.py:255
  17.3 1.4 %collective-permute-start.7 = (bf16[128,512]{1,0:T(8,128)(2,1)S(1)}, bf16[128,512]{1,0:T(8,128)(2,1)S(1)}, u32[]{:S(2)}, u32[]{:S(2)}) collective-permute-start(bf16[128,512]{1,0:T(8,128)(2,1)S(1)} %get-tuple-element.44), channel_id=1, source_target_pairs={{0,6},{2,4},{4,2},{6,0},{8,14},{10,12},{12,10},{14,8},{16,22},{18,... | collective-permute-start | bytes 393224 | tf_op jit(solution)/shard_map/ppermute | solution.py:255
  18.8 0.5 collective-permute-start.5
  19.3 0.7 %collective-permute-done.2.refs_1_ = bf16[128,512]{1,0:T(8,128)(2,1)S(1)} collective-permute-done((bf16[128,512]{1,0:T(8,128)(2,1)S(1)}, bf16[128,512]{1,0:T(8,128)(2,1)S(1)}, u32[]{:S(2)}, u32[]{:S(2)}) %collective-permute-start.2) | collective-permute-done | bytes 131104 | tf_op jit(solution)/shard_map/ppermute | solution.py:255
  20.0 2.7 %shard_map.95 = (bf16[2048,512]{1,0:T(8,128)(2,1)S(1)}, f32[8,512]{1,0:T(8,128)S(1)}, f32[128,512]{1,0:T(8,128)S(1)}, f32[128,512]{1,0:T(8,128)S(1)}, bf16[128,5...) custom-call(f32[8,512]{1,0:T(8,128)S(1)} %get-tuple-element.37.caps_ref, ...), custom_call_target="tpu_custom_call" | custom-call | tf_op jit(solution)/shard_map/pallas_call | solution.py:32
  22.7 1.6 %collective-permute-start.11 = (bf16[128,512]{1,0:T(8,128)(2,1)S(1)}, bf16[128,512]{1,0:T(8,128)(2,1)S(1)}, u32[]{:S(2)}, u32[]{:S(2)}) collective-permute-start(bf16[128,512]{1,0:T(8,128)(2,1)S(1)} %get-tuple-element.57), channel_id=1, source_target_pairs={{0,2},{2,0},{4,6},{6,4},{8,10},{10,8},{12,14},{14,12},{16,18},{18,... | collective-permute-start | bytes 393224 | tf_op jit(solution)/shard_map/ppermute | solution.py:255
  24.3 1.5 %collective-permute-start.12 = (bf16[128,512]{1,0:T(8,128)(2,1)S(1)}, bf16[128,512]{1,0:T(8,128)(2,1)S(1)}, u32[]{:S(2)}, u32[]{:S(2)}) collective-permute-start(bf16[128,512]{1,0:T(8,128)(2,1)S(1)} %get-tuple-element.58), channel_id=1, source_target_pairs={{0,4},{2,6},{4,0},{6,2},{8,12},{10,14},{12,8},{14,10},{16,20},{18,... | collective-permute-start | bytes 393224 | tf_op jit(solution)/shard_map/ppermute | solution.py:255
  25.8 0.5 collective-permute-start.13
  26.5 2.3 %shard_map.96 = (bf16[2560,512]{1,0:T(8,128)(2,1)S(1)}, f32[1,128]{1,0:T(1,128)S(1)}, f32[128,512]{1,0:T(8,128)S(1)}, f32[128,512]{1,0:T(8,128)S(1)}, bf16[128,5...) custom-call(bf16[2048,512]{1,0:T(8,128)(2,1)S(1)} %get-tuple-element.41.probs_ref, ...), custom_call_target="tpu_custom_call" | custom-call | tf_op jit(solution)/shard_map/pallas_call | solution.py:32
  28.9 2.5 %collective-permute-start.10 = (bf16[128,512]{1,0:T(8,128)(2,1)S(1)}, bf16[128,512]{1,0:T(8,128)(2,1)S(1)}, u32[]{:S(2)}, u32[]{:S(2)}) collective-permute-start(bf16[128,512]{1,0:T(8,128)(2,1)S(1)} %get-tuple-element.51), channel_id=1, source_target_pairs={{0,6},{2,4},{4,2},{6,0},{8,14},{10,12},{12,10},{14,8},{16,22},{18,... | collective-permute-start | bytes 393224 | tf_op jit(solution)/shard_map/ppermute | solution.py:255
  31.4 0.5 collective-permute-start.8
  31.9 0.5 collective-permute-start.9
  33.3 3.9 %collective-permute-start.19 = (bf16[128,512]{1,0:T(8,128)(2,1)S(1)}, bf16[128,512]{1,0:T(8,128)(2,1)S(1)}, u32[]{:S(2)}, u32[]{:S(2)}) collective-permute-start(bf16[128,512]{1,0:T(8,128)(2,1)S(1)} %get-tuple-element.65), channel_id=1, source_target_pairs={{0,24},{2,26},{4,28},{6,30},{8,0},{10,2},{12,4},{14,6},{16,8},{18,... | collective-permute-start | bytes 393224 | tf_op jit(solution)/shard_map/ppermute | solution.py:250
  37.2 1.1 %collective-permute-done.14 = f32[1,128]{1,0:T(1,128)S(1)} collective-permute-done((f32[1,128]{1,0:T(1,128)S(1)}, f32[1,128]{1,0:T(1,128)S(1)}, u32[]{:S(2)}, u32[]{:S(2)}) %collective-permute-start.14) | collective-permute-done | bytes 544 | tf_op jit(solution)/shard_map/ppermute | solution.py:255
  38.3 3.5 %collective-permute-done.15 = f32[1,128]{1,0:T(1,128)S(1)} collective-permute-done((f32[1,128]{1,0:T(1,128)S(1)}, f32[1,128]{1,0:T(1,128)S(1)}, u32[]{:S(2)}, u32[]{:S(2)}) %collective-permute-start.15) | collective-permute-done | bytes 544 | tf_op jit(solution)/shard_map/ppermute | solution.py:255
  41.8 1.7 %shard_map.97 = (bf16[128,2048]{1,0:T(8,128)(2,1)}, f32[1,128]{1,0:T(1,128)S(1)}) custom-call(bf16[2560,512]{1,0:T(8,128)(2,1)S(1)} %get-tuple-element.45.gscores_ref, bf16[128,1024]{1,0:T(8,128)(2,1)S(1)} %pad_maximum_fusion.1.own_ref.refs_0_, bf16[128,512]{1,0:T(8,128)(2,1)S(1)} %collective-permute-done.2.refs_1_, ...), custom_call_target="tpu_custom_call" | custom-call | tf_op jit(solution)/shard_map/pallas_call | solution.py:32
  43.5 0.6 %shard_map.98 = (f32[128,512]{1,0:T(8,128)S(1)}, bf16[128,512]{1,0:T(8,128)(2,1)S(1)}, f32[1,128]{1,0:T(1,128)}) custom-call(s32[1]{0:T(128)} %bitcast.place_ref, f32[128,512]{1,0:T(8,128)S(1)} %get-tuple-element.47.own_ref, f32[128,512]{1,0:T(8,128)S(1)} %get-tuple-element.48.before_ref, bf16[128,512]{1,0:T(8,128)(2,1)S(1)} %collective-permute-done.8.refs_0_, ...), custom_call_target="tpu_custom_call" | custom-call | tf_op jit(solution)/shard_map/pallas_call | solution.py:32
  44.1 2.2 %collective-permute-done.16 = f32[1,128]{1,0:T(1,128)S(1)} collective-permute-done((f32[1,128]{1,0:T(1,128)S(1)}, f32[1,128]{1,0:T(1,128)S(1)}, u32[]{:S(2)}, u32[]{:S(2)}) %collective-permute-start.16) | collective-permute-done | bytes 544 | tf_op jit(solution)/shard_map/ppermute | solution.py:255
  46.3 1.6 %collective-permute-start.18 = (f32[1,128]{1,0:T(1,128)S(1)}, f32[1,128]{1,0:T(1,128)S(1)}, u32[]{:S(2)}, u32[]{:S(2)}) collective-permute-start(f32[1,128]{1,0:T(1,128)S(1)} %get-tuple-element.63), channel_id=1, source_target_pairs={{0,2},{2,0},{4,6},{6,4},{8,10},{10,8},{12,14},{14,12},{16,18},{18,... | collective-permute-start | bytes 1544 | tf_op jit(solution)/shard_map/ppermute | solution.py:255
  48.3 0.7 %shard_map.102 = (bf16[128,512]{1,0:T(8,128)(2,1)}, f32[1,128]{1,0:T(1,128)S(1)}) custom-call(f32[128,512]{1,0:T(8,128)S(1)} %get-tuple-element.64.own_ref, bf16[128,512]{1,0:T(8,128)(2,1)S(1)} %collective-permute-done.19.last_ref), custom_call_target="tpu_custom_call" | custom-call | tf_op jit(solution)/shard_map/pallas_call | solution.py:32
  49.0 0.9 %collective-permute-done.18 = f32[1,128]{1,0:T(1,128)S(1)} collective-permute-done((f32[1,128]{1,0:T(1,128)S(1)}, f32[1,128]{1,0:T(1,128)S(1)}, u32[]{:S(2)}, u32[]{:S(2)}) %collective-permute-start.18) | collective-permute-done | bytes 544 | tf_op jit(solution)/shard_map/ppermute | solution.py:255
  49.9 1.1 %collective-permute-start.20 = (f32[1,128]{1,0:T(1,128)S(1)}, f32[1,128]{1,0:T(1,128)S(1)}, u32[]{:S(2)}, u32[]{:S(2)}) collective-permute-start(f32[1,128]{1,0:T(1,128)S(1)} %add_add_fusion), channel_id=1, source_target_pairs={{0,4},{2,6},{4,0},{6,2},{8,12},{10,14},{12,8},{14,10},{16,20},{18,... | collective-permute-start | bytes 1544 | tf_op jit(solution)/shard_map/ppermute | solution.py:255
  51.0 2.5 %collective-permute-done.20 = f32[1,128]{1,0:T(1,128)S(1)} collective-permute-done((f32[1,128]{1,0:T(1,128)S(1)}, f32[1,128]{1,0:T(1,128)S(1)}, u32[]{:S(2)}, u32[]{:S(2)}) %collective-permute-start.20) | collective-permute-done | bytes 544 | tf_op jit(solution)/shard_map/ppermute | solution.py:255
  53.5 0.7 %shard_map.103 = (bf16[128,512]{1,0:T(8,128)(2,1)}, f32[16]{0:T(128)}) custom-call(bf16[128,512]{1,0:T(8,128)(2,1)S(1)} %shard_map.101.keys_ref, f32[1,128]{1,0:T(1,128)S(1)} %add.27.sink_ref, f32[1,128]{1,0:T(1,128)S(1)} %get-tuple-element.66.done_ref), custom_call_target="tpu_custom_call" | custom-call | tf_op jit(solution)/shard_map/pallas_call | solution.py:32
  (33 shorter events, 1.7 us)
Async XLA Ops:
  0.6 14.5 %copy-start.1 = (f32[16]{0:T(128)S(1)}, f32[16]{0:T(128)}, u32[]{:S(2)}) copy-start(f32[16]{0:T(128)} %sinks_ref.1) | copy-start | bytes 196
  0.6 14.5 %copy-start = (s32[1,16]{1,0:T(1,128)S(1)}, s32[1,16]{1,0:T(1,128)}, u32[]{:S(2)}) copy-start(s32[1,16]{1,0:T(1,128)} %docs_ref.1) | copy-start | bytes 196
  0.7 9.6 %collective-permute-start.1 = (bf16[128,512]{1,0:T(8,128)(2,1)}, bf16[128,512]{1,0:T(8,128)(2,1)S(1)}, u32[]{:S(2)}, u32[]{:S(2)}) collective-permute-start(bf16[128,512]{1,0:T(8,128)(2,1)} %bitcast.10), channel_id=1, source_target_pairs={{0,8},{2,10},{4,12},{6,14},{8,16},{10,18},{12,20},{14,22},{16,24},... | collective-permute-start | bytes 393224 | tf_op jit(solution)/shard_map/ppermute | solution.py:252
  5.7 9.4 %collective-permute-start = (bf16[128,512]{1,0:T(8,128)(2,1)}, bf16[128,512]{1,0:T(8,128)(2,1)S(1)}, u32[]{:S(2)}, u32[]{:S(2)}) collective-permute-start(bf16[128,512]{1,0:T(8,128)(2,1)} %bitcast.12), channel_id=1, source_target_pairs={{0,8},{2,10},{4,12},{6,14},{8,16},{10,18},{12,20},{14,22},{16,24},... | collective-permute-start | bytes 393224 | tf_op jit(solution)/shard_map/ppermute | solution.py:252
  10.3 8.5 %collective-permute-start.3 = (bf16[128,512]{1,0:T(8,128)(2,1)S(1)}, bf16[128,512]{1,0:T(8,128)(2,1)S(1)}, u32[]{:S(2)}, u32[]{:S(2)}) collective-permute-start(bf16[128,512]{1,0:T(8,128)(2,1)S(1)} %get-tuple-element.40), channel_id=1, source_target_pairs={{0,4},{2,6},{4,0},{6,2},{8,12},{10,14},{12,8},{14,10},{16,20},{18,... | collective-permute-start | bytes 393224 | tf_op jit(solution)/shard_map/ppermute | solution.py:255
  11.9 7.4 %collective-permute-start.4 = (bf16[128,512]{1,0:T(8,128)(2,1)S(1)}, bf16[128,512]{1,0:T(8,128)(2,1)S(1)}, u32[]{:S(2)}, u32[]{:S(2)}) collective-permute-start(bf16[128,512]{1,0:T(8,128)(2,1)S(1)} %get-tuple-element.40), channel_id=1, source_target_pairs={{0,6},{2,4},{4,2},{6,0},{8,14},{10,12},{12,10},{14,8},{16,22},{18,... | collective-permute-start | bytes 393224 | tf_op jit(solution)/shard_map/ppermute | solution.py:255
  13.3 6.7 %collective-permute-start.2 = (bf16[128,512]{1,0:T(8,128)(2,1)S(1)}, bf16[128,512]{1,0:T(8,128)(2,1)S(1)}, u32[]{:S(2)}, u32[]{:S(2)}) collective-permute-start(bf16[128,512]{1,0:T(8,128)(2,1)S(1)} %get-tuple-element.39), channel_id=1, source_target_pairs={{0,2},{2,0},{4,6},{6,4},{8,10},{10,8},{12,14},{14,12},{16,18},{18,... | collective-permute-start | bytes 393224 | tf_op jit(solution)/shard_map/ppermute | solution.py:255
  15.7 10.1 %collective-permute-start.6 = (bf16[128,512]{1,0:T(8,128)(2,1)S(1)}, bf16[128,512]{1,0:T(8,128)(2,1)S(1)}, u32[]{:S(2)}, u32[]{:S(2)}) collective-permute-start(bf16[128,512]{1,0:T(8,128)(2,1)S(1)} %get-tuple-element.44), channel_id=1, source_target_pairs={{0,4},{2,6},{4,0},{6,2},{8,12},{10,14},{12,8},{14,10},{16,20},{18,... | collective-permute-start | bytes 393224 | tf_op jit(solution)/shard_map/ppermute | solution.py:255
  17.3 9.0 %collective-permute-start.7 = (bf16[128,512]{1,0:T(8,128)(2,1)S(1)}, bf16[128,512]{1,0:T(8,128)(2,1)S(1)}, u32[]{:S(2)}, u32[]{:S(2)}) collective-permute-start(bf16[128,512]{1,0:T(8,128)(2,1)S(1)} %get-tuple-element.44), channel_id=1, source_target_pairs={{0,6},{2,4},{4,2},{6,0},{8,14},{10,12},{12,10},{14,8},{16,22},{18,... | collective-permute-start | bytes 393224 | tf_op jit(solution)/shard_map/ppermute | solution.py:255
  18.8 7.7 %collective-permute-start.5 = (bf16[128,512]{1,0:T(8,128)(2,1)S(1)}, bf16[128,512]{1,0:T(8,128)(2,1)S(1)}, u32[]{:S(2)}, u32[]{:S(2)}) collective-permute-start(bf16[128,512]{1,0:T(8,128)(2,1)S(1)} %get-tuple-element.43), channel_id=1, source_target_pairs={{0,2},{2,0},{4,6},{6,4},{8,10},{10,8},{12,14},{14,12},{16,18},{18,... | collective-permute-start | bytes 393224 | tf_op jit(solution)/shard_map/ppermute | solution.py:255
  22.7 9.2 %collective-permute-start.11 = (bf16[128,512]{1,0:T(8,128)(2,1)S(1)}, bf16[128,512]{1,0:T(8,128)(2,1)S(1)}, u32[]{:S(2)}, u32[]{:S(2)}) collective-permute-start(bf16[128,512]{1,0:T(8,128)(2,1)S(1)} %get-tuple-element.57), channel_id=1, source_target_pairs={{0,2},{2,0},{4,6},{6,4},{8,10},{10,8},{12,14},{14,12},{16,18},{18,... | collective-permute-start | bytes 393224 | tf_op jit(solution)/shard_map/ppermute | solution.py:255
  24.3 8.3 %collective-permute-start.12 = (bf16[128,512]{1,0:T(8,128)(2,1)S(1)}, bf16[128,512]{1,0:T(8,128)(2,1)S(1)}, u32[]{:S(2)}, u32[]{:S(2)}) collective-permute-start(bf16[128,512]{1,0:T(8,128)(2,1)S(1)} %get-tuple-element.58), channel_id=1, source_target_pairs={{0,4},{2,6},{4,0},{6,2},{8,12},{10,14},{12,8},{14,10},{16,20},{18,... | collective-permute-start | bytes 393224 | tf_op jit(solution)/shard_map/ppermute | solution.py:255
  25.8 7.3 %collective-permute-start.13 = (bf16[128,512]{1,0:T(8,128)(2,1)S(1)}, bf16[128,512]{1,0:T(8,128)(2,1)S(1)}, u32[]{:S(2)}, u32[]{:S(2)}) collective-permute-start(bf16[128,512]{1,0:T(8,128)(2,1)S(1)} %get-tuple-element.59), channel_id=1, source_target_pairs={{0,6},{2,4},{4,2},{6,0},{8,14},{10,12},{12,10},{14,8},{16,22},{18,... | collective-permute-start | bytes 393224 | tf_op jit(solution)/shard_map/ppermute | solution.py:255
  28.9 14.7 %collective-permute-start.10 = (bf16[128,512]{1,0:T(8,128)(2,1)S(1)}, bf16[128,512]{1,0:T(8,128)(2,1)S(1)}, u32[]{:S(2)}, u32[]{:S(2)}) collective-permute-start(bf16[128,512]{1,0:T(8,128)(2,1)S(1)} %get-tuple-element.51), channel_id=1, source_target_pairs={{0,6},{2,4},{4,2},{6,0},{8,14},{10,12},{12,10},{14,8},{16,22},{18,... | collective-permute-start | bytes 393224 | tf_op jit(solution)/shard_map/ppermute | solution.py:255
  31.4 12.2 %collective-permute-start.8 = (bf16[128,512]{1,0:T(8,128)(2,1)S(1)}, bf16[128,512]{1,0:T(8,128)(2,1)S(1)}, u32[]{:S(2)}, u32[]{:S(2)}) collective-permute-start(bf16[128,512]{1,0:T(8,128)(2,1)S(1)} %get-tuple-element.49), channel_id=1, source_target_pairs={{0,2},{2,0},{4,6},{6,4},{8,10},{10,8},{12,14},{14,12},{16,18},{18,... | collective-permute-start | bytes 393224 | tf_op jit(solution)/shard_map/ppermute | solution.py:255
  31.9 11.6 %collective-permute-start.9 = (bf16[128,512]{1,0:T(8,128)(2,1)S(1)}, bf16[128,512]{1,0:T(8,128)(2,1)S(1)}, u32[]{:S(2)}, u32[]{:S(2)}) collective-permute-start(bf16[128,512]{1,0:T(8,128)(2,1)S(1)} %get-tuple-element.50), channel_id=1, source_target_pairs={{0,4},{2,6},{4,0},{6,2},{8,12},{10,14},{12,8},{14,10},{16,20},{18,... | collective-permute-start | bytes 393224 | tf_op jit(solution)/shard_map/ppermute | solution.py:255
  33.3 15.0 %collective-permute-start.19 = (bf16[128,512]{1,0:T(8,128)(2,1)S(1)}, bf16[128,512]{1,0:T(8,128)(2,1)S(1)}, u32[]{:S(2)}, u32[]{:S(2)}) collective-permute-start(bf16[128,512]{1,0:T(8,128)(2,1)S(1)} %get-tuple-element.65), channel_id=1, source_target_pairs={{0,24},{2,26},{4,28},{6,30},{8,0},{10,2},{12,4},{14,6},{16,8},{18,... | collective-permute-start | bytes 393224 | tf_op jit(solution)/shard_map/ppermute | solution.py:250
  37.2 1.1 %collective-permute-start.14 = (f32[1,128]{1,0:T(1,128)S(1)}, f32[1,128]{1,0:T(1,128)S(1)}, u32[]{:S(2)}, u32[]{:S(2)}) collective-permute-start(f32[1,128]{1,0:T(1,128)S(1)} %add.21), channel_id=1, source_target_pairs={{0,1},{1,0},{2,3},{3,2},{4,5},{5,4},{6,7},{7,6},{8,9},{9,8},{10,11... | collective-permute-start | bytes 1544 | tf_op jit(solution)/shard_map/ppermute | solution.py:255
  38.3 3.5 %collective-permute-start.15 = (f32[1,128]{1,0:T(1,128)S(1)}, f32[1,128]{1,0:T(1,128)S(1)}, u32[]{:S(2)}, u32[]{:S(2)}) collective-permute-start(f32[1,128]{1,0:T(1,128)S(1)} %add.22), channel_id=1, source_target_pairs={{0,8},{2,10},{4,12},{6,14},{8,0},{10,2},{12,4},{14,6},{16,24},{18,... | collective-permute-start | bytes 1544 | tf_op jit(solution)/shard_map/ppermute | solution.py:255
  41.8 4.4 %collective-permute-start.16 = (f32[1,128]{1,0:T(1,128)S(1)}, f32[1,128]{1,0:T(1,128)S(1)}, u32[]{:S(2)}, u32[]{:S(2)}) collective-permute-start(f32[1,128]{1,0:T(1,128)S(1)} %add.23), channel_id=1, source_target_pairs={{0,16},{2,18},{4,20},{6,22},{8,24},{10,26},{12,28},{14,30},{16,0},... | collective-permute-start | bytes 1544 | tf_op jit(solution)/shard_map/ppermute | solution.py:255
  46.3 3.6 %collective-permute-start.18 = (f32[1,128]{1,0:T(1,128)S(1)}, f32[1,128]{1,0:T(1,128)S(1)}, u32[]{:S(2)}, u32[]{:S(2)}) collective-permute-start(f32[1,128]{1,0:T(1,128)S(1)} %get-tuple-element.63), channel_id=1, source_target_pairs={{0,2},{2,0},{4,6},{6,4},{8,10},{10,8},{12,14},{14,12},{16,18},{18,... | collective-permute-start | bytes 1544 | tf_op jit(solution)/shard_map/ppermute | solution.py:255
  47.8 5.6 %collective-permute-start.17 = (bf16[128,512]{1,0:T(8,128)(2,1)S(1)}, bf16[128,512]{1,0:T(8,128)(2,1)S(1)}, u32[]{:S(2)}, u32[]{:S(2)}) collective-permute-start(bf16[128,512]{1,0:T(8,128)(2,1)S(1)} %get-tuple-element.62), channel_id=1, source_target_pairs={{0,24},{2,26},{4,28},{6,30},{8,0},{10,2},{12,4},{14,6},{16,8},{18,... | collective-permute-start | bytes 393224 | tf_op jit(solution)/shard_map/ppermute | solution.py:250
  49.9 3.5 %collective-permute-start.20 = (f32[1,128]{1,0:T(1,128)S(1)}, f32[1,128]{1,0:T(1,128)S(1)}, u32[]{:S(2)}, u32[]{:S(2)}) collective-permute-start(f32[1,128]{1,0:T(1,128)S(1)} %add_add_fusion), channel_id=1, source_target_pairs={{0,4},{2,6},{4,0},{6,2},{8,12},{10,14},{12,8},{14,10},{16,20},{18,... | collective-permute-start | bytes 1544 | tf_op jit(solution)/shard_map/ppermute | solution.py:255

commit v4 on v3

--- a/solution.py
+++ b/solution.py
@@ -9,6 +9,7 @@
 
 WINDOW = 512
 LOG2E = 1.4426950408889634
+TERM_ROWS = 16
 
 F32 = jnp.float32
 BF16 = jnp.bfloat16
@@ -28,14 +29,14 @@
     return lax.dot_general(a, b, (((0,), (0,)), ((), ())), preferred_element_type=F32)
 
 
-def kernel_call(body, out_shape, in_specs, operands):
+def kernel_call(body, out_shape, in_specs, operands, flops=0):
     return pl.pallas_call(
         body,
         out_shape=out_shape,
         in_specs=in_specs,
         out_specs=[VMEM] * len(out_shape),
         compiler_params=pltpu.CompilerParams(vmem_limit_bytes=24 * 1024 * 1024),
-        cost_estimate=pl.CostEstimate(flops=0, bytes_accessed=0, transcendentals=0),
+        cost_estimate=pl.CostEstimate(flops=flops, bytes_accessed=0, transcendentals=0),
     )(*operands)
 
 
@@ -44,12 +45,12 @@
 
 
 def choose(slot, own, before_ref, out_refs):
-    for bit, ref in enumerate(out_refs):
-        @pl.when(later(slot, 1 << bit))
+    for step, ref in enumerate(out_refs, 1):
+        @pl.when(later(slot, step))
         def _():
             ref[...] = own
 
-        @pl.when(jnp.logical_not(later(slot, 1 << bit)))
+        @pl.when(jnp.logical_not(later(slot, step)))
         def _():
             ref[...] = before_ref[...]
 
@@ -94,15 +95,29 @@
     return jnp.where(causal, x, zero), jnp.where(causal, zero, x)
 
 
+def split_terms(row):
+    parts = []
+    for _ in range(3):
+        parts.append(row.astype(BF16))
+        row = row - parts[-1].astype(F32)
+    return jnp.concatenate(parts + [jnp.zeros((TERM_ROWS - 3, row.shape[1]), BF16)], axis=0)
+
+
+def joined_terms(terms):
+    parts = terms.astype(F32)
+    return (parts[2:3] + parts[1:2]) + parts[0:1]
+
+
 def stacked(ref, first, group, size):
     return jnp.concatenate([ref[:, (first + j) * size:(first + j + 1) * size] for j in range(group)], axis=0)
 
 
-def store_shares(x, cut, rows, reach, own_ref, before_ref, message_refs):
-    own_ref[:, cut] = block(x, 0, rows)
-    before_ref[:, cut] = block(x, reach, rows)
+def store_shares(x, head, rows, reach, own_ref, before_ref, message_refs):
+    at = slice(head * rows, (head + 1) * rows)
+    own_ref[at, :] = block(x, 0, rows)
+    before_ref[at, :] = block(x, reach, rows)
     for i, ref in enumerate(message_refs, 1):
-        ref[:, cut] = block(x, i, rows).astype(BF16)
+        ref[at, :] = block(x, i, rows).astype(BF16)
 
 
 def probs_kernel(kv_heads, group, reach, rows, size, caps_ref, tops_ref, pair_ref, *refs):
@@ -140,7 +155,7 @@
         sink_ref[head:head + 1, :] = sink_weight * inverse
         first, last = parted(probs[0], causal)
         dv = dot_nn(jnp.concatenate([first] + probs[1:] + [last], axis=0), g)
-        store_shares(dv, cut, rows, reach, own_ref, before_ref, message_refs)
+        store_shares(dv, head, rows, reach, own_ref, before_ref, message_refs)
 
 
 def scores_kernel(kv_heads, group, reach, rows, size, probs_ref, sinkp_ref, pair_ref, *refs):
@@ -172,16 +187,20 @@
         span = (reach + 1) * rows
         gscores_ref[head * span:(head + 1) * span, :] = gscores
         dk = dot_nn(gscores, q) * scale
-        store_shares(dk, cut, rows, reach, own_ref, before_ref, message_refs)
+        store_shares(dk, head, rows, reach, own_ref, before_ref, message_refs)
         sink_terms = sinkp_ref[head:head + 1, :] * delta
         for j in range(group):
             term = jnp.sum(sink_terms[:, j * rows:(j + 1) * rows], axis=1, keepdims=True)
             sink_row = jnp.where(lane == head * group + j, -term, sink_row)
     sink_ref[...] = sink_row
-
-
-def queries_kernel(kv_heads, group, reach, rows, size, gscores_ref, *refs):
-    *blocks, dq_ref, done_ref = refs
+    terms = split_terms(sink_row)
+    for ref in message_refs:
+        ref[kv_heads * rows:, :] = terms
+
+
+def queries_kernel(kv_heads, group, reach, rows, size, gscores_ref, own_ref, last_ref, *refs):
+    *blocks, dv_ref, dq_ref, done_ref = refs
+    side_by_side(own_ref, last_ref[...], dv_ref)
     scale = size ** (-0.5)
     span = (reach + 1) * rows
     for head in range(kv_heads):
@@ -194,37 +213,55 @@
     done_ref[...] = jnp.zeros_like(done_ref)
 
 
-def combine_kernel(reach, place_ref, own_ref, before_ref, *refs):
-    *messages, own_out, before_out, done_ref = refs
+def combine(reach, place_ref, own_ref, before_ref, messages, own_out, before_out):
     slot = lax.rem(place_ref[0], reach)
     own, before = own_ref[...], before_ref[...]
     for step, message in enumerate(messages, 1):
         mine = later(slot, step)
-        back = message[...].astype(F32)
+        back = message[:own.shape[0], :].astype(F32)
         own = own + jnp.where(mine, back, 0.0)
         before = before + jnp.where(mine, 0.0, back)
     own_out[...] = own
     before_out[...] = before.astype(BF16)
-    done_ref[...] = jnp.zeros_like(done_ref)
-
-
-def joined_kernel(share_ref, sink_ref, done_ref, share_out, sink_out):
-    share_out[...] = share_ref[...]
-    sink_out[...] = sink_ref[...] + done_ref[...]
-
-
-def out_kernel(keys_ref, sink_ref, done_ref, keys_out, sink_out):
+
+
+def values_kernel(reach, place_ref, own_ref, before_ref, *refs):
+    *messages, own_out, before_out = refs
+    combine(reach, place_ref, own_ref, before_ref, messages, own_out, before_out)
+
+
+def sums_kernel(reach, place_ref, own_ref, before_ref, sink_ref, *refs):
+    *messages, own_out, before_out, sink_out = refs
+    height = own_ref.shape[0]
+    combine(reach, place_ref, own_ref, before_ref, messages, own_out, before_out.at[:height, :])
+    sink_row = sink_ref[...]
+    for message in messages:
+        sink_row = sink_row + joined_terms(message[height:, :])
+    before_out[height:, :] = split_terms(sink_row)
+    sink_out[...] = sink_row
+
+
+def side_by_side(own_ref, last, out_ref):
+    rows, width = out_ref.shape
+    total = own_ref[...] + last.astype(F32)
+    size = total.shape[1]
+    for head in range(width // size):
+        out_ref[:, head * size:(head + 1) * size] = block(total, head, rows).astype(BF16)
+
+
+def totals_kernel(own_ref, last_ref, sink_ref, *refs):
+    *sink_refs, keys_out, sink_out = refs
+    height = own_ref.shape[0]
+    side_by_side(own_ref, last_ref[:height, :], keys_out)
+    sink_row = sink_ref[...] + joined_terms(last_ref[height:, :])
+    for ref in sink_refs:
+        sink_row = sink_row + ref[...]
+    sink_out[...] = sink_row
+
+
+def out_kernel(keys_ref, sink_ref, keys_out, sink_out):
     keys_out[...] = keys_ref[...]
     sink_out[...] = sink_ref[0, :sink_out.shape[0]]
-
-
-def total_kernel(own_ref, last_ref, out_ref):
-    out_ref[...] = (own_ref[...] + last_ref[...].astype(F32)).astype(BF16)
-
-
-def end_kernel(own_ref, last_ref, out_ref, done_ref):
-    done_ref[...] = jnp.zeros_like(done_ref)
-    out_ref[...] = (own_ref[...] + last_ref[...].astype(F32)).astype(BF16)
 
 
 def local(queries, keys, values, grad_out, sinks, doc_ids):
@@ -238,27 +275,21 @@
     count = lax.axis_size("ctx")
     place = jnp.full((1,), lax.axis_index("ctx"), jnp.int32)
     queries, keys, values, grad_out = queries[0], keys[0], values[0], grad_out[0]
-    wide = jax.ShapeDtypeStruct(keys.shape, F32)
     narrow = jax.ShapeDtypeStruct(keys.shape, BF16)
+    wide = jax.ShapeDtypeStruct((kv_heads * rows, size), F32)
+    share = jax.ShapeDtypeStruct(wide.shape, BF16)
+    message = jax.ShapeDtypeStruct((kv_heads * rows + TERM_ROWS, size), BF16)
     row = jax.ShapeDtypeStruct((1, 128), F32)
     columns = group * rows
     table = jax.ShapeDtypeStruct((8 * (-(-max(reach + 1, kv_heads) // 8)), columns), F32)
     sizes = (kv_heads, group, reach, rows, size)
+    span = (reach + 1) * rows
 
     def along(x, distance):
-        if distance < 0:
-            return lax.ppermute(x, "ctx", [(i, (i + distance) % count) for i in range(count)])
-        first, last = max(0, -distance), min(count, count - distance)
-        return lax.ppermute(x, "ctx", [(i, i + distance) for i in range(first, last)])
+        return lax.ppermute(x, "ctx", [(i, (i + distance) % count) for i in range(count)])
 
     def exchanged(x, step, axis="ctx"):
         return lax.ppermute(x, axis, [(i, i ^ step) for i in range(lax.axis_size(axis))])
-
-    def summed_over(x, first, end):
-        while first < end:
-            x = x + exchanged(x, first)
-            first *= 2
-        return x
 
     keys_before = along(keys, reach)
     values_before = along(values, reach)
@@ -266,9 +297,10 @@
     pair = jnp.concatenate([queries, grad_out], axis=1)
 
     def gathered(own, chosen, before):
-        return [own, *(exchanged(chosen[step.bit_length() - 1], step) for step in range(1, reach)), before]
-
-    choices = [narrow] * (reach.bit_length() - 1)
+        arrived = [exchanged(chosen[step - 1], step) for step in range(1, reach)]
+        return [own, *arrived, before]
+
+    choices = [narrow] * (reach - 1)
     chosen = kernel_call(
         functools.partial(keys_kernel, reach), choices, [SMEM, VMEM, VMEM], (place, own, keys_before)
     )
@@ -282,7 +314,7 @@
     value_blocks = gathered(own, chosen, values_before)
     probs, sink_probs, values_own, values_share, *messages = kernel_call(
         functools.partial(probs_kernel, *sizes),
-        [jax.ShapeDtypeStruct((kv_heads * reach * rows, columns), BF16), table, wide, wide] + [narrow] * (reach - 1),
+        [jax.ShapeDtypeStruct((kv_heads * reach * rows, columns), BF16), table, wide, wide] + [share] * (reach - 1),
         [VMEM] * (4 + reach),
         (caps, tops, pair, *key_blocks),
     )
@@ -290,48 +322,46 @@
     gscores, sink_row, keys_own, keys_share, *messages = kernel_call(
         functools.partial(scores_kernel, *sizes),
         [jax.ShapeDtypeStruct((kv_heads * (reach + 1) * rows, columns), BF16), row, wide, wide]
-        + [narrow] * (reach - 1),
+        + [message] * (reach - 1),
         [VMEM] * (4 + reach),
         (probs, sink_probs, pair, *value_blocks),
     )
     keys_back = [exchanged(m, step) for step, m in enumerate(messages, 1)]
-    grad_queries, dq_done = kernel_call(
+    values_own, values_share = kernel_call(
+        functools.partial(values_kernel, reach),
+        [wide, share],
+        [SMEM] + [VMEM] * (reach + 1),
+        (place, values_own, values_share, *values_back),
+    )
+    values_last = along(values_share, -reach)
+    keys_own, keys_share, sink_row = kernel_call(
+        functools.partial(sums_kernel, reach),
+        [wide, message, row],
+        [SMEM] + [VMEM] * (reach + 2),
+        (place, keys_own, keys_share, sink_row, *keys_back),
+    )
+    keys_last = along(keys_share, -reach)
+    grad_values, grad_queries, done = kernel_call(
         functools.partial(queries_kernel, *sizes),
-        [jax.ShapeDtypeStruct(queries.shape, BF16), row],
-        [VMEM] * (2 + reach),
-        (gscores, *key_blocks),
-    )
-
-    def combined(own, share, back):
-        return kernel_call(
-            functools.partial(combine_kernel, reach),
-            [wide, narrow, row],
-            [SMEM] + [VMEM] * (reach + 1),
-            (place, own, share, *back),
-        )
-
-    values_own, values_share, done = combined(values_own, values_share, values_back)
-    values_last = along(values_share, -reach)
-    sink_row = sink_row + done
+        [narrow, jax.ShapeDtypeStruct(queries.shape, BF16), row],
+        [VMEM] * (4 + reach),
+        (gscores, values_own, values_last, *key_blocks),
+        2 * rows * group * span * size * kv_heads,
+    )
+    sink_rows = [sink_row] + [along(sink_row, -distance) for distance in range(2 * reach, count, reach)]
+    sink_rows.append(done)
+    grad_keys, sink_row = kernel_call(
+        totals_kernel,
+        [narrow, row],
+        [VMEM] * (2 + len(sink_rows)),
+        (keys_own, keys_last, *sink_rows),
+    )
     if lax.axis_size("dp") == 2:
         sink_row = sink_row + exchanged(sink_row, 1, "dp")
     else:
         sink_row = lax.psum(sink_row, "dp")
-    sink_row = summed_over(sink_row, reach, count)
-    keys_own, keys_share, _ = combined(keys_own, keys_share, keys_back)
-    keys_share, sink_row = kernel_call(
-        joined_kernel, [narrow, row], [VMEM] * 3, (keys_share, sink_row, dq_done)
-    )
-    keys_last = along(keys_share, -reach)
-    grad_values, done = kernel_call(end_kernel, [narrow, row], [VMEM] * 2, (values_own, values_last))
-    sink_row = sink_row + exchanged(sink_row, 1) + done
-    sink_row = summed_over(sink_row, 2, reach)
-    grad_keys, = kernel_call(total_kernel, [narrow], [VMEM] * 2, (keys_own, keys_last))
     grad_keys, grad_sinks = kernel_call(
-        out_kernel,
-        [narrow, jax.ShapeDtypeStruct(sinks.shape, F32)],
-        [VMEM] * 3,
-        (grad_keys, sink_row, done),
+        out_kernel, [narrow, jax.ShapeDtypeStruct(sinks.shape, F32)], [VMEM] * 2, (grad_keys, sink_row)
     )
     return grad_queries[None], grad_keys[None], grad_values[None], grad_sinks
 

time: 54.4 us -> 46.6 us (0.86)
  starting transfers between devices: 29.7 us -> 23.6 us
  Pallas kernels: 9.48 us -> 8.36 us
    ppermute x2 -> x0, starting transfers between devices: 8.55 us -> none  [along(): lax.ppermute(x, 'ctx', [(i, i + distance) for i in range(first, last)])]
    ppermute x17 -> x13, waiting for transfers between devices: 11.9 us -> 4.82 us  [exchanged(): lax.ppermute(x, axis, [(i, i ^ step) for i in range(lax.axis_size(axis))])]
    ppermute x2 -> x6, waiting for transfers between devices: 0.01 us -> 6.61 us  [along(): lax.ppermute(x, 'ctx', [(i, (i + distance) % count) for i in range(count)])]
    ppermute x2 -> x6, starting transfers between devices: 4.35 us -> 9.35 us  [along(): lax.ppermute(x, 'ctx', [(i, (i + distance) % count) for i in range(count)])]
    ppermute x17 -> x13, starting transfers between devices: 16.8 us -> 14.3 us  [exchanged(): lax.ppermute(x, axis, [(i, i ^ step) for i in range(lax.axis_size(axis))])]
    pallas_call x11 -> x9, Pallas kernels: 9.48 us -> 8.36 us  [kernel_call(): pl.pallas_call(body, out_shape=out_shape, in_specs=in_specs, out_specs=[V...]
  transfers between devices with their start and end apart: 21 -> 19, of which waited for: 9 -> 6; matrix products, arithmetic and copies ran while one was open for 4% -> 5% of each run, Pallas kernels for 16% -> 16%
where the time goes in v4:
time: 46.6 us; the launch traced here: 46.5 us
  starting transfers between devices  23.6 us (51%)
  waiting for transfers between devices  11.4 us (24%)
  Pallas kernels  8.36 us (18%)
  other arithmetic  2.27 us (5%)
  between operations  0.75 us (2%)
    ppermute x13, starting transfers between devices, exchanged(): lax.ppermute(x, axis, [(i, i ^ step) for i in range(lax.axis_size(axis))])  14.3 us
    ppermute x6, starting transfers between devices, along(): lax.ppermute(x, 'ctx', [(i, (i + distance) % count) for i in range(count)])  9.35 us
    pallas_call x9, Pallas kernels, kernel_call(): pl.pallas_call(body, out_shape=out_shape, in_specs=in_specs, out_specs=[V...  8.36 us
    ppermute x6, waiting for transfers between devices, along(): lax.ppermute(x, 'ctx', [(i, (i + distance) % count) for i in range(count)])  6.61 us
    ppermute x13, waiting for transfers between devices, exchanged(): lax.ppermute(x, axis, [(i, i ^ step) for i in range(lax.axis_size(axis))])  4.82 us
    concatenate x1, other arithmetic, local(): pair = jnp.concatenate([queries, grad_out], axis=1)  1.29 us
    concatenate x1, other arithmetic, local(): own = jnp.concatenate([keys, values], axis=1)  0.99 us
  transfers between devices with their start and end apart: 19, of which 6 were waited for; matrix products, arithmetic and copies ran while one was open for 5% of the time, Pallas kernels for 16%

profile of v4, /device:TPU:0, one launch (start us, length us, event | category | flops | bytes accessed | tf_op | source)
XLA Modules:
  0.0 46.5 jit_solution(9747603593504406006)
XLA Ops:
  0.7 3.1 %collective-permute-start.1 = (bf16[128,512]{1,0:T(8,128)(2,1)}, bf16[128,512]{1,0:T(8,128)(2,1)S(1)}, u32[]{:S(2)}, u32[]{:S(2)}) collective-permute-start(bf16[128,512]{1,0:T(8,128)(2,1)} %bitcast.10), channel_id=1, source_target_pairs={{0,8},{2,10},{4,12},{6,14},{8,16},{10,18},{12,20},{14,22},{16,24},... | collective-permute-start | bytes 393224 | tf_op jit(solution)/shard_map/ppermute | solution.py:289
  3.7 1.6 %collective-permute-start = (bf16[128,512]{1,0:T(8,128)(2,1)}, bf16[128,512]{1,0:T(8,128)(2,1)S(1)}, u32[]{:S(2)}, u32[]{:S(2)}) collective-permute-start(bf16[128,512]{1,0:T(8,128)(2,1)} %bitcast.12), channel_id=1, source_target_pairs={{0,8},{2,10},{4,12},{6,14},{8,16},{10,18},{12,20},{14,22},{16,24},... | collective-permute-start | bytes 393224 | tf_op jit(solution)/shard_map/ppermute | solution.py:289
  5.3 1.0 %pad_maximum_fusion.1.own_ref.refs_0_ = bf16[128,1024]{1,0:T(8,128)(2,1)S(1)} fusion(bf16[128,512]{1,0:T(8,128)(2,1)} %bitcast.13, bf16[128,512]{1,0:T(8,128)(2,1)} %bitcast.11), kind=kLoop, calls=%fused_computation.1 | loop fusion | flops 524288 | bytes 524288 | tf_op jit(solution)/shard_map/concatenate | solution.py:296
  6.3 4.0 %collective-permute-done.1.before_ref.refs_4_ = bf16[128,512]{1,0:T(8,128)(2,1)S(1)} collective-permute-done((bf16[128,512]{1,0:T(8,128)(2,1)}, bf16[128,512]{1,0:T(8,128)(2,1)S(1)}, u32[]{:S(2)}, u32[]{:S(2)}) %collective-permute-start.1) | collective-permute-done | bytes 131104 | tf_op jit(solution)/shard_map/ppermute | solution.py:289
  10.3 1.8 %collective-permute-start.2 = (bf16[128,512]{1,0:T(8,128)(2,1)S(1)}, bf16[128,512]{1,0:T(8,128)(2,1)S(1)}, u32[]{:S(2)}, u32[]{:S(2)}) collective-permute-start(bf16[128,512]{1,0:T(8,128)(2,1)S(1)} %get-tuple-element.40), channel_id=1, source_target_pairs={{0,2},{2,0},{4,6},{6,4},{8,10},{10,8},{12,14},{14,12},{16,18},{18,... | collective-permute-start | bytes 393224 | tf_op jit(solution)/shard_map/ppermute | solution.py:292
  12.1 1.5 %collective-permute-start.3 = (bf16[128,512]{1,0:T(8,128)(2,1)S(1)}, bf16[128,512]{1,0:T(8,128)(2,1)S(1)}, u32[]{:S(2)}, u32[]{:S(2)}) collective-permute-start(bf16[128,512]{1,0:T(8,128)(2,1)S(1)} %get-tuple-element.41), channel_id=1, source_target_pairs={{0,4},{2,6},{4,0},{6,2},{8,12},{10,14},{12,8},{14,10},{16,20},{18,... | collective-permute-start | bytes 393224 | tf_op jit(solution)/shard_map/ppermute | solution.py:292
  13.7 0.2 collective-permute-start.4
  13.9 1.3 %pad_maximum_fusion.pair_ref = bf16[128,4096]{1,0:T(8,128)(2,1)S(1)} fusion(bf16[128,2048]{1,0:T(8,128)(2,1)} %bitcast.8, bf16[128,2048]{1,0:T(8,128)(2,1)} %bitcast.9), kind=kLoop, calls=%fused_computation | loop fusion | flops 2097152 | bytes 2097152 | tf_op jit(solution)/shard_map/concatenate | solution.py:297
  15.2 0.6 %shard_map.93 = (f32[8,512]{1,0:T(8,128)S(1)}, f32[8,512]{1,0:T(8,128)S(1)}, bf16[128,512]{1,0:T(8,128)(2,1)S(1)}, bf16[128,512]{1,0:T(8,128)(2,1)S(1)}, bf16[128,512]{1,0:T(8,128)(2,1)S(1)}) custom-call(s32[1]{0:T(128)} %bitcast.place_ref, s32[1,16]{1,0:T(1,128)S(1)} %copy-done, f32[16]{0:T(128)S(1)} %copy-done.1, ...), custom_call_target="tpu_custom_call" | custom-call | tf_op jit(solution)/shard_map/pallas_call | solution.py:33
  15.8 1.8 %collective-permute-start.5 = (bf16[128,512]{1,0:T(8,128)(2,1)S(1)}, bf16[128,512]{1,0:T(8,128)(2,1)S(1)}, u32[]{:S(2)}, u32[]{:S(2)}) collective-permute-start(bf16[128,512]{1,0:T(8,128)(2,1)S(1)} %get-tuple-element.45), channel_id=1, source_target_pairs={{0,2},{2,0},{4,6},{6,4},{8,10},{10,8},{12,14},{14,12},{16,18},{18,... | collective-permute-start | bytes 393224 | tf_op jit(solution)/shard_map/ppermute | solution.py:292
  17.7 1.5 %collective-permute-start.6 = (bf16[128,512]{1,0:T(8,128)(2,1)S(1)}, bf16[128,512]{1,0:T(8,128)(2,1)S(1)}, u32[]{:S(2)}, u32[]{:S(2)}) collective-permute-start(bf16[128,512]{1,0:T(8,128)(2,1)S(1)} %get-tuple-element.46), channel_id=1, source_target_pairs={{0,4},{2,6},{4,0},{6,2},{8,12},{10,14},{12,8},{14,10},{16,20},{18,... | collective-permute-start | bytes 393224 | tf_op jit(solution)/shard_map/ppermute | solution.py:292
  19.2 0.2 collective-permute-start.7
  19.4 1.7 %collective-permute-done.4.refs_3_ = bf16[128,512]{1,0:T(8,128)(2,1)S(1)} collective-permute-done((bf16[128,512]{1,0:T(8,128)(2,1)S(1)}, bf16[128,512]{1,0:T(8,128)(2,1)S(1)}, u32[]{:S(2)}, u32[]{:S(2)}) %collective-permute-start.4) | collective-permute-done | bytes 131104 | tf_op jit(solution)/shard_map/ppermute | solution.py:292
  21.1 2.7 %shard_map.95 = (bf16[2048,512]{1,0:T(8,128)(2,1)S(1)}, f32[8,512]{1,0:T(8,128)S(1)}, f32[512,128]{1,0:T(8,128)S(1)}, f32[512,128]{1,0:T(8,128)S(1)}, bf16[512,1...) custom-call(f32[8,512]{1,0:T(8,128)S(1)} %get-tuple-element.38.caps_ref, ...), custom_call_target="tpu_custom_call" | custom-call | tf_op jit(solution)/shard_map/pallas_call | solution.py:33
  23.8 0.5 collective-permute-start.8
  24.2 1.2 %collective-permute-start.9 = (bf16[512,128]{1,0:T(8,128)(2,1)S(1)}, bf16[512,128]{1,0:T(8,128)(2,1)S(1)}, u32[]{:S(2)}, u32[]{:S(2)}) collective-permute-start(bf16[512,128]{1,0:T(8,128)(2,1)S(1)} %get-tuple-element.52), channel_id=1, source_target_pairs={{0,4},{2,6},{4,0},{6,2},{8,12},{10,14},{12,8},{14,10},{16,20},{18,... | collective-permute-start | bytes 393224 | tf_op jit(solution)/shard_map/ppermute | solution.py:292
  25.4 1.9 %collective-permute-start.10 = (bf16[512,128]{1,0:T(8,128)(2,1)S(1)}, bf16[512,128]{1,0:T(8,128)(2,1)S(1)}, u32[]{:S(2)}, u32[]{:S(2)}) collective-permute-start(bf16[512,128]{1,0:T(8,128)(2,1)S(1)} %get-tuple-element.53), channel_id=1, source_target_pairs={{0,6},{2,4},{4,2},{6,0},{8,14},{10,12},{12,10},{14,8},{16,22},{18,... | collective-permute-start | bytes 393224 | tf_op jit(solution)/shard_map/ppermute | solution.py:292
  27.3 2.2 %shard_map.96 = (bf16[2560,512]{1,0:T(8,128)(2,1)S(1)}, f32[1,128]{1,0:T(1,128)S(1)}, f32[512,128]{1,0:T(8,128)S(1)}, f32[512,128]{1,0:T(8,128)S(1)}, bf16[528,1...) custom-call(bf16[2048,512]{1,0:T(8,128)(2,1)S(1)} %get-tuple-element.43.probs_ref, ...), custom_call_target="tpu_custom_call" | custom-call | tf_op jit(solution)/shard_map/pallas_call | solution.py:33
  29.6 0.5 %collective-permute-start.12 = (bf16[528,128]{1,0:T(8,128)(2,1)S(1)}, bf16[528,128]{1,0:T(8,128)(2,1)S(1)}, u32[]{:S(2)}, u32[]{:S(2)}) collective-permute-start(bf16[528,128]{1,0:T(8,128)(2,1)S(1)} %get-tuple-element.60), channel_id=1, source_target_pairs={{0,2},{2,0},{4,6},{6,4},{8,10},{10,8},{12,14},{14,12},{16,18},{18,... | collective-permute-start | bytes 405512 | tf_op jit(solution)/shard_map/ppermute | solution.py:292
  30.1 1.2 %collective-permute-start.13 = (bf16[528,128]{1,0:T(8,128)(2,1)S(1)}, bf16[528,128]{1,0:T(8,128)(2,1)S(1)}, u32[]{:S(2)}, u32[]{:S(2)}) collective-permute-start(bf16[528,128]{1,0:T(8,128)(2,1)S(1)} %get-tuple-element.61), channel_id=1, source_target_pairs={{0,4},{2,6},{4,0},{6,2},{8,12},{10,14},{12,8},{14,10},{16,20},{18,... | collective-permute-start | bytes 405512 | tf_op jit(solution)/shard_map/ppermute | solution.py:292
  31.3 1.9 %collective-permute-start.14 = (bf16[528,128]{1,0:T(8,128)(2,1)S(1)}, bf16[528,128]{1,0:T(8,128)(2,1)S(1)}, u32[]{:S(2)}, u32[]{:S(2)}) collective-permute-start(bf16[528,128]{1,0:T(8,128)(2,1)S(1)} %get-tuple-element.62), channel_id=1, source_target_pairs={{0,6},{2,4},{4,2},{6,0},{8,14},{10,12},{12,10},{14,8},{16,22},{18,... | collective-permute-start | bytes 405512 | tf_op jit(solution)/shard_map/ppermute | solution.py:292
  33.2 0.2 shard_map.97
  33.4 1.8 %collective-permute-start.11 = (bf16[512,128]{1,0:T(8,128)(2,1)S(1)}, bf16[512,128]{1,0:T(8,128)(2,1)S(1)}, u32[]{:S(2)}, u32[]{:S(2)}) collective-permute-start(bf16[512,128]{1,0:T(8,128)(2,1)S(1)} %get-tuple-element.55), channel_id=1, source_target_pairs={{0,24},{2,26},{4,28},{6,30},{8,0},{10,2},{12,4},{14,6},{16,8},{18,... | collective-permute-start | bytes 393224 | tf_op jit(solution)/shard_map/ppermute | solution.py:289
  35.2 2.0 %collective-permute-done.14.refs_2_ = bf16[528,128]{1,0:T(8,128)(2,1)S(1)} collective-permute-done((bf16[528,128]{1,0:T(8,128)(2,1)S(1)}, bf16[528,128]{1,0:T(8,128)(2,1)S(1)}, u32[]{:S(2)}, u32[]{:S(2)}) %collective-permute-start.14) | collective-permute-done | bytes 135200 | tf_op jit(solution)/shard_map/ppermute | solution.py:292
  37.2 0.2 shard_map.99
  37.3 1.9 %collective-permute-start.15 = (bf16[528,128]{1,0:T(8,128)(2,1)S(1)}, bf16[528,128]{1,0:T(8,128)(2,1)S(1)}, u32[]{:S(2)}, u32[]{:S(2)}) collective-permute-start(bf16[528,128]{1,0:T(8,128)(2,1)S(1)} %get-tuple-element.64), channel_id=1, source_target_pairs={{0,24},{2,26},{4,28},{6,30},{8,0},{10,2},{12,4},{14,6},{16,8},{18,... | collective-permute-start | bytes 405512 | tf_op jit(solution)/shard_map/ppermute | solution.py:289
  39.2 0.2 collective-permute-start.17
  39.4 0.8 %collective-permute-start.16 = (f32[1,128]{1,0:T(1,128)S(1)}, f32[1,128]{1,0:T(1,128)S(1)}, u32[]{:S(2)}, u32[]{:S(2)}) collective-permute-start(f32[1,128]{1,0:T(1,128)S(1)} %get-tuple-element.65.sink_ref), channel_id=1, source_target_pairs={{0,16},{2,18},{4,20},{6,22},{8,24},{10,26},{12,28},{14,30},{16,0},... | collective-permute-start | bytes 1544 | tf_op jit(solution)/shard_map/ppermute | solution.py:289
  40.2 1.7 %shard_map.98 = (bf16[128,512]{1,0:T(8,128)(2,1)}, bf16[128,2048]{1,0:T(8,128)(2,1)}, f32[1,128]{1,0:T(1,128)S(1)}) custom-call(bf16[2560,512]{1,0:T(8,128)(2,1)S(1)} %get-tuple-element.48.gscores_ref, f32[512,128]{1,0:T(8,128)S(1)} %get-tuple-element.54.own_ref, bf16[512,128]{1,0:T(8,128)(2,1)S(1)} %collective-permute-done.11.last_ref, ...), custom_call_target="tpu_custom_call" | custom-call | flops 335544320 | tf_op jit(solution)/shard_map/pallas_call | solution.py:33
  41.9 2.6 %collective-permute-done.17.refs_1_ = f32[1,128]{1,0:T(1,128)S(1)} collective-permute-done((f32[1,128]{1,0:T(1,128)S(1)}, f32[1,128]{1,0:T(1,128)S(1)}, u32[]{:S(2)}, u32[]{:S(2)}) %collective-permute-start.17) | collective-permute-done | bytes 544 | tf_op jit(solution)/shard_map/ppermute | solution.py:289
  44.7 1.1 %collective-permute-done.18 = f32[1,128]{1,0:T(1,128)S(1)} collective-permute-done((f32[1,128]{1,0:T(1,128)S(1)}, f32[1,128]{1,0:T(1,128)S(1)}, u32[]{:S(2)}, u32[]{:S(2)}) %collective-permute-start.18) | collective-permute-done | bytes 544 | tf_op jit(solution)/shard_map/ppermute | solution.py:292
  45.8 0.7 %shard_map.101 = (bf16[128,512]{1,0:T(8,128)(2,1)}, f32[16]{0:T(128)}) custom-call(bf16[128,512]{1,0:T(8,128)(2,1)S(1)} %get-tuple-element.67.keys_ref, f32[1,128]{1,0:T(1,128)S(1)} %add.3.sink_ref), custom_call_target="tpu_custom_call" | custom-call | tf_op jit(solution)/shard_map/pallas_call | solution.py:33
  (22 shorter events, 0.3 us)
Async XLA Ops:
  0.6 14.6 %copy-start = (s32[1,16]{1,0:T(1,128)S(1)}, s32[1,16]{1,0:T(1,128)}, u32[]{:S(2)}) copy-start(s32[1,16]{1,0:T(1,128)} %docs_ref.1) | copy-start | bytes 196
  0.6 14.6 %copy-start.1 = (f32[16]{0:T(128)S(1)}, f32[16]{0:T(128)}, u32[]{:S(2)}) copy-start(f32[16]{0:T(128)} %sinks_ref.1) | copy-start | bytes 196
  0.7 9.6 %collective-permute-start.1 = (bf16[128,512]{1,0:T(8,128)(2,1)}, bf16[128,512]{1,0:T(8,128)(2,1)S(1)}, u32[]{:S(2)}, u32[]{:S(2)}) collective-permute-start(bf16[128,512]{1,0:T(8,128)(2,1)} %bitcast.10), channel_id=1, source_target_pairs={{0,8},{2,10},{4,12},{6,14},{8,16},{10,18},{12,20},{14,22},{16,24},... | collective-permute-start | bytes 393224 | tf_op jit(solution)/shard_map/ppermute | solution.py:289
  3.7 11.5 %collective-permute-start = (bf16[128,512]{1,0:T(8,128)(2,1)}, bf16[128,512]{1,0:T(8,128)(2,1)S(1)}, u32[]{:S(2)}, u32[]{:S(2)}) collective-permute-start(bf16[128,512]{1,0:T(8,128)(2,1)} %bitcast.12), channel_id=1, source_target_pairs={{0,8},{2,10},{4,12},{6,14},{8,16},{10,18},{12,20},{14,22},{16,24},... | collective-permute-start | bytes 393224 | tf_op jit(solution)/shard_map/ppermute | solution.py:289
  10.3 8.8 %collective-permute-start.2 = (bf16[128,512]{1,0:T(8,128)(2,1)S(1)}, bf16[128,512]{1,0:T(8,128)(2,1)S(1)}, u32[]{:S(2)}, u32[]{:S(2)}) collective-permute-start(bf16[128,512]{1,0:T(8,128)(2,1)S(1)} %get-tuple-element.40), channel_id=1, source_target_pairs={{0,2},{2,0},{4,6},{6,4},{8,10},{10,8},{12,14},{14,12},{16,18},{18,... | collective-permute-start | bytes 393224 | tf_op jit(solution)/shard_map/ppermute | solution.py:292
  12.1 7.3 %collective-permute-start.3 = (bf16[128,512]{1,0:T(8,128)(2,1)S(1)}, bf16[128,512]{1,0:T(8,128)(2,1)S(1)}, u32[]{:S(2)}, u32[]{:S(2)}) collective-permute-start(bf16[128,512]{1,0:T(8,128)(2,1)S(1)} %get-tuple-element.41), channel_id=1, source_target_pairs={{0,4},{2,6},{4,0},{6,2},{8,12},{10,14},{12,8},{14,10},{16,20},{18,... | collective-permute-start | bytes 393224 | tf_op jit(solution)/shard_map/ppermute | solution.py:292
  13.7 7.4 %collective-permute-start.4 = (bf16[128,512]{1,0:T(8,128)(2,1)S(1)}, bf16[128,512]{1,0:T(8,128)(2,1)S(1)}, u32[]{:S(2)}, u32[]{:S(2)}) collective-permute-start(bf16[128,512]{1,0:T(8,128)(2,1)S(1)} %get-tuple-element.42), channel_id=1, source_target_pairs={{0,6},{2,4},{4,2},{6,0},{8,14},{10,12},{12,10},{14,8},{16,22},{18,... | collective-permute-start | bytes 393224 | tf_op jit(solution)/shard_map/ppermute | solution.py:292
  15.8 9.6 %collective-permute-start.5 = (bf16[128,512]{1,0:T(8,128)(2,1)S(1)}, bf16[128,512]{1,0:T(8,128)(2,1)S(1)}, u32[]{:S(2)}, u32[]{:S(2)}) collective-permute-start(bf16[128,512]{1,0:T(8,128)(2,1)S(1)} %get-tuple-element.45), channel_id=1, source_target_pairs={{0,2},{2,0},{4,6},{6,4},{8,10},{10,8},{12,14},{14,12},{16,18},{18,... | collective-permute-start | bytes 393224 | tf_op jit(solution)/shard_map/ppermute | solution.py:292
  17.7 9.7 %collective-permute-start.6 = (bf16[128,512]{1,0:T(8,128)(2,1)S(1)}, bf16[128,512]{1,0:T(8,128)(2,1)S(1)}, u32[]{:S(2)}, u32[]{:S(2)}) collective-permute-start(bf16[128,512]{1,0:T(8,128)(2,1)S(1)} %get-tuple-element.46), channel_id=1, source_target_pairs={{0,4},{2,6},{4,0},{6,2},{8,12},{10,14},{12,8},{14,10},{16,20},{18,... | collective-permute-start | bytes 393224 | tf_op jit(solution)/shard_map/ppermute | solution.py:292
  19.2 8.2 %collective-permute-start.7 = (bf16[128,512]{1,0:T(8,128)(2,1)S(1)}, bf16[128,512]{1,0:T(8,128)(2,1)S(1)}, u32[]{:S(2)}, u32[]{:S(2)}) collective-permute-start(bf16[128,512]{1,0:T(8,128)(2,1)S(1)} %get-tuple-element.47), channel_id=1, source_target_pairs={{0,6},{2,4},{4,2},{6,0},{8,14},{10,12},{12,10},{14,8},{16,22},{18,... | collective-permute-start | bytes 393224 | tf_op jit(solution)/shard_map/ppermute | solution.py:292
  23.8 7.5 %collective-permute-start.8 = (bf16[512,128]{1,0:T(8,128)(2,1)S(1)}, bf16[512,128]{1,0:T(8,128)(2,1)S(1)}, u32[]{:S(2)}, u32[]{:S(2)}) collective-permute-start(bf16[512,128]{1,0:T(8,128)(2,1)S(1)} %get-tuple-element.51), channel_id=1, source_target_pairs={{0,2},{2,0},{4,6},{6,4},{8,10},{10,8},{12,14},{14,12},{16,18},{18,... | collective-permute-start | bytes 393224 | tf_op jit(solution)/shard_map/ppermute | solution.py:292
  24.2 9.0 %collective-permute-start.9 = (bf16[512,128]{1,0:T(8,128)(2,1)S(1)}, bf16[512,128]{1,0:T(8,128)(2,1)S(1)}, u32[]{:S(2)}, u32[]{:S(2)}) collective-permute-start(bf16[512,128]{1,0:T(8,128)(2,1)S(1)} %get-tuple-element.52), channel_id=1, source_target_pairs={{0,4},{2,6},{4,0},{6,2},{8,12},{10,14},{12,8},{14,10},{16,20},{18,... | collective-permute-start | bytes 393224 | tf_op jit(solution)/shard_map/ppermute | solution.py:292
  25.4 7.8 %collective-permute-start.10 = (bf16[512,128]{1,0:T(8,128)(2,1)S(1)}, bf16[512,128]{1,0:T(8,128)(2,1)S(1)}, u32[]{:S(2)}, u32[]{:S(2)}) collective-permute-start(bf16[512,128]{1,0:T(8,128)(2,1)S(1)} %get-tuple-element.53), channel_id=1, source_target_pairs={{0,6},{2,4},{4,2},{6,0},{8,14},{10,12},{12,10},{14,8},{16,22},{18,... | collective-permute-start | bytes 393224 | tf_op jit(solution)/shard_map/ppermute | solution.py:292
  29.6 5.6 %collective-permute-start.12 = (bf16[528,128]{1,0:T(8,128)(2,1)S(1)}, bf16[528,128]{1,0:T(8,128)(2,1)S(1)}, u32[]{:S(2)}, u32[]{:S(2)}) collective-permute-start(bf16[528,128]{1,0:T(8,128)(2,1)S(1)} %get-tuple-element.60), channel_id=1, source_target_pairs={{0,2},{2,0},{4,6},{6,4},{8,10},{10,8},{12,14},{14,12},{16,18},{18,... | collective-permute-start | bytes 405512 | tf_op jit(solution)/shard_map/ppermute | solution.py:292
  30.1 5.1 %collective-permute-start.13 = (bf16[528,128]{1,0:T(8,128)(2,1)S(1)}, bf16[528,128]{1,0:T(8,128)(2,1)S(1)}, u32[]{:S(2)}, u32[]{:S(2)}) collective-permute-start(bf16[528,128]{1,0:T(8,128)(2,1)S(1)} %get-tuple-element.61), channel_id=1, source_target_pairs={{0,4},{2,6},{4,0},{6,2},{8,12},{10,14},{12,8},{14,10},{16,20},{18,... | collective-permute-start | bytes 405512 | tf_op jit(solution)/shard_map/ppermute | solution.py:292
  31.3 5.9 %collective-permute-start.14 = (bf16[528,128]{1,0:T(8,128)(2,1)S(1)}, bf16[528,128]{1,0:T(8,128)(2,1)S(1)}, u32[]{:S(2)}, u32[]{:S(2)}) collective-permute-start(bf16[528,128]{1,0:T(8,128)(2,1)S(1)} %get-tuple-element.62), channel_id=1, source_target_pairs={{0,6},{2,4},{4,2},{6,0},{8,14},{10,12},{12,10},{14,8},{16,22},{18,... | collective-permute-start | bytes 405512 | tf_op jit(solution)/shard_map/ppermute | solution.py:292
  33.4 6.9 %collective-permute-start.11 = (bf16[512,128]{1,0:T(8,128)(2,1)S(1)}, bf16[512,128]{1,0:T(8,128)(2,1)S(1)}, u32[]{:S(2)}, u32[]{:S(2)}) collective-permute-start(bf16[512,128]{1,0:T(8,128)(2,1)S(1)} %get-tuple-element.55), channel_id=1, source_target_pairs={{0,24},{2,26},{4,28},{6,30},{8,0},{10,2},{12,4},{14,6},{16,8},{18,... | collective-permute-start | bytes 393224 | tf_op jit(solution)/shard_map/ppermute | solution.py:289
  37.3 7.2 %collective-permute-start.15 = (bf16[528,128]{1,0:T(8,128)(2,1)S(1)}, bf16[528,128]{1,0:T(8,128)(2,1)S(1)}, u32[]{:S(2)}, u32[]{:S(2)}) collective-permute-start(bf16[528,128]{1,0:T(8,128)(2,1)S(1)} %get-tuple-element.64), channel_id=1, source_target_pairs={{0,24},{2,26},{4,28},{6,30},{8,0},{10,2},{12,4},{14,6},{16,8},{18,... | collective-permute-start | bytes 405512 | tf_op jit(solution)/shard_map/ppermute | solution.py:289
  39.2 5.3 %collective-permute-start.17 = (f32[1,128]{1,0:T(1,128)S(1)}, f32[1,128]{1,0:T(1,128)S(1)}, u32[]{:S(2)}, u32[]{:S(2)}) collective-permute-start(f32[1,128]{1,0:T(1,128)S(1)} %get-tuple-element.65.sink_ref), channel_id=1, source_target_pairs={{0,8},{2,10},{4,12},{6,14},{8,16},{10,18},{12,20},{14,22},{16,24},... | collective-permute-start | bytes 1544 | tf_op jit(solution)/shard_map/ppermute | solution.py:289
  39.4 5.1 %collective-permute-start.16 = (f32[1,128]{1,0:T(1,128)S(1)}, f32[1,128]{1,0:T(1,128)S(1)}, u32[]{:S(2)}, u32[]{:S(2)}) collective-permute-start(f32[1,128]{1,0:T(1,128)S(1)} %get-tuple-element.65.sink_ref), channel_id=1, source_target_pairs={{0,16},{2,18},{4,20},{6,22},{8,24},{10,26},{12,28},{14,30},{16,0},... | collective-permute-start | bytes 1544 | tf_op jit(solution)/shard_map/ppermute | solution.py:289
  44.6 1.2 %collective-permute-start.18 = (f32[1,128]{1,0:T(1,128)S(1)}, f32[1,128]{1,0:T(1,128)S(1)}, u32[]{:S(2)}, u32[]{:S(2)}) collective-permute-start(f32[1,128]{1,0:T(1,128)S(1)} %get-tuple-element.68), channel_id=1, source_target_pairs={{0,1},{1,0},{2,3},{3,2},{4,5},{5,4},{6,7},{7,6},{8,9},{9,8},{10,11... | collective-permute-start | bytes 1544 | tf_op jit(solution)/shard_map/ppermute | solution.py:292

commit v5 on v4

--- a/solution.py
+++ b/solution.py
@@ -55,15 +55,14 @@
             ref[...] = before_ref[...]
 
 
-def keys_kernel(reach, place_ref, own_ref, before_ref, *out_refs):
-    choose(lax.rem(place_ref[0], reach), own_ref[:, :before_ref.shape[1]], before_ref, out_refs)
-
-
-def tables_kernel(reach, rows, group, place_ref, docs_ref, sinks_ref, own_ref, before_ref, pair_ref, *refs):
-    caps_ref, tops_ref, *out_refs = refs
+def choose_kernel(reach, first, place_ref, own_ref, before_ref, *refs):
+    width = before_ref.shape[1]
+    choose(lax.rem(place_ref[0], reach), own_ref[:, first * width:(first + 1) * width], before_ref, refs[-(reach - 1):])
+
+
+def tables_kernel(reach, rows, group, place_ref, docs_ref, sinks_ref, caps_ref, tops_ref):
     place = place_ref[0]
     slot = lax.rem(place, reach)
-    choose(slot, own_ref[:, before_ref.shape[1]:], before_ref, out_refs)
     doc = docs_ref[0, place]
     columns = caps_ref.shape[1]
     for step in range(1, reach + 1):
@@ -120,42 +119,65 @@
         ref[at, :] = block(x, i, rows).astype(BF16)
 
 
+def softmax_part(s_blocks, caps, top, to_log2):
+    sink_log = top
+    for i, s in enumerate(s_blocks):
+        high = jnp.max(s, axis=0, keepdims=True) * to_log2
+        top = jnp.maximum(top, jnp.minimum(high, caps[i]) if i else high)
+    sink_weight = jnp.exp2(sink_log - top)
+    summed = sink_weight
+    raised = []
+    for i, s in enumerate(s_blocks):
+        e = jnp.exp2(s * to_log2 - (jnp.maximum(top, -caps[i]) if i else top))
+        summed = summed + jnp.sum(e, axis=0, keepdims=True)
+        raised.append(e)
+    inverse = 1.0 / summed
+    probs = [(e * inverse).astype(BF16) for e in raised]
+    return probs, sink_weight * inverse
+
+
 def probs_kernel(kv_heads, group, reach, rows, size, caps_ref, tops_ref, pair_ref, *refs):
     blocks = refs[:reach + 1]
     probs_ref, sink_ref, own_ref, before_ref, *message_refs = refs[reach + 1:]
     to_log2 = size ** (-0.5) * LOG2E
     causal = causal_mask(rows, group)
     caps = [caps_ref[i:i + 1, :] for i in range(reach + 1)]
-    for head in range(kv_heads):
+
+    def scores_of(head):
         cut = slice(head * size, (head + 1) * size)
         q = stacked(pair_ref, head * group, group, size)
+        keys = jnp.concatenate([r[:, cut] for r in blocks], axis=0)
+        return dot_nt(keys, q)
+
+    waiting = None
+    following = scores_of(0)
+    for head in range(kv_heads):
         g = stacked(pair_ref, (kv_heads + head) * group, group, size)
-        keys = jnp.concatenate([r[:, cut] for r in blocks], axis=0)
-        scores = dot_nt(keys, q)
+        scores = following
+        if head + 1 < kv_heads:
+            following = scores_of(head + 1)
         s_blocks = [
             jnp.where(causal, block(scores, 0, rows), jnp.minimum(block(scores, reach, rows), caps[reach]))
         ] + [block(scores, i, rows) for i in range(1, reach)]
-        top = tops_ref[head:head + 1, :]
-        sink_log = top
-        for i, s in enumerate(s_blocks):
-            high = jnp.max(s, axis=0, keepdims=True) * to_log2
-            top = jnp.maximum(top, jnp.minimum(high, caps[i]) if i else high)
-        sink_weight = jnp.exp2(sink_log - top)
-        summed = sink_weight
-        raised = []
-        for i, s in enumerate(s_blocks):
-            e = jnp.exp2(s * to_log2 - (jnp.maximum(top, -caps[i]) if i else top))
-            summed = summed + jnp.sum(e, axis=0, keepdims=True)
-            raised.append(e)
-        inverse = 1.0 / summed
-        probs = [(e * inverse).astype(BF16) for e in raised]
+        parts = []
+        for chunk in range(2):
+            at = slice(chunk * group * rows // 2, (chunk + 1) * group * rows // 2)
+            parts.append(
+                softmax_part(
+                    [s[:, at] for s in s_blocks], [c[:, at] for c in caps], tops_ref[head:head + 1, at], to_log2
+                )
+            )
+        probs = [jnp.concatenate([p[0][i] for p in parts], axis=1) for i in range(reach)]
+        sinkp = jnp.concatenate([p[1] for p in parts], axis=1)
         for i, p in enumerate(probs):
             at = (head * reach + i) * rows
             probs_ref[at:at + rows, :] = p
-        sink_ref[head:head + 1, :] = sink_weight * inverse
+        sink_ref[head:head + 1, :] = sinkp
         first, last = parted(probs[0], causal)
-        dv = dot_nn(jnp.concatenate([first] + probs[1:] + [last], axis=0), g)
-        store_shares(dv, head, rows, reach, own_ref, before_ref, message_refs)
+        if waiting is not None:
+            store_shares(dot_nn(*waiting), head - 1, rows, reach, own_ref, before_ref, message_refs)
+        waiting = (jnp.concatenate([first] + probs[1:] + [last], axis=0), g)
+    store_shares(dot_nn(*waiting), kv_heads - 1, rows, reach, own_ref, before_ref, message_refs)
 
 
 def scores_kernel(kv_heads, group, reach, rows, size, probs_ref, sinkp_ref, pair_ref, *refs):
@@ -166,13 +188,21 @@
     causal = causal_mask(rows, group)
     lane = lax.broadcasted_iota(jnp.int32, (1, 128), 1)
     sink_row = jnp.zeros((1, 128), F32)
-    for head in range(kv_heads):
+
+    def gprobs_of(head):
         cut = slice(head * size, (head + 1) * size)
-        q = stacked(pair_ref, head * group, group, size)
         g = stacked(pair_ref, (kv_heads + head) * group, group, size)
         own_cut = slice((kv_heads + head) * size, (kv_heads + head + 1) * size)
         values = jnp.concatenate([blocks[0][:, own_cut]] + [r[:, cut] for r in blocks[1:]], axis=0)
-        gprobs = dot_nt(values, g)
+        return dot_nt(values, g)
+
+    waiting = None
+    following = gprobs_of(0)
+    for head in range(kv_heads):
+        q = stacked(pair_ref, head * group, group, size)
+        gprobs = following
+        if head + 1 < kv_heads:
+            following = gprobs_of(head + 1)
         t_blocks = [jnp.where(causal, block(gprobs, 0, rows), block(gprobs, reach, rows))]
         t_blocks += [block(gprobs, i, rows) for i in range(1, reach)]
         probs = [
@@ -186,12 +216,14 @@
         gscores = jnp.concatenate([first] + gscores[1:] + [last], axis=0)
         span = (reach + 1) * rows
         gscores_ref[head * span:(head + 1) * span, :] = gscores
-        dk = dot_nn(gscores, q) * scale
-        store_shares(dk, head, rows, reach, own_ref, before_ref, message_refs)
+        if waiting is not None:
+            store_shares(dot_nn(*waiting) * scale, head - 1, rows, reach, own_ref, before_ref, message_refs)
+        waiting = (gscores, q)
         sink_terms = sinkp_ref[head:head + 1, :] * delta
         for j in range(group):
             term = jnp.sum(sink_terms[:, j * rows:(j + 1) * rows], axis=1, keepdims=True)
             sink_row = jnp.where(lane == head * group + j, -term, sink_row)
+    store_shares(dot_nn(*waiting) * scale, kv_heads - 1, rows, reach, own_ref, before_ref, message_refs)
     sink_ref[...] = sink_row
     terms = split_terms(sink_row)
     for ref in message_refs:
@@ -300,16 +332,19 @@
         arrived = [exchanged(chosen[step - 1], step) for step in range(1, reach)]
         return [own, *arrived, before]
 
+    caps, tops = kernel_call(
+        functools.partial(tables_kernel, reach, rows, group), [table, table], [SMEM] * 3, (place, doc_ids, sinks)
+    )
     choices = [narrow] * (reach - 1)
     chosen = kernel_call(
-        functools.partial(keys_kernel, reach), choices, [SMEM, VMEM, VMEM], (place, own, keys_before)
+        functools.partial(choose_kernel, reach, 0),
+        choices,
+        [SMEM] + [VMEM] * 4,
+        (place, own, keys_before, pair, caps),
     )
     key_blocks = gathered(own, chosen, keys_before)
-    caps, tops, *chosen = kernel_call(
-        functools.partial(tables_kernel, reach, rows, group),
-        [table, table] + choices,
-        [SMEM] * 3 + [VMEM] * 3,
-        (place, doc_ids, sinks, own, values_before, pair),
+    chosen = kernel_call(
+        functools.partial(choose_kernel, reach, 1), choices, [SMEM] + [VMEM] * 2, (place, own, values_before)
     )
     value_blocks = gathered(own, chosen, values_before)
     probs, sink_probs, values_own, values_share, *messages = kernel_call(

time: 46.6 us -> 46.1 us (0.989)
  starting transfers between devices: 23.6 us -> 25.3 us
  other arithmetic: 2.27 us -> 1.29 us
  Pallas kernels: 8.36 us -> 7.56 us
  waiting for transfers between devices: 11.4 us -> 10.9 us
    ppermute x13, starting transfers between devices: 14.3 us -> 16.3 us  [exchanged(): lax.ppermute(x, axis, [(i, i ^ step) for i in range(lax.axis_size(axis))])]
    concatenate x1, other arithmetic: 0.99 us -> 0.02 us  [local(): own = jnp.concatenate([keys, values], axis=1)]
    ppermute x6, waiting for transfers between devices: 6.61 us -> 5.68 us  [along(): lax.ppermute(x, 'ctx', [(i, (i + distance) % count) for i in range(count)])]
    pallas_call x9 -> x10, Pallas kernels: 8.36 us -> 7.56 us  [kernel_call(): pl.pallas_call(body, out_shape=out_shape, in_specs=in_specs, out_specs=[V...]
  transfers between devices with their start and end apart: 19 -> 19, of which waited for: 6 -> 8; matrix products, arithmetic and copies ran while one was open for 5% -> 3% of each run, Pallas kernels for 16% -> 15%
where the time goes in v5:
time: 46.1 us; the launch traced here: 45.9 us
  starting transfers between devices  25.3 us (55%)
  waiting for transfers between devices  10.9 us (24%)
  Pallas kernels  7.56 us (16%)
  other arithmetic  1.29 us (3%)
  between operations  0.78 us (2%)
    ppermute x13, starting transfers between devices, exchanged(): lax.ppermute(x, axis, [(i, i ^ step) for i in range(lax.axis_size(axis))])  16.3 us
    ppermute x6, starting transfers between devices, along(): lax.ppermute(x, 'ctx', [(i, (i + distance) % count) for i in range(count)])  9.03 us
    pallas_call x10, Pallas kernels, kernel_call(): pl.pallas_call(body, out_shape=out_shape, in_specs=in_specs, out_specs=[V...  7.56 us
    ppermute x6, waiting for transfers between devices, along(): lax.ppermute(x, 'ctx', [(i, (i + distance) % count) for i in range(count)])  5.68 us
    ppermute x13, waiting for transfers between devices, exchanged(): lax.ppermute(x, axis, [(i, i ^ step) for i in range(lax.axis_size(axis))])  5.25 us
    concatenate x1, other arithmetic, local(): pair = jnp.concatenate([queries, grad_out], axis=1)  1.27 us
  transfers between devices with their start and end apart: 19, of which 8 were waited for; matrix products, arithmetic and copies ran while one was open for 3% of the time, Pallas kernels for 15%

profile of v5, /device:TPU:0, one launch (start us, length us, event | category | flops | bytes accessed | tf_op | source)
XLA Modules:
  0.0 45.9 jit_solution(10736555568366772238)
XLA Ops:
  0.7 3.1 %collective-permute-start = (bf16[128,512]{1,0:T(8,128)(2,1)}, bf16[128,512]{1,0:T(8,128)(2,1)S(1)}, u32[]{:S(2)}, u32[]{:S(2)}) collective-permute-start(bf16[128,512]{1,0:T(8,128)(2,1)} %bitcast.10), channel_id=1, source_target_pairs={{0,8},{2,10},{4,12},{6,14},{8,16},{10,18},{12,20},{14,22},{16,24},... | collective-permute-start | bytes 393224 | tf_op jit(solution)/shard_map/ppermute | solution.py:321
  3.7 1.6 %collective-permute-start.4 = (bf16[128,512]{1,0:T(8,128)(2,1)}, bf16[128,512]{1,0:T(8,128)(2,1)S(1)}, u32[]{:S(2)}, u32[]{:S(2)}) collective-permute-start(bf16[128,512]{1,0:T(8,128)(2,1)} %bitcast.12), channel_id=1, source_target_pairs={{0,8},{2,10},{4,12},{6,14},{8,16},{10,18},{12,20},{14,22},{16,24},... | collective-permute-start | bytes 393224 | tf_op jit(solution)/shard_map/ppermute | solution.py:321
  5.3 1.3 %pad_maximum_fusion.refs_0_.pair_ref = bf16[128,4096]{1,0:T(8,128)(2,1)S(1)} fusion(bf16[128,2048]{1,0:T(8,128)(2,1)} %bitcast.8, bf16[128,2048]{1,0:T(8,128)(2,1)} %bitcast.9), kind=kLoop, calls=%fused_computation | loop fusion | flops 2097152 | bytes 2097152 | tf_op jit(solution)/shard_map/concatenate | solution.py:329
  6.7 0.6 %shard_map.93 = (f32[8,512]{1,0:T(8,128)S(1)}, f32[8,512]{1,0:T(8,128)S(1)}) custom-call(s32[1]{0:T(128)} %bitcast.place_ref, s32[1,16]{1,0:T(1,128)S(1)} %copy-done, f32[16]{0:T(128)S(1)} %copy-done.1), custom_call_target="tpu_custom_call" | custom-call | tf_op jit(solution)/shard_map/pallas_call | solution.py:33
  7.3 3.1 %collective-permute-done.before_ref.refs_4_ = bf16[128,512]{1,0:T(8,128)(2,1)S(1)} collective-permute-done((bf16[128,512]{1,0:T(8,128)(2,1)}, bf16[128,512]{1,0:T(8,128)(2,1)S(1)}, u32[]{:S(2)}, u32[]{:S(2)}) %collective-permute-start) | collective-permute-done | bytes 131104 | tf_op jit(solution)/shard_map/ppermute | solution.py:321
  10.4 1.8 %collective-permute-start.1 = (bf16[128,512]{1,0:T(8,128)(2,1)S(1)}, bf16[128,512]{1,0:T(8,128)(2,1)S(1)}, u32[]{:S(2)}, u32[]{:S(2)}) collective-permute-start(bf16[128,512]{1,0:T(8,128)(2,1)S(1)} %get-tuple-element.40), channel_id=1, source_target_pairs={{0,2},{2,0},{4,6},{6,4},{8,10},{10,8},{12,14},{14,12},{16,18},{18,... | collective-permute-start | bytes 393224 | tf_op jit(solution)/shard_map/ppermute | solution.py:324
  12.2 1.5 %collective-permute-start.2 = (bf16[128,512]{1,0:T(8,128)(2,1)S(1)}, bf16[128,512]{1,0:T(8,128)(2,1)S(1)}, u32[]{:S(2)}, u32[]{:S(2)}) collective-permute-start(bf16[128,512]{1,0:T(8,128)(2,1)S(1)} %get-tuple-element.41), channel_id=1, source_target_pairs={{0,4},{2,6},{4,0},{6,2},{8,12},{10,14},{12,8},{14,10},{16,20},{18,... | collective-permute-start | bytes 393224 | tf_op jit(solution)/shard_map/ppermute | solution.py:324
  13.7 0.2 collective-permute-start.3
  14.0 1.8 %collective-permute-start.5 = (bf16[128,512]{1,0:T(8,128)(2,1)S(1)}, bf16[128,512]{1,0:T(8,128)(2,1)S(1)}, u32[]{:S(2)}, u32[]{:S(2)}) collective-permute-start(bf16[128,512]{1,0:T(8,128)(2,1)S(1)} %get-tuple-element.45), channel_id=1, source_target_pairs={{0,2},{2,0},{4,6},{6,4},{8,10},{10,8},{12,14},{14,12},{16,18},{18,... | collective-permute-start | bytes 393224 | tf_op jit(solution)/shard_map/ppermute | solution.py:324
  15.8 1.5 %collective-permute-start.6 = (bf16[128,512]{1,0:T(8,128)(2,1)S(1)}, bf16[128,512]{1,0:T(8,128)(2,1)S(1)}, u32[]{:S(2)}, u32[]{:S(2)}) collective-permute-start(bf16[128,512]{1,0:T(8,128)(2,1)S(1)} %get-tuple-element.46), channel_id=1, source_target_pairs={{0,4},{2,6},{4,0},{6,2},{8,12},{10,14},{12,8},{14,10},{16,20},{18,... | collective-permute-start | bytes 393224 | tf_op jit(solution)/shard_map/ppermute | solution.py:324
  17.3 2.3 %collective-permute-start.7 = (bf16[128,512]{1,0:T(8,128)(2,1)S(1)}, bf16[128,512]{1,0:T(8,128)(2,1)S(1)}, u32[]{:S(2)}, u32[]{:S(2)}) collective-permute-start(bf16[128,512]{1,0:T(8,128)(2,1)S(1)} %get-tuple-element.47), channel_id=1, source_target_pairs={{0,6},{2,4},{4,2},{6,0},{8,14},{10,12},{12,10},{14,8},{16,22},{18,... | collective-permute-start | bytes 393224 | tf_op jit(solution)/shard_map/ppermute | solution.py:324
  19.6 0.8 %collective-permute-done.2.refs_2_ = bf16[128,512]{1,0:T(8,128)(2,1)S(1)} collective-permute-done((bf16[128,512]{1,0:T(8,128)(2,1)S(1)}, bf16[128,512]{1,0:T(8,128)(2,1)S(1)}, u32[]{:S(2)}, u32[]{:S(2)}) %collective-permute-start.2) | collective-permute-done | bytes 131104 | tf_op jit(solution)/shard_map/ppermute | solution.py:324
  20.4 0.7 %collective-permute-done.3.refs_3_ = bf16[128,512]{1,0:T(8,128)(2,1)S(1)} collective-permute-done((bf16[128,512]{1,0:T(8,128)(2,1)S(1)}, bf16[128,512]{1,0:T(8,128)(2,1)S(1)}, u32[]{:S(2)}, u32[]{:S(2)}) %collective-permute-start.3) | collective-permute-done | bytes 131104 | tf_op jit(solution)/shard_map/ppermute | solution.py:324
  21.1 2.1 %shard_map.95 = (bf16[2048,512]{1,0:T(8,128)(2,1)S(1)}, f32[8,512]{1,0:T(8,128)S(1)}, f32[512,128]{1,0:T(8,128)S(1)}, f32[512,128]{1,0:T(8,128)S(1)}, bf16[512,1...) custom-call(f32[8,512]{1,0:T(8,128)S(1)} %get-tuple-element.38.refs_1_.caps_ref, ...), custom_call_target="tpu_custom_call" | custom-call | tf_op jit(solution)/shard_map/pallas_call | solution.py:33
  23.3 1.3 %collective-permute-start.8 = (bf16[512,128]{1,0:T(8,128)(2,1)S(1)}, bf16[512,128]{1,0:T(8,128)(2,1)S(1)}, u32[]{:S(2)}, u32[]{:S(2)}) collective-permute-start(bf16[512,128]{1,0:T(8,128)(2,1)S(1)} %get-tuple-element.51), channel_id=1, source_target_pairs={{0,2},{2,0},{4,6},{6,4},{8,10},{10,8},{12,14},{14,12},{16,18},{18,... | collective-permute-start | bytes 393224 | tf_op jit(solution)/shard_map/ppermute | solution.py:324
  24.5 0.8 %collective-permute-start.9 = (bf16[512,128]{1,0:T(8,128)(2,1)S(1)}, bf16[512,128]{1,0:T(8,128)(2,1)S(1)}, u32[]{:S(2)}, u32[]{:S(2)}) collective-permute-start(bf16[512,128]{1,0:T(8,128)(2,1)S(1)} %get-tuple-element.52), channel_id=1, source_target_pairs={{0,4},{2,6},{4,0},{6,2},{8,12},{10,14},{12,8},{14,10},{16,20},{18,... | collective-permute-start | bytes 393224 | tf_op jit(solution)/shard_map/ppermute | solution.py:324
  25.3 1.5 %collective-permute-start.10 = (bf16[512,128]{1,0:T(8,128)(2,1)S(1)}, bf16[512,128]{1,0:T(8,128)(2,1)S(1)}, u32[]{:S(2)}, u32[]{:S(2)}) collective-permute-start(bf16[512,128]{1,0:T(8,128)(2,1)S(1)} %get-tuple-element.53), channel_id=1, source_target_pairs={{0,6},{2,4},{4,2},{6,0},{8,14},{10,12},{12,10},{14,8},{16,22},{18,... | collective-permute-start | bytes 393224 | tf_op jit(solution)/shard_map/ppermute | solution.py:324
  26.8 2.0 %shard_map.97 = (bf16[2560,512]{1,0:T(8,128)(2,1)S(1)}, f32[1,128]{1,0:T(1,128)S(1)}, f32[512,128]{1,0:T(8,128)S(1)}, f32[512,128]{1,0:T(8,128)S(1)}, bf16[528,1...) custom-call(bf16[2048,512]{1,0:T(8,128)(2,1)S(1)} %get-tuple-element.43.probs_ref, ...), custom_call_target="tpu_custom_call" | custom-call | tf_op jit(solution)/shard_map/pallas_call | solution.py:33
  28.8 1.3 %collective-permute-start.12 = (bf16[528,128]{1,0:T(8,128)(2,1)S(1)}, bf16[528,128]{1,0:T(8,128)(2,1)S(1)}, u32[]{:S(2)}, u32[]{:S(2)}) collective-permute-start(bf16[528,128]{1,0:T(8,128)(2,1)S(1)} %get-tuple-element.60), channel_id=1, source_target_pairs={{0,2},{2,0},{4,6},{6,4},{8,10},{10,8},{12,14},{14,12},{16,18},{18,... | collective-permute-start | bytes 405512 | tf_op jit(solution)/shard_map/ppermute | solution.py:324
  30.1 0.8 %collective-permute-start.13 = (bf16[528,128]{1,0:T(8,128)(2,1)S(1)}, bf16[528,128]{1,0:T(8,128)(2,1)S(1)}, u32[]{:S(2)}, u32[]{:S(2)}) collective-permute-start(bf16[528,128]{1,0:T(8,128)(2,1)S(1)} %get-tuple-element.61), channel_id=1, source_target_pairs={{0,4},{2,6},{4,0},{6,2},{8,12},{10,14},{12,8},{14,10},{16,20},{18,... | collective-permute-start | bytes 405512 | tf_op jit(solution)/shard_map/ppermute | solution.py:324
  30.9 1.5 %collective-permute-start.14 = (bf16[528,128]{1,0:T(8,128)(2,1)S(1)}, bf16[528,128]{1,0:T(8,128)(2,1)S(1)}, u32[]{:S(2)}, u32[]{:S(2)}) collective-permute-start(bf16[528,128]{1,0:T(8,128)(2,1)S(1)} %get-tuple-element.62), channel_id=1, source_target_pairs={{0,6},{2,4},{4,2},{6,0},{8,14},{10,12},{12,10},{14,8},{16,22},{18,... | collective-permute-start | bytes 405512 | tf_op jit(solution)/shard_map/ppermute | solution.py:324
  32.4 0.6 %collective-permute-done.10.refs_2_ = bf16[512,128]{1,0:T(8,128)(2,1)S(1)} collective-permute-done((bf16[512,128]{1,0:T(8,128)(2,1)S(1)}, bf16[512,128]{1,0:T(8,128)(2,1)S(1)}, u32[]{:S(2)}, u32[]{:S(2)}) %collective-permute-start.10) | collective-permute-done | bytes 131104 | tf_op jit(solution)/shard_map/ppermute | solution.py:324
  33.1 1.7 %collective-permute-start.11 = (bf16[512,128]{1,0:T(8,128)(2,1)S(1)}, bf16[512,128]{1,0:T(8,128)(2,1)S(1)}, u32[]{:S(2)}, u32[]{:S(2)}) collective-permute-start(bf16[512,128]{1,0:T(8,128)(2,1)S(1)} %get-tuple-element.55), channel_id=1, source_target_pairs={{0,24},{2,26},{4,28},{6,30},{8,0},{10,2},{12,4},{14,6},{16,8},{18,... | collective-permute-start | bytes 393224 | tf_op jit(solution)/shard_map/ppermute | solution.py:321
  34.8 0.3 collective-permute-done.13.refs_1_
  35.1 1.7 %collective-permute-done.14.refs_2_ = bf16[528,128]{1,0:T(8,128)(2,1)S(1)} collective-permute-done((bf16[528,128]{1,0:T(8,128)(2,1)S(1)}, bf16[528,128]{1,0:T(8,128)(2,1)S(1)}, u32[]{:S(2)}, u32[]{:S(2)}) %collective-permute-start.14) | collective-permute-done | bytes 135200 | tf_op jit(solution)/shard_map/ppermute | solution.py:324
  37.0 1.7 %collective-permute-start.15 = (bf16[528,128]{1,0:T(8,128)(2,1)S(1)}, bf16[528,128]{1,0:T(8,128)(2,1)S(1)}, u32[]{:S(2)}, u32[]{:S(2)}) collective-permute-start(bf16[528,128]{1,0:T(8,128)(2,1)S(1)} %get-tuple-element.64), channel_id=1, source_target_pairs={{0,24},{2,26},{4,28},{6,30},{8,0},{10,2},{12,4},{14,6},{16,8},{18,... | collective-permute-start | bytes 405512 | tf_op jit(solution)/shard_map/ppermute | solution.py:321
  38.7 0.4 collective-permute-start.17
  39.1 0.6 %collective-permute-start.16 = (f32[1,128]{1,0:T(1,128)S(1)}, f32[1,128]{1,0:T(1,128)S(1)}, u32[]{:S(2)}, u32[]{:S(2)}) collective-permute-start(f32[1,128]{1,0:T(1,128)S(1)} %get-tuple-element.65.sink_ref), channel_id=1, source_target_pairs={{0,16},{2,18},{4,20},{6,22},{8,24},{10,26},{12,28},{14,30},{16,0},... | collective-permute-start | bytes 1544 | tf_op jit(solution)/shard_map/ppermute | solution.py:321
  39.7 1.7 %shard_map.99 = (bf16[128,512]{1,0:T(8,128)(2,1)}, bf16[128,2048]{1,0:T(8,128)(2,1)}, f32[1,128]{1,0:T(1,128)S(1)}) custom-call(bf16[2560,512]{1,0:T(8,128)(2,1)S(1)} %get-tuple-element.48.gscores_ref, f32[512,128]{1,0:T(8,128)S(1)} %get-tuple-element.54.own_ref, bf16[512,128]{1,0:T(8,128)(2,1)S(1)} %collective-permute-done.11.last_ref, ...), custom_call_target="tpu_custom_call" | custom-call | flops 335544320 | tf_op jit(solution)/shard_map/pallas_call | solution.py:33
  41.4 2.6 %collective-permute-done.17.refs_1_ = f32[1,128]{1,0:T(1,128)S(1)} collective-permute-done((f32[1,128]{1,0:T(1,128)S(1)}, f32[1,128]{1,0:T(1,128)S(1)}, u32[]{:S(2)}, u32[]{:S(2)}) %collective-permute-start.17) | collective-permute-done | bytes 544 | tf_op jit(solution)/shard_map/ppermute | solution.py:321
  44.1 1.1 %collective-permute-done.18 = f32[1,128]{1,0:T(1,128)S(1)} collective-permute-done((f32[1,128]{1,0:T(1,128)S(1)}, f32[1,128]{1,0:T(1,128)S(1)}, u32[]{:S(2)}, u32[]{:S(2)}) %collective-permute-start.18) | collective-permute-done | bytes 544 | tf_op jit(solution)/shard_map/ppermute | solution.py:324
  45.3 0.7 %shard_map.102 = (bf16[128,512]{1,0:T(8,128)(2,1)}, f32[16]{0:T(128)}) custom-call(bf16[128,512]{1,0:T(8,128)(2,1)S(1)} %get-tuple-element.67.keys_ref, f32[1,128]{1,0:T(1,128)S(1)} %add.3.sink_ref), custom_call_target="tpu_custom_call" | custom-call | tf_op jit(solution)/shard_map/pallas_call | solution.py:33
  (27 shorter events, 0.6 us)
Async XLA Ops:
  0.6 6.0 %copy-start.2 = (bf16[1,128,512]{2,1,0:T(8,128)(2,1)S(1)}, bf16[1,128,512]{2,1,0:T(8,128)(2,1)}, u32[]{:S(2)}) copy-start(bf16[1,128,512]{2,1,0:T(8,128)(2,1)} %param.7) | copy-start | bytes 393220
  0.6 6.0 %copy-start.3 = (bf16[1,128,512]{2,1,0:T(8,128)(2,1)S(1)}, bf16[1,128,512]{2,1,0:T(8,128)(2,1)}, u32[]{:S(2)}) copy-start(bf16[1,128,512]{2,1,0:T(8,128)(2,1)} %param.8) | copy-start | bytes 393220
  0.7 6.0 %copy-start = (s32[1,16]{1,0:T(1,128)S(1)}, s32[1,16]{1,0:T(1,128)}, u32[]{:S(2)}) copy-start(s32[1,16]{1,0:T(1,128)} %docs_ref.1) | copy-start | bytes 196
  0.7 6.0 %copy-start.1 = (f32[16]{0:T(128)S(1)}, f32[16]{0:T(128)}, u32[]{:S(2)}) copy-start(f32[16]{0:T(128)} %sinks_ref.1) | copy-start | bytes 196
  0.7 9.6 %collective-permute-start = (bf16[128,512]{1,0:T(8,128)(2,1)}, bf16[128,512]{1,0:T(8,128)(2,1)S(1)}, u32[]{:S(2)}, u32[]{:S(2)}) collective-permute-start(bf16[128,512]{1,0:T(8,128)(2,1)} %bitcast.10), channel_id=1, source_target_pairs={{0,8},{2,10},{4,12},{6,14},{8,16},{10,18},{12,20},{14,22},{16,24},... | collective-permute-start | bytes 393224 | tf_op jit(solution)/shard_map/ppermute | solution.py:321
  3.7 10.2 %collective-permute-start.4 = (bf16[128,512]{1,0:T(8,128)(2,1)}, bf16[128,512]{1,0:T(8,128)(2,1)S(1)}, u32[]{:S(2)}, u32[]{:S(2)}) collective-permute-start(bf16[128,512]{1,0:T(8,128)(2,1)} %bitcast.12), channel_id=1, source_target_pairs={{0,8},{2,10},{4,12},{6,14},{8,16},{10,18},{12,20},{14,22},{16,24},... | collective-permute-start | bytes 393224 | tf_op jit(solution)/shard_map/ppermute | solution.py:321
  10.4 6.9 %collective-permute-start.1 = (bf16[128,512]{1,0:T(8,128)(2,1)S(1)}, bf16[128,512]{1,0:T(8,128)(2,1)S(1)}, u32[]{:S(2)}, u32[]{:S(2)}) collective-permute-start(bf16[128,512]{1,0:T(8,128)(2,1)S(1)} %get-tuple-element.40), channel_id=1, source_target_pairs={{0,2},{2,0},{4,6},{6,4},{8,10},{10,8},{12,14},{14,12},{16,18},{18,... | collective-permute-start | bytes 393224 | tf_op jit(solution)/shard_map/ppermute | solution.py:324
  12.2 8.2 %collective-permute-start.2 = (bf16[128,512]{1,0:T(8,128)(2,1)S(1)}, bf16[128,512]{1,0:T(8,128)(2,1)S(1)}, u32[]{:S(2)}, u32[]{:S(2)}) collective-permute-start(bf16[128,512]{1,0:T(8,128)(2,1)S(1)} %get-tuple-element.41), channel_id=1, source_target_pairs={{0,4},{2,6},{4,0},{6,2},{8,12},{10,14},{12,8},{14,10},{16,20},{18,... | collective-permute-start | bytes 393224 | tf_op jit(solution)/shard_map/ppermute | solution.py:324
  13.7 7.4 %collective-permute-start.3 = (bf16[128,512]{1,0:T(8,128)(2,1)S(1)}, bf16[128,512]{1,0:T(8,128)(2,1)S(1)}, u32[]{:S(2)}, u32[]{:S(2)}) collective-permute-start(bf16[128,512]{1,0:T(8,128)(2,1)S(1)} %get-tuple-element.42), channel_id=1, source_target_pairs={{0,6},{2,4},{4,2},{6,0},{8,14},{10,12},{12,10},{14,8},{16,22},{18,... | collective-permute-start | bytes 393224 | tf_op jit(solution)/shard_map/ppermute | solution.py:324
  14.0 11.4 %collective-permute-start.5 = (bf16[128,512]{1,0:T(8,128)(2,1)S(1)}, bf16[128,512]{1,0:T(8,128)(2,1)S(1)}, u32[]{:S(2)}, u32[]{:S(2)}) collective-permute-start(bf16[128,512]{1,0:T(8,128)(2,1)S(1)} %get-tuple-element.45), channel_id=1, source_target_pairs={{0,2},{2,0},{4,6},{6,4},{8,10},{10,8},{12,14},{14,12},{16,18},{18,... | collective-permute-start | bytes 393224 | tf_op jit(solution)/shard_map/ppermute | solution.py:324
  15.8 11.0 %collective-permute-start.6 = (bf16[128,512]{1,0:T(8,128)(2,1)S(1)}, bf16[128,512]{1,0:T(8,128)(2,1)S(1)}, u32[]{:S(2)}, u32[]{:S(2)}) collective-permute-start(bf16[128,512]{1,0:T(8,128)(2,1)S(1)} %get-tuple-element.46), channel_id=1, source_target_pairs={{0,4},{2,6},{4,0},{6,2},{8,12},{10,14},{12,8},{14,10},{16,20},{18,... | collective-permute-start | bytes 393224 | tf_op jit(solution)/shard_map/ppermute | solution.py:324
  17.3 9.5 %collective-permute-start.7 = (bf16[128,512]{1,0:T(8,128)(2,1)S(1)}, bf16[128,512]{1,0:T(8,128)(2,1)S(1)}, u32[]{:S(2)}, u32[]{:S(2)}) collective-permute-start(bf16[128,512]{1,0:T(8,128)(2,1)S(1)} %get-tuple-element.47), channel_id=1, source_target_pairs={{0,6},{2,4},{4,2},{6,0},{8,14},{10,12},{12,10},{14,8},{16,22},{18,... | collective-permute-start | bytes 393224 | tf_op jit(solution)/shard_map/ppermute | solution.py:324
  23.3 7.6 %collective-permute-start.8 = (bf16[512,128]{1,0:T(8,128)(2,1)S(1)}, bf16[512,128]{1,0:T(8,128)(2,1)S(1)}, u32[]{:S(2)}, u32[]{:S(2)}) collective-permute-start(bf16[512,128]{1,0:T(8,128)(2,1)S(1)} %get-tuple-element.51), channel_id=1, source_target_pairs={{0,2},{2,0},{4,6},{6,4},{8,10},{10,8},{12,14},{14,12},{16,18},{18,... | collective-permute-start | bytes 393224 | tf_op jit(solution)/shard_map/ppermute | solution.py:324
  24.5 7.9 %collective-permute-start.9 = (bf16[512,128]{1,0:T(8,128)(2,1)S(1)}, bf16[512,128]{1,0:T(8,128)(2,1)S(1)}, u32[]{:S(2)}, u32[]{:S(2)}) collective-permute-start(bf16[512,128]{1,0:T(8,128)(2,1)S(1)} %get-tuple-element.52), channel_id=1, source_target_pairs={{0,4},{2,6},{4,0},{6,2},{8,12},{10,14},{12,8},{14,10},{16,20},{18,... | collective-permute-start | bytes 393224 | tf_op jit(solution)/shard_map/ppermute | solution.py:324
  25.3 7.6 %collective-permute-start.10 = (bf16[512,128]{1,0:T(8,128)(2,1)S(1)}, bf16[512,128]{1,0:T(8,128)(2,1)S(1)}, u32[]{:S(2)}, u32[]{:S(2)}) collective-permute-start(bf16[512,128]{1,0:T(8,128)(2,1)S(1)} %get-tuple-element.53), channel_id=1, source_target_pairs={{0,6},{2,4},{4,2},{6,0},{8,14},{10,12},{12,10},{14,8},{16,22},{18,... | collective-permute-start | bytes 393224 | tf_op jit(solution)/shard_map/ppermute | solution.py:324
  28.8 6.0 %collective-permute-start.12 = (bf16[528,128]{1,0:T(8,128)(2,1)S(1)}, bf16[528,128]{1,0:T(8,128)(2,1)S(1)}, u32[]{:S(2)}, u32[]{:S(2)}) collective-permute-start(bf16[528,128]{1,0:T(8,128)(2,1)S(1)} %get-tuple-element.60), channel_id=1, source_target_pairs={{0,2},{2,0},{4,6},{6,4},{8,10},{10,8},{12,14},{14,12},{16,18},{18,... | collective-permute-start | bytes 405512 | tf_op jit(solution)/shard_map/ppermute | solution.py:324
  30.1 5.0 %collective-permute-start.13 = (bf16[528,128]{1,0:T(8,128)(2,1)S(1)}, bf16[528,128]{1,0:T(8,128)(2,1)S(1)}, u32[]{:S(2)}, u32[]{:S(2)}) collective-permute-start(bf16[528,128]{1,0:T(8,128)(2,1)S(1)} %get-tuple-element.61), channel_id=1, source_target_pairs={{0,4},{2,6},{4,0},{6,2},{8,12},{10,14},{12,8},{14,10},{16,20},{18,... | collective-permute-start | bytes 405512 | tf_op jit(solution)/shard_map/ppermute | solution.py:324
  30.9 5.9 %collective-permute-start.14 = (bf16[528,128]{1,0:T(8,128)(2,1)S(1)}, bf16[528,128]{1,0:T(8,128)(2,1)S(1)}, u32[]{:S(2)}, u32[]{:S(2)}) collective-permute-start(bf16[528,128]{1,0:T(8,128)(2,1)S(1)} %get-tuple-element.62), channel_id=1, source_target_pairs={{0,6},{2,4},{4,2},{6,0},{8,14},{10,12},{12,10},{14,8},{16,22},{18,... | collective-permute-start | bytes 405512 | tf_op jit(solution)/shard_map/ppermute | solution.py:324
  33.1 6.6 %collective-permute-start.11 = (bf16[512,128]{1,0:T(8,128)(2,1)S(1)}, bf16[512,128]{1,0:T(8,128)(2,1)S(1)}, u32[]{:S(2)}, u32[]{:S(2)}) collective-permute-start(bf16[512,128]{1,0:T(8,128)(2,1)S(1)} %get-tuple-element.55), channel_id=1, source_target_pairs={{0,24},{2,26},{4,28},{6,30},{8,0},{10,2},{12,4},{14,6},{16,8},{18,... | collective-permute-start | bytes 393224 | tf_op jit(solution)/shard_map/ppermute | solution.py:321
  37.0 7.0 %collective-permute-start.15 = (bf16[528,128]{1,0:T(8,128)(2,1)S(1)}, bf16[528,128]{1,0:T(8,128)(2,1)S(1)}, u32[]{:S(2)}, u32[]{:S(2)}) collective-permute-start(bf16[528,128]{1,0:T(8,128)(2,1)S(1)} %get-tuple-element.64), channel_id=1, source_target_pairs={{0,24},{2,26},{4,28},{6,30},{8,0},{10,2},{12,4},{14,6},{16,8},{18,... | collective-permute-start | bytes 405512 | tf_op jit(solution)/shard_map/ppermute | solution.py:321
  38.7 5.3 %collective-permute-start.17 = (f32[1,128]{1,0:T(1,128)S(1)}, f32[1,128]{1,0:T(1,128)S(1)}, u32[]{:S(2)}, u32[]{:S(2)}) collective-permute-start(f32[1,128]{1,0:T(1,128)S(1)} %get-tuple-element.65.sink_ref), channel_id=1, source_target_pairs={{0,8},{2,10},{4,12},{6,14},{8,16},{10,18},{12,20},{14,22},{16,24},... | collective-permute-start | bytes 1544 | tf_op jit(solution)/shard_map/ppermute | solution.py:321
  39.1 4.9 %collective-permute-start.16 = (f32[1,128]{1,0:T(1,128)S(1)}, f32[1,128]{1,0:T(1,128)S(1)}, u32[]{:S(2)}, u32[]{:S(2)}) collective-permute-start(f32[1,128]{1,0:T(1,128)S(1)} %get-tuple-element.65.sink_ref), channel_id=1, source_target_pairs={{0,16},{2,18},{4,20},{6,22},{8,24},{10,26},{12,28},{14,30},{16,0},... | collective-permute-start | bytes 1544 | tf_op jit(solution)/shard_map/ppermute | solution.py:321
  44.1 1.2 %collective-permute-start.18 = (f32[1,128]{1,0:T(1,128)S(1)}, f32[1,128]{1,0:T(1,128)S(1)}, u32[]{:S(2)}, u32[]{:S(2)}) collective-permute-start(f32[1,128]{1,0:T(1,128)S(1)} %get-tuple-element.68), channel_id=1, source_target_pairs={{0,1},{1,0},{2,3},{3,2},{4,5},{5,4},{6,7},{7,6},{8,9},{9,8},{10,11... | collective-permute-start | bytes 1544 | tf_op jit(solution)/shard_map/ppermute | solution.py:324

commit v6 on v5

--- a/solution.py
+++ b/solution.py
@@ -60,7 +60,8 @@
     choose(lax.rem(place_ref[0], reach), own_ref[:, first * width:(first + 1) * width], before_ref, refs[-(reach - 1):])
 
 
-def tables_kernel(reach, rows, group, place_ref, docs_ref, sinks_ref, caps_ref, tops_ref):
+def tables_kernel(reach, rows, group, place_ref, docs_ref, sinks_ref, own_ref, caps_ref, tops_ref, values_ref):
+    values_ref[...] = own_ref[:, values_ref.shape[1]:]
     place = place_ref[0]
     slot = lax.rem(place, reach)
     doc = docs_ref[0, place]
@@ -324,27 +325,30 @@
         return lax.ppermute(x, axis, [(i, i ^ step) for i in range(lax.axis_size(axis))])
 
     keys_before = along(keys, reach)
-    values_before = along(values, reach)
     own = jnp.concatenate([keys, values], axis=1)
     pair = jnp.concatenate([queries, grad_out], axis=1)
+    caps, tops, passed_values = kernel_call(
+        functools.partial(tables_kernel, reach, rows, group),
+        [table, table, narrow],
+        [SMEM] * 3 + [VMEM],
+        (place, doc_ids, sinks, own),
+    )
+    values_before = along(passed_values, reach)
 
     def gathered(own, chosen, before):
         arrived = [exchanged(chosen[step - 1], step) for step in range(1, reach)]
         return [own, *arrived, before]
 
-    caps, tops = kernel_call(
-        functools.partial(tables_kernel, reach, rows, group), [table, table], [SMEM] * 3, (place, doc_ids, sinks)
-    )
     choices = [narrow] * (reach - 1)
     chosen = kernel_call(
         functools.partial(choose_kernel, reach, 0),
         choices,
-        [SMEM] + [VMEM] * 4,
-        (place, own, keys_before, pair, caps),
+        [SMEM] + [VMEM] * 3,
+        (place, own, keys_before, caps),
     )
     key_blocks = gathered(own, chosen, keys_before)
     chosen = kernel_call(
-        functools.partial(choose_kernel, reach, 1), choices, [SMEM] + [VMEM] * 2, (place, own, values_before)
+        functools.partial(choose_kernel, reach, 1), choices, [SMEM] + [VMEM] * 3, (place, own, values_before, pair)
     )
     value_blocks = gathered(own, chosen, values_before)
     probs, sink_probs, values_own, values_share, *messages = kernel_call(

time: 46.1 us -> 45.1 us (0.978)
  starting transfers between devices: 25.3 us -> 23.5 us
  waiting for transfers between devices: 10.9 us -> 9.56 us
  local copies, waits for them, and re-layouts: 0.02 us -> 1.31 us
  other arithmetic: 1.29 us -> 2.28 us
    ppermute x13, starting transfers between devices: 16.3 us -> 14.3 us  [exchanged(): lax.ppermute(x, axis, [(i, i ^ step) for i in range(lax.axis_size(axis))])]
    ppermute x6, waiting for transfers between devices: 5.68 us -> 3.83 us  [along(): lax.ppermute(x, 'ctx', [(i, (i + distance) % count) for i in range(count)])]
    unnamed x8 -> x4, local copies, waits for them, and re-layouts: 0.02 us -> 1.31 us
    concatenate x1, other arithmetic: 0.02 us -> 0.99 us  [local(): own = jnp.concatenate([keys, values], axis=1)]
    ppermute x13, waiting for transfers between devices: 5.25 us -> 5.73 us  [exchanged(): lax.ppermute(x, axis, [(i, i ^ step) for i in range(lax.axis_size(axis))])]
  transfers between devices with their start and end apart: 19 -> 19, of which waited for: 8 -> 8; matrix products, arithmetic and copies ran while one was open for 3% -> 5% of each run, Pallas kernels for 15% -> 15%
where the time goes in v6:
time: 45.1 us; the launch traced here: 45 us
  starting transfers between devices  23.5 us (52%)
  waiting for transfers between devices  9.56 us (21%)
  Pallas kernels  7.55 us (17%)
  other arithmetic  2.28 us (5%)
  local copies, waits for them, and re-layouts  1.31 us (3%)
  between operations  0.73 us (2%)
    ppermute x13, starting transfers between devices, exchanged(): lax.ppermute(x, axis, [(i, i ^ step) for i in range(lax.axis_size(axis))])  14.3 us
    ppermute x6, starting transfers between devices, along(): lax.ppermute(x, 'ctx', [(i, (i + distance) % count) for i in range(count)])  9.24 us
    pallas_call x10, Pallas kernels, kernel_call(): pl.pallas_call(body, out_shape=out_shape, in_specs=in_specs, out_specs=[V...  7.55 us
    ppermute x13, waiting for transfers between devices, exchanged(): lax.ppermute(x, axis, [(i, i ^ step) for i in range(lax.axis_size(axis))])  5.73 us
    ppermute x6, waiting for transfers between devices, along(): lax.ppermute(x, 'ctx', [(i, (i + distance) % count) for i in range(count)])  3.83 us
    unnamed x4, local copies, waits for them, and re-layouts  1.31 us
    concatenate x1, other arithmetic, local(): pair = jnp.concatenate([queries, grad_out], axis=1)  1.29 us
    concatenate x1, other arithmetic, local(): own = jnp.concatenate([keys, values], axis=1)  0.99 us
  transfers between devices with their start and end apart: 19, of which 8 were waited for; matrix products, arithmetic and copies ran while one was open for 5% of the time, Pallas kernels for 15%

profile of v6, /device:TPU:0, one launch (start us, length us, event | category | flops | bytes accessed | tf_op | source)
XLA Modules:
  0.0 45.0 jit_solution(6265904410735552151)
XLA Ops:
  0.6 3.1 %collective-permute-start = (bf16[128,512]{1,0:T(8,128)(2,1)}, bf16[128,512]{1,0:T(8,128)(2,1)S(1)}, u32[]{:S(2)}, u32[]{:S(2)}) collective-permute-start(bf16[128,512]{1,0:T(8,128)(2,1)} %bitcast.11), channel_id=1, source_target_pairs={{0,8},{2,10},{4,12},{6,14},{8,16},{10,18},{12,20},{14,22},{16,24},... | collective-permute-start | bytes 393224 | tf_op jit(solution)/shard_map/ppermute | solution.py:322
  3.7 1.0 %pad_maximum_fusion.1.own_ref.refs_0_ = bf16[128,1024]{1,0:T(8,128)(2,1)S(1)} fusion(bf16[128,512]{1,0:T(8,128)(2,1)} %bitcast.10, bf16[128,512]{1,0:T(8,128)(2,1)} %bitcast.12), kind=kLoop, calls=%fused_computation.1 | loop fusion | flops 524288 | bytes 524288 | tf_op jit(solution)/shard_map/concatenate | solution.py:328
  4.7 0.6 %copy-done = s32[1,16]{1,0:T(1,128)S(1)} copy-done((s32[1,16]{1,0:T(1,128)S(1)}, s32[1,16]{1,0:T(1,128)}, u32[]{:S(2)}) %copy-start) | copy-done | bytes 88
  5.4 0.7 %copy-done.1 = f32[16]{0:T(128)S(1)} copy-done((f32[16]{0:T(128)S(1)}, f32[16]{0:T(128)}, u32[]{:S(2)}) %copy-start.1) | copy-done | bytes 88
  6.0 0.6 %shard_map.93 = (f32[8,512]{1,0:T(8,128)S(1)}, f32[8,512]{1,0:T(8,128)S(1)}, bf16[128,512]{1,0:T(8,128)(2,1)S(1)}) custom-call(s32[1]{0:T(128)} %bitcast.place_ref, s32[1,16]{1,0:T(1,128)S(1)} %copy-done, f32[16]{0:T(128)S(1)} %copy-done.1, bf16[128,1024]{1,0:T(8,128)(2,1)S(1)} %pad_maximum_fusion.1.own_ref.refs_0_), custom_call_target="tpu_custom_call" | custom-call | tf_op jit(solution)/shard_map/pallas_call | solution.py:33
  6.6 1.6 %collective-permute-start.4 = (bf16[128,512]{1,0:T(8,128)(2,1)S(1)}, bf16[128,512]{1,0:T(8,128)(2,1)S(1)}, u32[]{:S(2)}, u32[]{:S(2)}) collective-permute-start(bf16[128,512]{1,0:T(8,128)(2,1)S(1)} %get-tuple-element.46), channel_id=1, source_target_pairs={{0,8},{2,10},{4,12},{6,14},{8,16},{10,18},{12,20},{14,22},{16,24},... | collective-permute-start | bytes 393224 | tf_op jit(solution)/shard_map/ppermute | solution.py:322
  8.2 1.2 %collective-permute-done.before_ref.refs_4_ = bf16[128,512]{1,0:T(8,128)(2,1)S(1)} collective-permute-done((bf16[128,512]{1,0:T(8,128)(2,1)}, bf16[128,512]{1,0:T(8,128)(2,1)S(1)}, u32[]{:S(2)}, u32[]{:S(2)}) %collective-permute-start) | collective-permute-done | bytes 131104 | tf_op jit(solution)/shard_map/ppermute | solution.py:322
  9.5 1.6 %collective-permute-start.1 = (bf16[128,512]{1,0:T(8,128)(2,1)S(1)}, bf16[128,512]{1,0:T(8,128)(2,1)S(1)}, u32[]{:S(2)}, u32[]{:S(2)}) collective-permute-start(bf16[128,512]{1,0:T(8,128)(2,1)S(1)} %get-tuple-element.41), channel_id=1, source_target_pairs={{0,2},{2,0},{4,6},{6,4},{8,10},{10,8},{12,14},{14,12},{16,18},{18,... | collective-permute-start | bytes 393224 | tf_op jit(solution)/shard_map/ppermute | solution.py:325
  11.0 1.5 %collective-permute-start.2 = (bf16[128,512]{1,0:T(8,128)(2,1)S(1)}, bf16[128,512]{1,0:T(8,128)(2,1)S(1)}, u32[]{:S(2)}, u32[]{:S(2)}) collective-permute-start(bf16[128,512]{1,0:T(8,128)(2,1)S(1)} %get-tuple-element.42), channel_id=1, source_target_pairs={{0,4},{2,6},{4,0},{6,2},{8,12},{10,14},{12,8},{14,10},{16,20},{18,... | collective-permute-start | bytes 393224 | tf_op jit(solution)/shard_map/ppermute | solution.py:325
  12.6 0.5 %collective-permute-start.3 = (bf16[128,512]{1,0:T(8,128)(2,1)S(1)}, bf16[128,512]{1,0:T(8,128)(2,1)S(1)}, u32[]{:S(2)}, u32[]{:S(2)}) collective-permute-start(bf16[128,512]{1,0:T(8,128)(2,1)S(1)} %get-tuple-element.43), channel_id=1, source_target_pairs={{0,6},{2,4},{4,2},{6,0},{8,14},{10,12},{12,10},{14,8},{16,22},{18,... | collective-permute-start | bytes 393224 | tf_op jit(solution)/shard_map/ppermute | solution.py:325
  13.0 1.3 %pad_maximum_fusion.pair_ref.refs_0_ = bf16[128,4096]{1,0:T(8,128)(2,1)S(1)} fusion(bf16[128,2048]{1,0:T(8,128)(2,1)} %bitcast.8, bf16[128,2048]{1,0:T(8,128)(2,1)} %bitcast.9), kind=kLoop, calls=%fused_computation | loop fusion | flops 2097152 | bytes 2097152 | tf_op jit(solution)/shard_map/concatenate | solution.py:329
  14.4 1.6 %collective-permute-start.5 = (bf16[128,512]{1,0:T(8,128)(2,1)S(1)}, bf16[128,512]{1,0:T(8,128)(2,1)S(1)}, u32[]{:S(2)}, u32[]{:S(2)}) collective-permute-start(bf16[128,512]{1,0:T(8,128)(2,1)S(1)} %get-tuple-element.47), channel_id=1, source_target_pairs={{0,2},{2,0},{4,6},{6,4},{8,10},{10,8},{12,14},{14,12},{16,18},{18,... | collective-permute-start | bytes 393224 | tf_op jit(solution)/shard_map/ppermute | solution.py:325
  16.0 1.5 %collective-permute-start.6 = (bf16[128,512]{1,0:T(8,128)(2,1)S(1)}, bf16[128,512]{1,0:T(8,128)(2,1)S(1)}, u32[]{:S(2)}, u32[]{:S(2)}) collective-permute-start(bf16[128,512]{1,0:T(8,128)(2,1)S(1)} %get-tuple-element.48), channel_id=1, source_target_pairs={{0,4},{2,6},{4,0},{6,2},{8,12},{10,14},{12,8},{14,10},{16,20},{18,... | collective-permute-start | bytes 393224 | tf_op jit(solution)/shard_map/ppermute | solution.py:325
  17.5 0.5 %collective-permute-start.7 = (bf16[128,512]{1,0:T(8,128)(2,1)S(1)}, bf16[128,512]{1,0:T(8,128)(2,1)S(1)}, u32[]{:S(2)}, u32[]{:S(2)}) collective-permute-start(bf16[128,512]{1,0:T(8,128)(2,1)S(1)} %get-tuple-element.49), channel_id=1, source_target_pairs={{0,6},{2,4},{4,2},{6,0},{8,14},{10,12},{12,10},{14,8},{16,22},{18,... | collective-permute-start | bytes 393224 | tf_op jit(solution)/shard_map/ppermute | solution.py:325
  18.4 1.5 %collective-permute-done.3.refs_3_ = bf16[128,512]{1,0:T(8,128)(2,1)S(1)} collective-permute-done((bf16[128,512]{1,0:T(8,128)(2,1)S(1)}, bf16[128,512]{1,0:T(8,128)(2,1)S(1)}, u32[]{:S(2)}, u32[]{:S(2)}) %collective-permute-start.3) | collective-permute-done | bytes 131104 | tf_op jit(solution)/shard_map/ppermute | solution.py:325
  19.9 2.1 %shard_map.95 = (bf16[2048,512]{1,0:T(8,128)(2,1)S(1)}, f32[8,512]{1,0:T(8,128)S(1)}, f32[512,128]{1,0:T(8,128)S(1)}, f32[512,128]{1,0:T(8,128)S(1)}, bf16[512,1...) custom-call(f32[8,512]{1,0:T(8,128)S(1)} %get-tuple-element.39.refs_0_.caps_ref, ...), custom_call_target="tpu_custom_call" | custom-call | tf_op jit(solution)/shard_map/pallas_call | solution.py:33
  22.1 1.0 %collective-permute-start.8 = (bf16[512,128]{1,0:T(8,128)(2,1)S(1)}, bf16[512,128]{1,0:T(8,128)(2,1)S(1)}, u32[]{:S(2)}, u32[]{:S(2)}) collective-permute-start(bf16[512,128]{1,0:T(8,128)(2,1)S(1)} %get-tuple-element.53), channel_id=1, source_target_pairs={{0,2},{2,0},{4,6},{6,4},{8,10},{10,8},{12,14},{14,12},{16,18},{18,... | collective-permute-start | bytes 393224 | tf_op jit(solution)/shard_map/ppermute | solution.py:325
  23.1 0.9 %collective-permute-start.9 = (bf16[512,128]{1,0:T(8,128)(2,1)S(1)}, bf16[512,128]{1,0:T(8,128)(2,1)S(1)}, u32[]{:S(2)}, u32[]{:S(2)}) collective-permute-start(bf16[512,128]{1,0:T(8,128)(2,1)S(1)} %get-tuple-element.54), channel_id=1, source_target_pairs={{0,4},{2,6},{4,0},{6,2},{8,12},{10,14},{12,8},{14,10},{16,20},{18,... | collective-permute-start | bytes 393224 | tf_op jit(solution)/shard_map/ppermute | solution.py:325
  24.0 1.6 %collective-permute-start.10 = (bf16[512,128]{1,0:T(8,128)(2,1)S(1)}, bf16[512,128]{1,0:T(8,128)(2,1)S(1)}, u32[]{:S(2)}, u32[]{:S(2)}) collective-permute-start(bf16[512,128]{1,0:T(8,128)(2,1)S(1)} %get-tuple-element.55), channel_id=1, source_target_pairs={{0,6},{2,4},{4,2},{6,0},{8,14},{10,12},{12,10},{14,8},{16,22},{18,... | collective-permute-start | bytes 393224 | tf_op jit(solution)/shard_map/ppermute | solution.py:325
  25.6 2.0 %shard_map.97 = (bf16[2560,512]{1,0:T(8,128)(2,1)S(1)}, f32[1,128]{1,0:T(1,128)S(1)}, f32[512,128]{1,0:T(8,128)S(1)}, f32[512,128]{1,0:T(8,128)S(1)}, bf16[528,1...) custom-call(bf16[2048,512]{1,0:T(8,128)(2,1)S(1)} %get-tuple-element.44.probs_ref, ...), custom_call_target="tpu_custom_call" | custom-call | tf_op jit(solution)/shard_map/pallas_call | solution.py:33
  27.6 1.0 %collective-permute-start.12 = (bf16[528,128]{1,0:T(8,128)(2,1)S(1)}, bf16[528,128]{1,0:T(8,128)(2,1)S(1)}, u32[]{:S(2)}, u32[]{:S(2)}) collective-permute-start(bf16[528,128]{1,0:T(8,128)(2,1)S(1)} %get-tuple-element.62), channel_id=1, source_target_pairs={{0,2},{2,0},{4,6},{6,4},{8,10},{10,8},{12,14},{14,12},{16,18},{18,... | collective-permute-start | bytes 405512 | tf_op jit(solution)/shard_map/ppermute | solution.py:325
  28.6 1.1 %collective-permute-start.13 = (bf16[528,128]{1,0:T(8,128)(2,1)S(1)}, bf16[528,128]{1,0:T(8,128)(2,1)S(1)}, u32[]{:S(2)}, u32[]{:S(2)}) collective-permute-start(bf16[528,128]{1,0:T(8,128)(2,1)S(1)} %get-tuple-element.63), channel_id=1, source_target_pairs={{0,4},{2,6},{4,0},{6,2},{8,12},{10,14},{12,8},{14,10},{16,20},{18,... | collective-permute-start | bytes 405512 | tf_op jit(solution)/shard_map/ppermute | solution.py:325
  29.8 1.4 %collective-permute-start.14 = (bf16[528,128]{1,0:T(8,128)(2,1)S(1)}, bf16[528,128]{1,0:T(8,128)(2,1)S(1)}, u32[]{:S(2)}, u32[]{:S(2)}) collective-permute-start(bf16[528,128]{1,0:T(8,128)(2,1)S(1)} %get-tuple-element.64), channel_id=1, source_target_pairs={{0,6},{2,4},{4,2},{6,0},{8,14},{10,12},{12,10},{14,8},{16,22},{18,... | collective-permute-start | bytes 405512 | tf_op jit(solution)/shard_map/ppermute | solution.py:325
  31.6 1.8 %collective-permute-start.11 = (bf16[512,128]{1,0:T(8,128)(2,1)S(1)}, bf16[512,128]{1,0:T(8,128)(2,1)S(1)}, u32[]{:S(2)}, u32[]{:S(2)}) collective-permute-start(bf16[512,128]{1,0:T(8,128)(2,1)S(1)} %get-tuple-element.57), channel_id=1, source_target_pairs={{0,24},{2,26},{4,28},{6,30},{8,0},{10,2},{12,4},{14,6},{16,8},{18,... | collective-permute-start | bytes 393224 | tf_op jit(solution)/shard_map/ppermute | solution.py:322
  33.4 1.0 %collective-permute-done.13.refs_1_ = bf16[528,128]{1,0:T(8,128)(2,1)S(1)} collective-permute-done((bf16[528,128]{1,0:T(8,128)(2,1)S(1)}, bf16[528,128]{1,0:T(8,128)(2,1)S(1)}, u32[]{:S(2)}, u32[]{:S(2)}) %collective-permute-start.13) | collective-permute-done | bytes 135200 | tf_op jit(solution)/shard_map/ppermute | solution.py:325
  34.3 1.4 %collective-permute-done.14.refs_2_ = bf16[528,128]{1,0:T(8,128)(2,1)S(1)} collective-permute-done((bf16[528,128]{1,0:T(8,128)(2,1)S(1)}, bf16[528,128]{1,0:T(8,128)(2,1)S(1)}, u32[]{:S(2)}, u32[]{:S(2)}) %collective-permute-start.14) | collective-permute-done | bytes 135200 | tf_op jit(solution)/shard_map/ppermute | solution.py:325
  36.0 1.8 %collective-permute-start.15 = (bf16[528,128]{1,0:T(8,128)(2,1)S(1)}, bf16[528,128]{1,0:T(8,128)(2,1)S(1)}, u32[]{:S(2)}, u32[]{:S(2)}) collective-permute-start(bf16[528,128]{1,0:T(8,128)(2,1)S(1)} %get-tuple-element.66), channel_id=1, source_target_pairs={{0,24},{2,26},{4,28},{6,30},{8,0},{10,2},{12,4},{14,6},{16,8},{18,... | collective-permute-start | bytes 405512 | tf_op jit(solution)/shard_map/ppermute | solution.py:322
  38.0 0.7 %collective-permute-start.16 = (f32[1,128]{1,0:T(1,128)S(1)}, f32[1,128]{1,0:T(1,128)S(1)}, u32[]{:S(2)}, u32[]{:S(2)}) collective-permute-start(f32[1,128]{1,0:T(1,128)S(1)} %get-tuple-element.67.sink_ref), channel_id=1, source_target_pairs={{0,16},{2,18},{4,20},{6,22},{8,24},{10,26},{12,28},{14,30},{16,0},... | collective-permute-start | bytes 1544 | tf_op jit(solution)/shard_map/ppermute | solution.py:322
  38.7 1.7 %shard_map.99 = (bf16[128,512]{1,0:T(8,128)(2,1)}, bf16[128,2048]{1,0:T(8,128)(2,1)}, f32[1,128]{1,0:T(1,128)S(1)}) custom-call(bf16[2560,512]{1,0:T(8,128)(2,1)S(1)} %get-tuple-element.50.gscores_ref, f32[512,128]{1,0:T(8,128)S(1)} %get-tuple-element.56.own_ref, bf16[512,128]{1,0:T(8,128)(2,1)S(1)} %collective-permute-done.11.last_ref, ...), custom_call_target="tpu_custom_call" | custom-call | flops 335544320 | tf_op jit(solution)/shard_map/pallas_call | solution.py:33
  40.4 2.6 %collective-permute-done.17.refs_1_ = f32[1,128]{1,0:T(1,128)S(1)} collective-permute-done((f32[1,128]{1,0:T(1,128)S(1)}, f32[1,128]{1,0:T(1,128)S(1)}, u32[]{:S(2)}, u32[]{:S(2)}) %collective-permute-start.17) | collective-permute-done | bytes 544 | tf_op jit(solution)/shard_map/ppermute | solution.py:322
  43.2 1.1 %collective-permute-done.18 = f32[1,128]{1,0:T(1,128)S(1)} collective-permute-done((f32[1,128]{1,0:T(1,128)S(1)}, f32[1,128]{1,0:T(1,128)S(1)}, u32[]{:S(2)}, u32[]{:S(2)}) %collective-permute-start.18) | collective-permute-done | bytes 544 | tf_op jit(solution)/shard_map/ppermute | solution.py:325
  44.3 0.7 %shard_map.102 = (bf16[128,512]{1,0:T(8,128)(2,1)}, f32[16]{0:T(128)}) custom-call(bf16[128,512]{1,0:T(8,128)(2,1)S(1)} %get-tuple-element.69.keys_ref, f32[1,128]{1,0:T(1,128)S(1)} %add.3.sink_ref), custom_call_target="tpu_custom_call" | custom-call | tf_op jit(solution)/shard_map/pallas_call | solution.py:33
  (23 shorter events, 1.6 us)
Async XLA Ops:
  0.6 8.8 %collective-permute-start = (bf16[128,512]{1,0:T(8,128)(2,1)}, bf16[128,512]{1,0:T(8,128)(2,1)S(1)}, u32[]{:S(2)}, u32[]{:S(2)}) collective-permute-start(bf16[128,512]{1,0:T(8,128)(2,1)} %bitcast.11), channel_id=1, source_target_pairs={{0,8},{2,10},{4,12},{6,14},{8,16},{10,18},{12,20},{14,22},{16,24},... | collective-permute-start | bytes 393224 | tf_op jit(solution)/shard_map/ppermute | solution.py:322
  4.7 0.7 %copy-start = (s32[1,16]{1,0:T(1,128)S(1)}, s32[1,16]{1,0:T(1,128)}, u32[]{:S(2)}) copy-start(s32[1,16]{1,0:T(1,128)} %docs_ref.1) | copy-start | bytes 196
  5.4 0.7 %copy-start.1 = (f32[16]{0:T(128)S(1)}, f32[16]{0:T(128)}, u32[]{:S(2)}) copy-start(f32[16]{0:T(128)} %sinks_ref.1) | copy-start | bytes 196
  6.6 7.7 %collective-permute-start.4 = (bf16[128,512]{1,0:T(8,128)(2,1)S(1)}, bf16[128,512]{1,0:T(8,128)(2,1)S(1)}, u32[]{:S(2)}, u32[]{:S(2)}) collective-permute-start(bf16[128,512]{1,0:T(8,128)(2,1)S(1)} %get-tuple-element.46), channel_id=1, source_target_pairs={{0,8},{2,10},{4,12},{6,14},{8,16},{10,18},{12,20},{14,22},{16,24},... | collective-permute-start | bytes 393224 | tf_op jit(solution)/shard_map/ppermute | solution.py:322
  9.5 8.0 %collective-permute-start.1 = (bf16[128,512]{1,0:T(8,128)(2,1)S(1)}, bf16[128,512]{1,0:T(8,128)(2,1)S(1)}, u32[]{:S(2)}, u32[]{:S(2)}) collective-permute-start(bf16[128,512]{1,0:T(8,128)(2,1)S(1)} %get-tuple-element.41), channel_id=1, source_target_pairs={{0,2},{2,0},{4,6},{6,4},{8,10},{10,8},{12,14},{14,12},{16,18},{18,... | collective-permute-start | bytes 393224 | tf_op jit(solution)/shard_map/ppermute | solution.py:325
  11.0 7.4 %collective-permute-start.2 = (bf16[128,512]{1,0:T(8,128)(2,1)S(1)}, bf16[128,512]{1,0:T(8,128)(2,1)S(1)}, u32[]{:S(2)}, u32[]{:S(2)}) collective-permute-start(bf16[128,512]{1,0:T(8,128)(2,1)S(1)} %get-tuple-element.42), channel_id=1, source_target_pairs={{0,4},{2,6},{4,0},{6,2},{8,12},{10,14},{12,8},{14,10},{16,20},{18,... | collective-permute-start | bytes 393224 | tf_op jit(solution)/shard_map/ppermute | solution.py:325
  12.6 7.4 %collective-permute-start.3 = (bf16[128,512]{1,0:T(8,128)(2,1)S(1)}, bf16[128,512]{1,0:T(8,128)(2,1)S(1)}, u32[]{:S(2)}, u32[]{:S(2)}) collective-permute-start(bf16[128,512]{1,0:T(8,128)(2,1)S(1)} %get-tuple-element.43), channel_id=1, source_target_pairs={{0,6},{2,4},{4,2},{6,0},{8,14},{10,12},{12,10},{14,8},{16,22},{18,... | collective-permute-start | bytes 393224 | tf_op jit(solution)/shard_map/ppermute | solution.py:325
  14.4 9.6 %collective-permute-start.5 = (bf16[128,512]{1,0:T(8,128)(2,1)S(1)}, bf16[128,512]{1,0:T(8,128)(2,1)S(1)}, u32[]{:S(2)}, u32[]{:S(2)}) collective-permute-start(bf16[128,512]{1,0:T(8,128)(2,1)S(1)} %get-tuple-element.47), channel_id=1, source_target_pairs={{0,2},{2,0},{4,6},{6,4},{8,10},{10,8},{12,14},{14,12},{16,18},{18,... | collective-permute-start | bytes 393224 | tf_op jit(solution)/shard_map/ppermute | solution.py:325
  16.0 9.7 %collective-permute-start.6 = (bf16[128,512]{1,0:T(8,128)(2,1)S(1)}, bf16[128,512]{1,0:T(8,128)(2,1)S(1)}, u32[]{:S(2)}, u32[]{:S(2)}) collective-permute-start(bf16[128,512]{1,0:T(8,128)(2,1)S(1)} %get-tuple-element.48), channel_id=1, source_target_pairs={{0,4},{2,6},{4,0},{6,2},{8,12},{10,14},{12,8},{14,10},{16,20},{18,... | collective-permute-start | bytes 393224 | tf_op jit(solution)/shard_map/ppermute | solution.py:325
  17.5 8.1 %collective-permute-start.7 = (bf16[128,512]{1,0:T(8,128)(2,1)S(1)}, bf16[128,512]{1,0:T(8,128)(2,1)S(1)}, u32[]{:S(2)}, u32[]{:S(2)}) collective-permute-start(bf16[128,512]{1,0:T(8,128)(2,1)S(1)} %get-tuple-element.49), channel_id=1, source_target_pairs={{0,6},{2,4},{4,2},{6,0},{8,14},{10,12},{12,10},{14,8},{16,22},{18,... | collective-permute-start | bytes 393224 | tf_op jit(solution)/shard_map/ppermute | solution.py:325
  22.1 7.7 %collective-permute-start.8 = (bf16[512,128]{1,0:T(8,128)(2,1)S(1)}, bf16[512,128]{1,0:T(8,128)(2,1)S(1)}, u32[]{:S(2)}, u32[]{:S(2)}) collective-permute-start(bf16[512,128]{1,0:T(8,128)(2,1)S(1)} %get-tuple-element.53), channel_id=1, source_target_pairs={{0,2},{2,0},{4,6},{6,4},{8,10},{10,8},{12,14},{14,12},{16,18},{18,... | collective-permute-start | bytes 393224 | tf_op jit(solution)/shard_map/ppermute | solution.py:325
  23.1 8.1 %collective-permute-start.9 = (bf16[512,128]{1,0:T(8,128)(2,1)S(1)}, bf16[512,128]{1,0:T(8,128)(2,1)S(1)}, u32[]{:S(2)}, u32[]{:S(2)}) collective-permute-start(bf16[512,128]{1,0:T(8,128)(2,1)S(1)} %get-tuple-element.54), channel_id=1, source_target_pairs={{0,4},{2,6},{4,0},{6,2},{8,12},{10,14},{12,8},{14,10},{16,20},{18,... | collective-permute-start | bytes 393224 | tf_op jit(solution)/shard_map/ppermute | solution.py:325
  24.0 7.5 %collective-permute-start.10 = (bf16[512,128]{1,0:T(8,128)(2,1)S(1)}, bf16[512,128]{1,0:T(8,128)(2,1)S(1)}, u32[]{:S(2)}, u32[]{:S(2)}) collective-permute-start(bf16[512,128]{1,0:T(8,128)(2,1)S(1)} %get-tuple-element.55), channel_id=1, source_target_pairs={{0,6},{2,4},{4,2},{6,0},{8,14},{10,12},{12,10},{14,8},{16,22},{18,... | collective-permute-start | bytes 393224 | tf_op jit(solution)/shard_map/ppermute | solution.py:325
  27.6 5.7 %collective-permute-start.12 = (bf16[528,128]{1,0:T(8,128)(2,1)S(1)}, bf16[528,128]{1,0:T(8,128)(2,1)S(1)}, u32[]{:S(2)}, u32[]{:S(2)}) collective-permute-start(bf16[528,128]{1,0:T(8,128)(2,1)S(1)} %get-tuple-element.62), channel_id=1, source_target_pairs={{0,2},{2,0},{4,6},{6,4},{8,10},{10,8},{12,14},{14,12},{16,18},{18,... | collective-permute-start | bytes 405512 | tf_op jit(solution)/shard_map/ppermute | solution.py:325
  28.6 5.7 %collective-permute-start.13 = (bf16[528,128]{1,0:T(8,128)(2,1)S(1)}, bf16[528,128]{1,0:T(8,128)(2,1)S(1)}, u32[]{:S(2)}, u32[]{:S(2)}) collective-permute-start(bf16[528,128]{1,0:T(8,128)(2,1)S(1)} %get-tuple-element.63), channel_id=1, source_target_pairs={{0,4},{2,6},{4,0},{6,2},{8,12},{10,14},{12,8},{14,10},{16,20},{18,... | collective-permute-start | bytes 405512 | tf_op jit(solution)/shard_map/ppermute | solution.py:325
  29.8 6.0 %collective-permute-start.14 = (bf16[528,128]{1,0:T(8,128)(2,1)S(1)}, bf16[528,128]{1,0:T(8,128)(2,1)S(1)}, u32[]{:S(2)}, u32[]{:S(2)}) collective-permute-start(bf16[528,128]{1,0:T(8,128)(2,1)S(1)} %get-tuple-element.64), channel_id=1, source_target_pairs={{0,6},{2,4},{4,2},{6,0},{8,14},{10,12},{12,10},{14,8},{16,22},{18,... | collective-permute-start | bytes 405512 | tf_op jit(solution)/shard_map/ppermute | solution.py:325
  31.6 7.1 %collective-permute-start.11 = (bf16[512,128]{1,0:T(8,128)(2,1)S(1)}, bf16[512,128]{1,0:T(8,128)(2,1)S(1)}, u32[]{:S(2)}, u32[]{:S(2)}) collective-permute-start(bf16[512,128]{1,0:T(8,128)(2,1)S(1)} %get-tuple-element.57), channel_id=1, source_target_pairs={{0,24},{2,26},{4,28},{6,30},{8,0},{10,2},{12,4},{14,6},{16,8},{18,... | collective-permute-start | bytes 393224 | tf_op jit(solution)/shard_map/ppermute | solution.py:322
  36.0 7.1 %collective-permute-start.15 = (bf16[528,128]{1,0:T(8,128)(2,1)S(1)}, bf16[528,128]{1,0:T(8,128)(2,1)S(1)}, u32[]{:S(2)}, u32[]{:S(2)}) collective-permute-start(bf16[528,128]{1,0:T(8,128)(2,1)S(1)} %get-tuple-element.66), channel_id=1, source_target_pairs={{0,24},{2,26},{4,28},{6,30},{8,0},{10,2},{12,4},{14,6},{16,8},{18,... | collective-permute-start | bytes 405512 | tf_op jit(solution)/shard_map/ppermute | solution.py:322
  37.7 5.3 %collective-permute-start.17 = (f32[1,128]{1,0:T(1,128)S(1)}, f32[1,128]{1,0:T(1,128)S(1)}, u32[]{:S(2)}, u32[]{:S(2)}) collective-permute-start(f32[1,128]{1,0:T(1,128)S(1)} %get-tuple-element.67.sink_ref), channel_id=1, source_target_pairs={{0,8},{2,10},{4,12},{6,14},{8,16},{10,18},{12,20},{14,22},{16,24},... | collective-permute-start | bytes 1544 | tf_op jit(solution)/shard_map/ppermute | solution.py:322
  38.0 5.0 %collective-permute-start.16 = (f32[1,128]{1,0:T(1,128)S(1)}, f32[1,128]{1,0:T(1,128)S(1)}, u32[]{:S(2)}, u32[]{:S(2)}) collective-permute-start(f32[1,128]{1,0:T(1,128)S(1)} %get-tuple-element.67.sink_ref), channel_id=1, source_target_pairs={{0,16},{2,18},{4,20},{6,22},{8,24},{10,26},{12,28},{14,30},{16,0},... | collective-permute-start | bytes 1544 | tf_op jit(solution)/shard_map/ppermute | solution.py:322
  43.1 1.2 %collective-permute-start.18 = (f32[1,128]{1,0:T(1,128)S(1)}, f32[1,128]{1,0:T(1,128)S(1)}, u32[]{:S(2)}, u32[]{:S(2)}) collective-permute-start(f32[1,128]{1,0:T(1,128)S(1)} %get-tuple-element.70), channel_id=1, source_target_pairs={{0,1},{1,0},{2,3},{3,2},{4,5},{5,4},{6,7},{7,6},{8,9},{9,8},{10,11... | collective-permute-start | bytes 1544 | tf_op jit(solution)/shard_map/ppermute | solution.py:325

commit v7 on v6

--- a/solution.py
+++ b/solution.py
@@ -282,19 +282,21 @@
         out_ref[:, head * size:(head + 1) * size] = block(total, head, rows).astype(BF16)
 
 
-def totals_kernel(own_ref, last_ref, sink_ref, *refs):
-    *sink_refs, keys_out, sink_out = refs
-    height = own_ref.shape[0]
-    side_by_side(own_ref, last_ref[:height, :], keys_out)
-    sink_row = sink_ref[...] + joined_terms(last_ref[height:, :])
+def planes_kernel(last_ref, sink_ref, *refs):
+    *sink_refs, sink_out = refs
+    sink_row = sink_ref[...] + joined_terms(last_ref[last_ref.shape[0] - TERM_ROWS:, :])
     for ref in sink_refs:
         sink_row = sink_row + ref[...]
     sink_out[...] = sink_row
 
 
-def out_kernel(keys_ref, sink_ref, keys_out, sink_out):
-    keys_out[...] = keys_ref[...]
-    sink_out[...] = sink_ref[0, :sink_out.shape[0]]
+def keys_end_kernel(own_ref, last_ref, keys_out, done_ref):
+    side_by_side(own_ref, last_ref[:own_ref.shape[0], :], keys_out)
+    done_ref[...] = jnp.zeros_like(done_ref)
+
+
+def out_kernel(sink_ref, done_ref, sink_out):
+    sink_out[...] = (sink_ref[...] + done_ref[...])[0, :sink_out.shape[0]]
 
 
 def local(queries, keys, values, grad_out, sinks, doc_ids):
@@ -389,19 +391,13 @@
     )
     sink_rows = [sink_row] + [along(sink_row, -distance) for distance in range(2 * reach, count, reach)]
     sink_rows.append(done)
-    grad_keys, sink_row = kernel_call(
-        totals_kernel,
-        [narrow, row],
-        [VMEM] * (2 + len(sink_rows)),
-        (keys_own, keys_last, *sink_rows),
-    )
+    sink_row, = kernel_call(planes_kernel, [row], [VMEM] * (1 + len(sink_rows)), (keys_last, *sink_rows))
+    grad_keys, done = kernel_call(keys_end_kernel, [narrow, row], [VMEM] * 2, (keys_own, keys_last))
     if lax.axis_size("dp") == 2:
         sink_row = sink_row + exchanged(sink_row, 1, "dp")
     else:
         sink_row = lax.psum(sink_row, "dp")
-    grad_keys, grad_sinks = kernel_call(
-        out_kernel, [narrow, jax.ShapeDtypeStruct(sinks.shape, F32)], [VMEM] * 2, (grad_keys, sink_row)
-    )
+    grad_sinks, = kernel_call(out_kernel, [jax.ShapeDtypeStruct(sinks.shape, F32)], [VMEM] * 2, (sink_row, done))
     return grad_queries[None], grad_keys[None], grad_values[None], grad_sinks
 
 

time: 45.1 us -> 45 us (level)
  waiting for transfers between devices: 9.56 us -> 8.88 us
  Pallas kernels: 7.55 us -> 8.06 us
    ppermute x13, waiting for transfers between devices: 5.73 us -> 5.05 us  [exchanged(): lax.ppermute(x, axis, [(i, i ^ step) for i in range(lax.axis_size(axis))])]
    pallas_call x10 -> x11, Pallas kernels: 7.55 us -> 8.06 us  [kernel_call(): pl.pallas_call(body, out_shape=out_shape, in_specs=in_specs, out_specs=[V...]
  transfers between devices with their start and end apart: 19 -> 19, of which waited for: 8 -> 8; matrix products, arithmetic and copies ran while one was open for 5% -> 5% of each run, Pallas kernels for 15% -> 17%
where the time goes in v7:
time: 45 us; the launch traced here: 44.8 us
  starting transfers between devices  23.5 us (52%)
  waiting for transfers between devices  8.88 us (20%)
  Pallas kernels  8.06 us (18%)
  other arithmetic  2.28 us (5%)
  local copies, waits for them, and re-layouts  1.31 us (3%)
  between operations  0.73 us (2%)
    ppermute x13, starting transfers between devices, exchanged(): lax.ppermute(x, axis, [(i, i ^ step) for i in range(lax.axis_size(axis))])  14.3 us
    ppermute x6, starting transfers between devices, along(): lax.ppermute(x, 'ctx', [(i, (i + distance) % count) for i in range(count)])  9.24 us
    pallas_call x11, Pallas kernels, kernel_call(): pl.pallas_call(body, out_shape=out_shape, in_specs=in_specs, out_specs=[V...  8.06 us
    ppermute x13, waiting for transfers between devices, exchanged(): lax.ppermute(x, axis, [(i, i ^ step) for i in range(lax.axis_size(axis))])  5.05 us
    ppermute x6, waiting for transfers between devices, along(): lax.ppermute(x, 'ctx', [(i, (i + distance) % count) for i in range(count)])  3.83 us
    unnamed x4, local copies, waits for them, and re-layouts  1.31 us
    concatenate x1, other arithmetic, local(): pair = jnp.concatenate([queries, grad_out], axis=1)  1.29 us
    concatenate x1, other arithmetic, local(): own = jnp.concatenate([keys, values], axis=1)  0.99 us
  transfers between devices with their start and end apart: 19, of which 8 were waited for; matrix products, arithmetic and copies ran while one was open for 5% of the time, Pallas kernels for 17%

profile of v7, /device:TPU:0, one launch (start us, length us, event | category | flops | bytes accessed | tf_op | source)
XLA Modules:
  0.0 44.8 jit_solution(5962312175400485248)
XLA Ops:
  0.6 3.1 %collective-permute-start = (bf16[128,512]{1,0:T(8,128)(2,1)}, bf16[128,512]{1,0:T(8,128)(2,1)S(1)}, u32[]{:S(2)}, u32[]{:S(2)}) collective-permute-start(bf16[128,512]{1,0:T(8,128)(2,1)} %bitcast.11), channel_id=1, source_target_pairs={{0,8},{2,10},{4,12},{6,14},{8,16},{10,18},{12,20},{14,22},{16,24},... | collective-permute-start | bytes 393224 | tf_op jit(solution)/shard_map/ppermute | solution.py:324
  3.7 1.0 %pad_maximum_fusion.1.own_ref.refs_0_ = bf16[128,1024]{1,0:T(8,128)(2,1)S(1)} fusion(bf16[128,512]{1,0:T(8,128)(2,1)} %bitcast.10, bf16[128,512]{1,0:T(8,128)(2,1)} %bitcast.12), kind=kLoop, calls=%fused_computation.1 | loop fusion | flops 524288 | bytes 524288 | tf_op jit(solution)/shard_map/concatenate | solution.py:330
  4.7 0.6 %copy-done = s32[1,16]{1,0:T(1,128)S(1)} copy-done((s32[1,16]{1,0:T(1,128)S(1)}, s32[1,16]{1,0:T(1,128)}, u32[]{:S(2)}) %copy-start) | copy-done | bytes 88
  5.4 0.7 %copy-done.1 = f32[16]{0:T(128)S(1)} copy-done((f32[16]{0:T(128)S(1)}, f32[16]{0:T(128)}, u32[]{:S(2)}) %copy-start.1) | copy-done | bytes 88
  6.0 0.6 %shard_map.93 = (f32[8,512]{1,0:T(8,128)S(1)}, f32[8,512]{1,0:T(8,128)S(1)}, bf16[128,512]{1,0:T(8,128)(2,1)S(1)}) custom-call(s32[1]{0:T(128)} %bitcast.place_ref, s32[1,16]{1,0:T(1,128)S(1)} %copy-done, f32[16]{0:T(128)S(1)} %copy-done.1, bf16[128,1024]{1,0:T(8,128)(2,1)S(1)} %pad_maximum_fusion.1.own_ref.refs_0_), custom_call_target="tpu_custom_call" | custom-call | tf_op jit(solution)/shard_map/pallas_call | solution.py:33
  6.6 1.6 %collective-permute-start.4 = (bf16[128,512]{1,0:T(8,128)(2,1)S(1)}, bf16[128,512]{1,0:T(8,128)(2,1)S(1)}, u32[]{:S(2)}, u32[]{:S(2)}) collective-permute-start(bf16[128,512]{1,0:T(8,128)(2,1)S(1)} %get-tuple-element.44), channel_id=1, source_target_pairs={{0,8},{2,10},{4,12},{6,14},{8,16},{10,18},{12,20},{14,22},{16,24},... | collective-permute-start | bytes 393224 | tf_op jit(solution)/shard_map/ppermute | solution.py:324
  8.2 1.2 %collective-permute-done.before_ref.refs_4_ = bf16[128,512]{1,0:T(8,128)(2,1)S(1)} collective-permute-done((bf16[128,512]{1,0:T(8,128)(2,1)}, bf16[128,512]{1,0:T(8,128)(2,1)S(1)}, u32[]{:S(2)}, u32[]{:S(2)}) %collective-permute-start) | collective-permute-done | bytes 131104 | tf_op jit(solution)/shard_map/ppermute | solution.py:324
  9.5 1.6 %collective-permute-start.1 = (bf16[128,512]{1,0:T(8,128)(2,1)S(1)}, bf16[128,512]{1,0:T(8,128)(2,1)S(1)}, u32[]{:S(2)}, u32[]{:S(2)}) collective-permute-start(bf16[128,512]{1,0:T(8,128)(2,1)S(1)} %get-tuple-element.39), channel_id=1, source_target_pairs={{0,2},{2,0},{4,6},{6,4},{8,10},{10,8},{12,14},{14,12},{16,18},{18,... | collective-permute-start | bytes 393224 | tf_op jit(solution)/shard_map/ppermute | solution.py:327
  11.0 1.5 %collective-permute-start.2 = (bf16[128,512]{1,0:T(8,128)(2,1)S(1)}, bf16[128,512]{1,0:T(8,128)(2,1)S(1)}, u32[]{:S(2)}, u32[]{:S(2)}) collective-permute-start(bf16[128,512]{1,0:T(8,128)(2,1)S(1)} %get-tuple-element.40), channel_id=1, source_target_pairs={{0,4},{2,6},{4,0},{6,2},{8,12},{10,14},{12,8},{14,10},{16,20},{18,... | collective-permute-start | bytes 393224 | tf_op jit(solution)/shard_map/ppermute | solution.py:327
  12.6 0.5 %collective-permute-start.3 = (bf16[128,512]{1,0:T(8,128)(2,1)S(1)}, bf16[128,512]{1,0:T(8,128)(2,1)S(1)}, u32[]{:S(2)}, u32[]{:S(2)}) collective-permute-start(bf16[128,512]{1,0:T(8,128)(2,1)S(1)} %get-tuple-element.41), channel_id=1, source_target_pairs={{0,6},{2,4},{4,2},{6,0},{8,14},{10,12},{12,10},{14,8},{16,22},{18,... | collective-permute-start | bytes 393224 | tf_op jit(solution)/shard_map/ppermute | solution.py:327
  13.0 1.3 %pad_maximum_fusion.pair_ref.refs_0_ = bf16[128,4096]{1,0:T(8,128)(2,1)S(1)} fusion(bf16[128,2048]{1,0:T(8,128)(2,1)} %bitcast.8, bf16[128,2048]{1,0:T(8,128)(2,1)} %bitcast.9), kind=kLoop, calls=%fused_computation | loop fusion | flops 2097152 | bytes 2097152 | tf_op jit(solution)/shard_map/concatenate | solution.py:331
  14.4 1.6 %collective-permute-start.5 = (bf16[128,512]{1,0:T(8,128)(2,1)S(1)}, bf16[128,512]{1,0:T(8,128)(2,1)S(1)}, u32[]{:S(2)}, u32[]{:S(2)}) collective-permute-start(bf16[128,512]{1,0:T(8,128)(2,1)S(1)} %get-tuple-element.45), channel_id=1, source_target_pairs={{0,2},{2,0},{4,6},{6,4},{8,10},{10,8},{12,14},{14,12},{16,18},{18,... | collective-permute-start | bytes 393224 | tf_op jit(solution)/shard_map/ppermute | solution.py:327
  16.0 1.5 %collective-permute-start.6 = (bf16[128,512]{1,0:T(8,128)(2,1)S(1)}, bf16[128,512]{1,0:T(8,128)(2,1)S(1)}, u32[]{:S(2)}, u32[]{:S(2)}) collective-permute-start(bf16[128,512]{1,0:T(8,128)(2,1)S(1)} %get-tuple-element.46), channel_id=1, source_target_pairs={{0,4},{2,6},{4,0},{6,2},{8,12},{10,14},{12,8},{14,10},{16,20},{18,... | collective-permute-start | bytes 393224 | tf_op jit(solution)/shard_map/ppermute | solution.py:327
  17.5 0.5 %collective-permute-start.7 = (bf16[128,512]{1,0:T(8,128)(2,1)S(1)}, bf16[128,512]{1,0:T(8,128)(2,1)S(1)}, u32[]{:S(2)}, u32[]{:S(2)}) collective-permute-start(bf16[128,512]{1,0:T(8,128)(2,1)S(1)} %get-tuple-element.47), channel_id=1, source_target_pairs={{0,6},{2,4},{4,2},{6,0},{8,14},{10,12},{12,10},{14,8},{16,22},{18,... | collective-permute-start | bytes 393224 | tf_op jit(solution)/shard_map/ppermute | solution.py:327
  18.4 1.5 %collective-permute-done.3.refs_3_ = bf16[128,512]{1,0:T(8,128)(2,1)S(1)} collective-permute-done((bf16[128,512]{1,0:T(8,128)(2,1)S(1)}, bf16[128,512]{1,0:T(8,128)(2,1)S(1)}, u32[]{:S(2)}, u32[]{:S(2)}) %collective-permute-start.3) | collective-permute-done | bytes 131104 | tf_op jit(solution)/shard_map/ppermute | solution.py:327
  19.9 2.1 %shard_map.95 = (bf16[2048,512]{1,0:T(8,128)(2,1)S(1)}, f32[8,512]{1,0:T(8,128)S(1)}, f32[512,128]{1,0:T(8,128)S(1)}, f32[512,128]{1,0:T(8,128)S(1)}, bf16[512,1...) custom-call(f32[8,512]{1,0:T(8,128)S(1)} %get-tuple-element.37.refs_0_.caps_ref, ...), custom_call_target="tpu_custom_call" | custom-call | tf_op jit(solution)/shard_map/pallas_call | solution.py:33
  22.1 1.0 %collective-permute-start.8 = (bf16[512,128]{1,0:T(8,128)(2,1)S(1)}, bf16[512,128]{1,0:T(8,128)(2,1)S(1)}, u32[]{:S(2)}, u32[]{:S(2)}) collective-permute-start(bf16[512,128]{1,0:T(8,128)(2,1)S(1)} %get-tuple-element.51), channel_id=1, source_target_pairs={{0,2},{2,0},{4,6},{6,4},{8,10},{10,8},{12,14},{14,12},{16,18},{18,... | collective-permute-start | bytes 393224 | tf_op jit(solution)/shard_map/ppermute | solution.py:327
  23.1 0.9 %collective-permute-start.9 = (bf16[512,128]{1,0:T(8,128)(2,1)S(1)}, bf16[512,128]{1,0:T(8,128)(2,1)S(1)}, u32[]{:S(2)}, u32[]{:S(2)}) collective-permute-start(bf16[512,128]{1,0:T(8,128)(2,1)S(1)} %get-tuple-element.52), channel_id=1, source_target_pairs={{0,4},{2,6},{4,0},{6,2},{8,12},{10,14},{12,8},{14,10},{16,20},{18,... | collective-permute-start | bytes 393224 | tf_op jit(solution)/shard_map/ppermute | solution.py:327
  24.0 1.6 %collective-permute-start.10 = (bf16[512,128]{1,0:T(8,128)(2,1)S(1)}, bf16[512,128]{1,0:T(8,128)(2,1)S(1)}, u32[]{:S(2)}, u32[]{:S(2)}) collective-permute-start(bf16[512,128]{1,0:T(8,128)(2,1)S(1)} %get-tuple-element.53), channel_id=1, source_target_pairs={{0,6},{2,4},{4,2},{6,0},{8,14},{10,12},{12,10},{14,8},{16,22},{18,... | collective-permute-start | bytes 393224 | tf_op jit(solution)/shard_map/ppermute | solution.py:327
  25.6 2.0 %shard_map.97 = (bf16[2560,512]{1,0:T(8,128)(2,1)S(1)}, f32[1,128]{1,0:T(1,128)S(1)}, f32[512,128]{1,0:T(8,128)S(1)}, f32[512,128]{1,0:T(8,128)S(1)}, bf16[528,1...) custom-call(bf16[2048,512]{1,0:T(8,128)(2,1)S(1)} %get-tuple-element.42.probs_ref, ...), custom_call_target="tpu_custom_call" | custom-call | tf_op jit(solution)/shard_map/pallas_call | solution.py:33
  27.6 1.0 %collective-permute-start.12 = (bf16[528,128]{1,0:T(8,128)(2,1)S(1)}, bf16[528,128]{1,0:T(8,128)(2,1)S(1)}, u32[]{:S(2)}, u32[]{:S(2)}) collective-permute-start(bf16[528,128]{1,0:T(8,128)(2,1)S(1)} %get-tuple-element.60), channel_id=1, source_target_pairs={{0,2},{2,0},{4,6},{6,4},{8,10},{10,8},{12,14},{14,12},{16,18},{18,... | collective-permute-start | bytes 405512 | tf_op jit(solution)/shard_map/ppermute | solution.py:327
  28.6 1.1 %collective-permute-start.13 = (bf16[528,128]{1,0:T(8,128)(2,1)S(1)}, bf16[528,128]{1,0:T(8,128)(2,1)S(1)}, u32[]{:S(2)}, u32[]{:S(2)}) collective-permute-start(bf16[528,128]{1,0:T(8,128)(2,1)S(1)} %get-tuple-element.61), channel_id=1, source_target_pairs={{0,4},{2,6},{4,0},{6,2},{8,12},{10,14},{12,8},{14,10},{16,20},{18,... | collective-permute-start | bytes 405512 | tf_op jit(solution)/shard_map/ppermute | solution.py:327
  29.8 1.4 %collective-permute-start.14 = (bf16[528,128]{1,0:T(8,128)(2,1)S(1)}, bf16[528,128]{1,0:T(8,128)(2,1)S(1)}, u32[]{:S(2)}, u32[]{:S(2)}) collective-permute-start(bf16[528,128]{1,0:T(8,128)(2,1)S(1)} %get-tuple-element.62), channel_id=1, source_target_pairs={{0,6},{2,4},{4,2},{6,0},{8,14},{10,12},{12,10},{14,8},{16,22},{18,... | collective-permute-start | bytes 405512 | tf_op jit(solution)/shard_map/ppermute | solution.py:327
  31.6 1.8 %collective-permute-start.11 = (bf16[512,128]{1,0:T(8,128)(2,1)S(1)}, bf16[512,128]{1,0:T(8,128)(2,1)S(1)}, u32[]{:S(2)}, u32[]{:S(2)}) collective-permute-start(bf16[512,128]{1,0:T(8,128)(2,1)S(1)} %get-tuple-element.55), channel_id=1, source_target_pairs={{0,24},{2,26},{4,28},{6,30},{8,0},{10,2},{12,4},{14,6},{16,8},{18,... | collective-permute-start | bytes 393224 | tf_op jit(solution)/shard_map/ppermute | solution.py:324
  33.4 1.0 %collective-permute-done.13.refs_1_ = bf16[528,128]{1,0:T(8,128)(2,1)S(1)} collective-permute-done((bf16[528,128]{1,0:T(8,128)(2,1)S(1)}, bf16[528,128]{1,0:T(8,128)(2,1)S(1)}, u32[]{:S(2)}, u32[]{:S(2)}) %collective-permute-start.13) | collective-permute-done | bytes 135200 | tf_op jit(solution)/shard_map/ppermute | solution.py:327
  34.3 1.4 %collective-permute-done.14.refs_2_ = bf16[528,128]{1,0:T(8,128)(2,1)S(1)} collective-permute-done((bf16[528,128]{1,0:T(8,128)(2,1)S(1)}, bf16[528,128]{1,0:T(8,128)(2,1)S(1)}, u32[]{:S(2)}, u32[]{:S(2)}) %collective-permute-start.14) | collective-permute-done | bytes 135200 | tf_op jit(solution)/shard_map/ppermute | solution.py:327
  36.0 1.8 %collective-permute-start.15 = (bf16[528,128]{1,0:T(8,128)(2,1)S(1)}, bf16[528,128]{1,0:T(8,128)(2,1)S(1)}, u32[]{:S(2)}, u32[]{:S(2)}) collective-permute-start(bf16[528,128]{1,0:T(8,128)(2,1)S(1)} %get-tuple-element.64), channel_id=1, source_target_pairs={{0,24},{2,26},{4,28},{6,30},{8,0},{10,2},{12,4},{14,6},{16,8},{18,... | collective-permute-start | bytes 405512 | tf_op jit(solution)/shard_map/ppermute | solution.py:324
  38.0 0.7 %collective-permute-start.16 = (f32[1,128]{1,0:T(1,128)S(1)}, f32[1,128]{1,0:T(1,128)S(1)}, u32[]{:S(2)}, u32[]{:S(2)}) collective-permute-start(f32[1,128]{1,0:T(1,128)S(1)} %get-tuple-element.67.sink_ref), channel_id=1, source_target_pairs={{0,16},{2,18},{4,20},{6,22},{8,24},{10,26},{12,28},{14,30},{16,0},... | collective-permute-start | bytes 1544 | tf_op jit(solution)/shard_map/ppermute | solution.py:324
  38.7 1.7 %shard_map.99 = (bf16[128,512]{1,0:T(8,128)(2,1)}, bf16[128,2048]{1,0:T(8,128)(2,1)}, f32[1,128]{1,0:T(1,128)S(1)}) custom-call(bf16[2560,512]{1,0:T(8,128)(2,1)S(1)} %get-tuple-element.48.gscores_ref, f32[512,128]{1,0:T(8,128)S(1)} %get-tuple-element.54.own_ref, bf16[512,128]{1,0:T(8,128)(2,1)S(1)} %collective-permute-done.11.last_ref, ...), custom_call_target="tpu_custom_call" | custom-call | flops 335544320 | tf_op jit(solution)/shard_map/pallas_call | solution.py:33
  40.4 2.6 %collective-permute-done.17.refs_1_ = f32[1,128]{1,0:T(1,128)S(1)} collective-permute-done((f32[1,128]{1,0:T(1,128)S(1)}, f32[1,128]{1,0:T(1,128)S(1)}, u32[]{:S(2)}, u32[]{:S(2)}) %collective-permute-start.17) | collective-permute-done | bytes 544 | tf_op jit(solution)/shard_map/ppermute | solution.py:324
  43.2 0.7 %shard_map.101 = (bf16[128,512]{1,0:T(8,128)(2,1)}, f32[1,128]{1,0:T(1,128)S(1)}) custom-call(f32[512,128]{1,0:T(8,128)S(1)} %get-tuple-element.63.own_ref, bf16[528,128]{1,0:T(8,128)(2,1)S(1)} %collective-permute-done.15.last_ref), custom_call_target="tpu_custom_call" | custom-call | tf_op jit(solution)/shard_map/pallas_call | solution.py:33
  44.3 0.5 %shard_map.103 = f32[16]{0:T(128)} custom-call(f32[1,128]{1,0:T(1,128)S(1)} %add.3.sink_ref, f32[1,128]{1,0:T(1,128)S(1)} %get-tuple-element.69.done_ref), custom_call_target="tpu_custom_call" | custom-call | tf_op jit(solution)/shard_map/pallas_call | solution.py:33
  (24 shorter events, 2.0 us)
Async XLA Ops:
  0.6 8.8 %collective-permute-start = (bf16[128,512]{1,0:T(8,128)(2,1)}, bf16[128,512]{1,0:T(8,128)(2,1)S(1)}, u32[]{:S(2)}, u32[]{:S(2)}) collective-permute-start(bf16[128,512]{1,0:T(8,128)(2,1)} %bitcast.11), channel_id=1, source_target_pairs={{0,8},{2,10},{4,12},{6,14},{8,16},{10,18},{12,20},{14,22},{16,24},... | collective-permute-start | bytes 393224 | tf_op jit(solution)/shard_map/ppermute | solution.py:324
  4.7 0.7 %copy-start = (s32[1,16]{1,0:T(1,128)S(1)}, s32[1,16]{1,0:T(1,128)}, u32[]{:S(2)}) copy-start(s32[1,16]{1,0:T(1,128)} %docs_ref.1) | copy-start | bytes 196
  5.4 0.7 %copy-start.1 = (f32[16]{0:T(128)S(1)}, f32[16]{0:T(128)}, u32[]{:S(2)}) copy-start(f32[16]{0:T(128)} %sinks_ref.1) | copy-start | bytes 196
  6.6 7.7 %collective-permute-start.4 = (bf16[128,512]{1,0:T(8,128)(2,1)S(1)}, bf16[128,512]{1,0:T(8,128)(2,1)S(1)}, u32[]{:S(2)}, u32[]{:S(2)}) collective-permute-start(bf16[128,512]{1,0:T(8,128)(2,1)S(1)} %get-tuple-element.44), channel_id=1, source_target_pairs={{0,8},{2,10},{4,12},{6,14},{8,16},{10,18},{12,20},{14,22},{16,24},... | collective-permute-start | bytes 393224 | tf_op jit(solution)/shard_map/ppermute | solution.py:324
  9.5 8.0 %collective-permute-start.1 = (bf16[128,512]{1,0:T(8,128)(2,1)S(1)}, bf16[128,512]{1,0:T(8,128)(2,1)S(1)}, u32[]{:S(2)}, u32[]{:S(2)}) collective-permute-start(bf16[128,512]{1,0:T(8,128)(2,1)S(1)} %get-tuple-element.39), channel_id=1, source_target_pairs={{0,2},{2,0},{4,6},{6,4},{8,10},{10,8},{12,14},{14,12},{16,18},{18,... | collective-permute-start | bytes 393224 | tf_op jit(solution)/shard_map/ppermute | solution.py:327
  11.0 7.4 %collective-permute-start.2 = (bf16[128,512]{1,0:T(8,128)(2,1)S(1)}, bf16[128,512]{1,0:T(8,128)(2,1)S(1)}, u32[]{:S(2)}, u32[]{:S(2)}) collective-permute-start(bf16[128,512]{1,0:T(8,128)(2,1)S(1)} %get-tuple-element.40), channel_id=1, source_target_pairs={{0,4},{2,6},{4,0},{6,2},{8,12},{10,14},{12,8},{14,10},{16,20},{18,... | collective-permute-start | bytes 393224 | tf_op jit(solution)/shard_map/ppermute | solution.py:327
  12.6 7.4 %collective-permute-start.3 = (bf16[128,512]{1,0:T(8,128)(2,1)S(1)}, bf16[128,512]{1,0:T(8,128)(2,1)S(1)}, u32[]{:S(2)}, u32[]{:S(2)}) collective-permute-start(bf16[128,512]{1,0:T(8,128)(2,1)S(1)} %get-tuple-element.41), channel_id=1, source_target_pairs={{0,6},{2,4},{4,2},{6,0},{8,14},{10,12},{12,10},{14,8},{16,22},{18,... | collective-permute-start | bytes 393224 | tf_op jit(solution)/shard_map/ppermute | solution.py:327
  14.4 9.6 %collective-permute-start.5 = (bf16[128,512]{1,0:T(8,128)(2,1)S(1)}, bf16[128,512]{1,0:T(8,128)(2,1)S(1)}, u32[]{:S(2)}, u32[]{:S(2)}) collective-permute-start(bf16[128,512]{1,0:T(8,128)(2,1)S(1)} %get-tuple-element.45), channel_id=1, source_target_pairs={{0,2},{2,0},{4,6},{6,4},{8,10},{10,8},{12,14},{14,12},{16,18},{18,... | collective-permute-start | bytes 393224 | tf_op jit(solution)/shard_map/ppermute | solution.py:327
  16.0 9.7 %collective-permute-start.6 = (bf16[128,512]{1,0:T(8,128)(2,1)S(1)}, bf16[128,512]{1,0:T(8,128)(2,1)S(1)}, u32[]{:S(2)}, u32[]{:S(2)}) collective-permute-start(bf16[128,512]{1,0:T(8,128)(2,1)S(1)} %get-tuple-element.46), channel_id=1, source_target_pairs={{0,4},{2,6},{4,0},{6,2},{8,12},{10,14},{12,8},{14,10},{16,20},{18,... | collective-permute-start | bytes 393224 | tf_op jit(solution)/shard_map/ppermute | solution.py:327
  17.5 8.1 %collective-permute-start.7 = (bf16[128,512]{1,0:T(8,128)(2,1)S(1)}, bf16[128,512]{1,0:T(8,128)(2,1)S(1)}, u32[]{:S(2)}, u32[]{:S(2)}) collective-permute-start(bf16[128,512]{1,0:T(8,128)(2,1)S(1)} %get-tuple-element.47), channel_id=1, source_target_pairs={{0,6},{2,4},{4,2},{6,0},{8,14},{10,12},{12,10},{14,8},{16,22},{18,... | collective-permute-start | bytes 393224 | tf_op jit(solution)/shard_map/ppermute | solution.py:327
  22.1 7.7 %collective-permute-start.8 = (bf16[512,128]{1,0:T(8,128)(2,1)S(1)}, bf16[512,128]{1,0:T(8,128)(2,1)S(1)}, u32[]{:S(2)}, u32[]{:S(2)}) collective-permute-start(bf16[512,128]{1,0:T(8,128)(2,1)S(1)} %get-tuple-element.51), channel_id=1, source_target_pairs={{0,2},{2,0},{4,6},{6,4},{8,10},{10,8},{12,14},{14,12},{16,18},{18,... | collective-permute-start | bytes 393224 | tf_op jit(solution)/shard_map/ppermute | solution.py:327
  23.1 8.1 %collective-permute-start.9 = (bf16[512,128]{1,0:T(8,128)(2,1)S(1)}, bf16[512,128]{1,0:T(8,128)(2,1)S(1)}, u32[]{:S(2)}, u32[]{:S(2)}) collective-permute-start(bf16[512,128]{1,0:T(8,128)(2,1)S(1)} %get-tuple-element.52), channel_id=1, source_target_pairs={{0,4},{2,6},{4,0},{6,2},{8,12},{10,14},{12,8},{14,10},{16,20},{18,... | collective-permute-start | bytes 393224 | tf_op jit(solution)/shard_map/ppermute | solution.py:327
  24.0 7.5 %collective-permute-start.10 = (bf16[512,128]{1,0:T(8,128)(2,1)S(1)}, bf16[512,128]{1,0:T(8,128)(2,1)S(1)}, u32[]{:S(2)}, u32[]{:S(2)}) collective-permute-start(bf16[512,128]{1,0:T(8,128)(2,1)S(1)} %get-tuple-element.53), channel_id=1, source_target_pairs={{0,6},{2,4},{4,2},{6,0},{8,14},{10,12},{12,10},{14,8},{16,22},{18,... | collective-permute-start | bytes 393224 | tf_op jit(solution)/shard_map/ppermute | solution.py:327
  27.6 5.7 %collective-permute-start.12 = (bf16[528,128]{1,0:T(8,128)(2,1)S(1)}, bf16[528,128]{1,0:T(8,128)(2,1)S(1)}, u32[]{:S(2)}, u32[]{:S(2)}) collective-permute-start(bf16[528,128]{1,0:T(8,128)(2,1)S(1)} %get-tuple-element.60), channel_id=1, source_target_pairs={{0,2},{2,0},{4,6},{6,4},{8,10},{10,8},{12,14},{14,12},{16,18},{18,... | collective-permute-start | bytes 405512 | tf_op jit(solution)/shard_map/ppermute | solution.py:327
  28.6 5.7 %collective-permute-start.13 = (bf16[528,128]{1,0:T(8,128)(2,1)S(1)}, bf16[528,128]{1,0:T(8,128)(2,1)S(1)}, u32[]{:S(2)}, u32[]{:S(2)}) collective-permute-start(bf16[528,128]{1,0:T(8,128)(2,1)S(1)} %get-tuple-element.61), channel_id=1, source_target_pairs={{0,4},{2,6},{4,0},{6,2},{8,12},{10,14},{12,8},{14,10},{16,20},{18,... | collective-permute-start | bytes 405512 | tf_op jit(solution)/shard_map/ppermute | solution.py:327
  29.8 6.0 %collective-permute-start.14 = (bf16[528,128]{1,0:T(8,128)(2,1)S(1)}, bf16[528,128]{1,0:T(8,128)(2,1)S(1)}, u32[]{:S(2)}, u32[]{:S(2)}) collective-permute-start(bf16[528,128]{1,0:T(8,128)(2,1)S(1)} %get-tuple-element.62), channel_id=1, source_target_pairs={{0,6},{2,4},{4,2},{6,0},{8,14},{10,12},{12,10},{14,8},{16,22},{18,... | collective-permute-start | bytes 405512 | tf_op jit(solution)/shard_map/ppermute | solution.py:327
  31.6 7.1 %collective-permute-start.11 = (bf16[512,128]{1,0:T(8,128)(2,1)S(1)}, bf16[512,128]{1,0:T(8,128)(2,1)S(1)}, u32[]{:S(2)}, u32[]{:S(2)}) collective-permute-start(bf16[512,128]{1,0:T(8,128)(2,1)S(1)} %get-tuple-element.55), channel_id=1, source_target_pairs={{0,24},{2,26},{4,28},{6,30},{8,0},{10,2},{12,4},{14,6},{16,8},{18,... | collective-permute-start | bytes 393224 | tf_op jit(solution)/shard_map/ppermute | solution.py:324
  36.0 7.1 %collective-permute-start.15 = (bf16[528,128]{1,0:T(8,128)(2,1)S(1)}, bf16[528,128]{1,0:T(8,128)(2,1)S(1)}, u32[]{:S(2)}, u32[]{:S(2)}) collective-permute-start(bf16[528,128]{1,0:T(8,128)(2,1)S(1)} %get-tuple-element.64), channel_id=1, source_target_pairs={{0,24},{2,26},{4,28},{6,30},{8,0},{10,2},{12,4},{14,6},{16,8},{18,... | collective-permute-start | bytes 405512 | tf_op jit(solution)/shard_map/ppermute | solution.py:324
  37.7 5.3 %collective-permute-start.17 = (f32[1,128]{1,0:T(1,128)S(1)}, f32[1,128]{1,0:T(1,128)S(1)}, u32[]{:S(2)}, u32[]{:S(2)}) collective-permute-start(f32[1,128]{1,0:T(1,128)S(1)} %get-tuple-element.67.sink_ref), channel_id=1, source_target_pairs={{0,8},{2,10},{4,12},{6,14},{8,16},{10,18},{12,20},{14,22},{16,24},... | collective-permute-start | bytes 1544 | tf_op jit(solution)/shard_map/ppermute | solution.py:324
  38.0 5.0 %collective-permute-start.16 = (f32[1,128]{1,0:T(1,128)S(1)}, f32[1,128]{1,0:T(1,128)S(1)}, u32[]{:S(2)}, u32[]{:S(2)}) collective-permute-start(f32[1,128]{1,0:T(1,128)S(1)} %get-tuple-element.67.sink_ref), channel_id=1, source_target_pairs={{0,16},{2,18},{4,20},{6,22},{8,24},{10,26},{12,28},{14,30},{16,0},... | collective-permute-start | bytes 1544 | tf_op jit(solution)/shard_map/ppermute | solution.py:324
  43.1 1.2 %collective-permute-start.18 = (f32[1,128]{1,0:T(1,128)S(1)}, f32[1,128]{1,0:T(1,128)S(1)}, u32[]{:S(2)}, u32[]{:S(2)}) collective-permute-start(f32[1,128]{1,0:T(1,128)S(1)} %shard_map.102), channel_id=1, source_target_pairs={{0,1},{1,0},{2,3},{3,2},{4,5},{5,4},{6,7},{7,6},{8,9},{9,8},{10,11... | collective-permute-start | bytes 1544 | tf_op jit(solution)/shard_map/ppermute | solution.py:327

commit v8 on v7

--- a/solution.py
+++ b/solution.py
@@ -239,7 +239,7 @@
     for head in range(kv_heads):
         cut = slice(head * size, (head + 1) * size)
         keys = jnp.concatenate([r[:, cut] for r in blocks], axis=0)
-        dq = (dot_tn(gscores_ref[head * span:(head + 1) * span, :], keys) * scale).astype(BF16)
+        dq = jnp.transpose((dot_tn(keys, gscores_ref[head * span:(head + 1) * span, :]) * scale).astype(BF16))
         for j in range(group):
             at = (head * group + j) * size
             dq_ref[:, at:at + size] = dq[j * rows:(j + 1) * rows]

time: 45 us -> 45 us (level)
  transfers between devices with their start and end apart: 19 -> 19, of which waited for: 8 -> 8; matrix products, arithmetic and copies ran while one was open for 5% -> 5% of each run, Pallas kernels for 17% -> 16%
where the time goes in v8:
time: 45 us; the launch traced here: 44.8 us
  starting transfers between devices  23.5 us (52%)
  waiting for transfers between devices  9.09 us (20%)
  Pallas kernels  7.85 us (17%)
  other arithmetic  2.28 us (5%)
  local copies, waits for them, and re-layouts  1.31 us (3%)
  between operations  0.73 us (2%)
    ppermute x13, starting transfers between devices, exchanged(): lax.ppermute(x, axis, [(i, i ^ step) for i in range(lax.axis_size(axis))])  14.3 us
    ppermute x6, starting transfers between devices, along(): lax.ppermute(x, 'ctx', [(i, (i + distance) % count) for i in range(count)])  9.24 us
    pallas_call x11, Pallas kernels, kernel_call(): pl.pallas_call(body, out_shape=out_shape, in_specs=in_specs, out_specs=[V...  7.85 us
    ppermute x13, waiting for transfers between devices, exchanged(): lax.ppermute(x, axis, [(i, i ^ step) for i in range(lax.axis_size(axis))])  5.05 us
    ppermute x6, waiting for transfers between devices, along(): lax.ppermute(x, 'ctx', [(i, (i + distance) % count) for i in range(count)])  4.04 us
    unnamed x4, local copies, waits for them, and re-layouts  1.31 us
    concatenate x1, other arithmetic, local(): pair = jnp.concatenate([queries, grad_out], axis=1)  1.29 us
    concatenate x1, other arithmetic, local(): own = jnp.concatenate([keys, values], axis=1)  0.99 us
  transfers between devices with their start and end apart: 19, of which 8 were waited for; matrix products, arithmetic and copies ran while one was open for 5% of the time, Pallas kernels for 16%

profile of v8, /device:TPU:0, one launch (start us, length us, event | category | flops | bytes accessed | tf_op | source)
XLA Modules:
  0.0 44.8 jit_solution(14580247011705790098)
XLA Ops:
  0.6 3.1 %collective-permute-start = (bf16[128,512]{1,0:T(8,128)(2,1)}, bf16[128,512]{1,0:T(8,128)(2,1)S(1)}, u32[]{:S(2)}, u32[]{:S(2)}) collective-permute-start(bf16[128,512]{1,0:T(8,128)(2,1)} %bitcast.11), channel_id=1, source_target_pairs={{0,8},{2,10},{4,12},{6,14},{8,16},{10,18},{12,20},{14,22},{16,24},... | collective-permute-start | bytes 393224 | tf_op jit(solution)/shard_map/ppermute | solution.py:324
  3.7 1.0 %pad_maximum_fusion.1.own_ref.refs_0_ = bf16[128,1024]{1,0:T(8,128)(2,1)S(1)} fusion(bf16[128,512]{1,0:T(8,128)(2,1)} %bitcast.10, bf16[128,512]{1,0:T(8,128)(2,1)} %bitcast.12), kind=kLoop, calls=%fused_computation.1 | loop fusion | flops 524288 | bytes 524288 | tf_op jit(solution)/shard_map/concatenate | solution.py:330
  4.7 0.6 %copy-done = s32[1,16]{1,0:T(1,128)S(1)} copy-done((s32[1,16]{1,0:T(1,128)S(1)}, s32[1,16]{1,0:T(1,128)}, u32[]{:S(2)}) %copy-start) | copy-done | bytes 88
  5.4 0.7 %copy-done.1 = f32[16]{0:T(128)S(1)} copy-done((f32[16]{0:T(128)S(1)}, f32[16]{0:T(128)}, u32[]{:S(2)}) %copy-start.1) | copy-done | bytes 88
  6.0 0.6 %shard_map.93 = (f32[8,512]{1,0:T(8,128)S(1)}, f32[8,512]{1,0:T(8,128)S(1)}, bf16[128,512]{1,0:T(8,128)(2,1)S(1)}) custom-call(s32[1]{0:T(128)} %bitcast.place_ref, s32[1,16]{1,0:T(1,128)S(1)} %copy-done, f32[16]{0:T(128)S(1)} %copy-done.1, bf16[128,1024]{1,0:T(8,128)(2,1)S(1)} %pad_maximum_fusion.1.own_ref.refs_0_), custom_call_target="tpu_custom_call" | custom-call | tf_op jit(solution)/shard_map/pallas_call | solution.py:33
  6.6 1.6 %collective-permute-start.4 = (bf16[128,512]{1,0:T(8,128)(2,1)S(1)}, bf16[128,512]{1,0:T(8,128)(2,1)S(1)}, u32[]{:S(2)}, u32[]{:S(2)}) collective-permute-start(bf16[128,512]{1,0:T(8,128)(2,1)S(1)} %get-tuple-element.44), channel_id=1, source_target_pairs={{0,8},{2,10},{4,12},{6,14},{8,16},{10,18},{12,20},{14,22},{16,24},... | collective-permute-start | bytes 393224 | tf_op jit(solution)/shard_map/ppermute | solution.py:324
  8.2 1.2 %collective-permute-done.before_ref.refs_4_ = bf16[128,512]{1,0:T(8,128)(2,1)S(1)} collective-permute-done((bf16[128,512]{1,0:T(8,128)(2,1)}, bf16[128,512]{1,0:T(8,128)(2,1)S(1)}, u32[]{:S(2)}, u32[]{:S(2)}) %collective-permute-start) | collective-permute-done | bytes 131104 | tf_op jit(solution)/shard_map/ppermute | solution.py:324
  9.5 1.6 %collective-permute-start.1 = (bf16[128,512]{1,0:T(8,128)(2,1)S(1)}, bf16[128,512]{1,0:T(8,128)(2,1)S(1)}, u32[]{:S(2)}, u32[]{:S(2)}) collective-permute-start(bf16[128,512]{1,0:T(8,128)(2,1)S(1)} %get-tuple-element.39), channel_id=1, source_target_pairs={{0,2},{2,0},{4,6},{6,4},{8,10},{10,8},{12,14},{14,12},{16,18},{18,... | collective-permute-start | bytes 393224 | tf_op jit(solution)/shard_map/ppermute | solution.py:327
  11.0 1.5 %collective-permute-start.2 = (bf16[128,512]{1,0:T(8,128)(2,1)S(1)}, bf16[128,512]{1,0:T(8,128)(2,1)S(1)}, u32[]{:S(2)}, u32[]{:S(2)}) collective-permute-start(bf16[128,512]{1,0:T(8,128)(2,1)S(1)} %get-tuple-element.40), channel_id=1, source_target_pairs={{0,4},{2,6},{4,0},{6,2},{8,12},{10,14},{12,8},{14,10},{16,20},{18,... | collective-permute-start | bytes 393224 | tf_op jit(solution)/shard_map/ppermute | solution.py:327
  12.6 0.5 %collective-permute-start.3 = (bf16[128,512]{1,0:T(8,128)(2,1)S(1)}, bf16[128,512]{1,0:T(8,128)(2,1)S(1)}, u32[]{:S(2)}, u32[]{:S(2)}) collective-permute-start(bf16[128,512]{1,0:T(8,128)(2,1)S(1)} %get-tuple-element.41), channel_id=1, source_target_pairs={{0,6},{2,4},{4,2},{6,0},{8,14},{10,12},{12,10},{14,8},{16,22},{18,... | collective-permute-start | bytes 393224 | tf_op jit(solution)/shard_map/ppermute | solution.py:327
  13.0 1.3 %pad_maximum_fusion.pair_ref.refs_0_ = bf16[128,4096]{1,0:T(8,128)(2,1)S(1)} fusion(bf16[128,2048]{1,0:T(8,128)(2,1)} %bitcast.8, bf16[128,2048]{1,0:T(8,128)(2,1)} %bitcast.9), kind=kLoop, calls=%fused_computation | loop fusion | flops 2097152 | bytes 2097152 | tf_op jit(solution)/shard_map/concatenate | solution.py:331
  14.4 1.6 %collective-permute-start.5 = (bf16[128,512]{1,0:T(8,128)(2,1)S(1)}, bf16[128,512]{1,0:T(8,128)(2,1)S(1)}, u32[]{:S(2)}, u32[]{:S(2)}) collective-permute-start(bf16[128,512]{1,0:T(8,128)(2,1)S(1)} %get-tuple-element.45), channel_id=1, source_target_pairs={{0,2},{2,0},{4,6},{6,4},{8,10},{10,8},{12,14},{14,12},{16,18},{18,... | collective-permute-start | bytes 393224 | tf_op jit(solution)/shard_map/ppermute | solution.py:327
  16.0 1.5 %collective-permute-start.6 = (bf16[128,512]{1,0:T(8,128)(2,1)S(1)}, bf16[128,512]{1,0:T(8,128)(2,1)S(1)}, u32[]{:S(2)}, u32[]{:S(2)}) collective-permute-start(bf16[128,512]{1,0:T(8,128)(2,1)S(1)} %get-tuple-element.46), channel_id=1, source_target_pairs={{0,4},{2,6},{4,0},{6,2},{8,12},{10,14},{12,8},{14,10},{16,20},{18,... | collective-permute-start | bytes 393224 | tf_op jit(solution)/shard_map/ppermute | solution.py:327
  17.5 0.5 %collective-permute-start.7 = (bf16[128,512]{1,0:T(8,128)(2,1)S(1)}, bf16[128,512]{1,0:T(8,128)(2,1)S(1)}, u32[]{:S(2)}, u32[]{:S(2)}) collective-permute-start(bf16[128,512]{1,0:T(8,128)(2,1)S(1)} %get-tuple-element.47), channel_id=1, source_target_pairs={{0,6},{2,4},{4,2},{6,0},{8,14},{10,12},{12,10},{14,8},{16,22},{18,... | collective-permute-start | bytes 393224 | tf_op jit(solution)/shard_map/ppermute | solution.py:327
  18.4 1.5 %collective-permute-done.3.refs_3_ = bf16[128,512]{1,0:T(8,128)(2,1)S(1)} collective-permute-done((bf16[128,512]{1,0:T(8,128)(2,1)S(1)}, bf16[128,512]{1,0:T(8,128)(2,1)S(1)}, u32[]{:S(2)}, u32[]{:S(2)}) %collective-permute-start.3) | collective-permute-done | bytes 131104 | tf_op jit(solution)/shard_map/ppermute | solution.py:327
  19.9 2.1 %shard_map.95 = (bf16[2048,512]{1,0:T(8,128)(2,1)S(1)}, f32[8,512]{1,0:T(8,128)S(1)}, f32[512,128]{1,0:T(8,128)S(1)}, f32[512,128]{1,0:T(8,128)S(1)}, bf16[512,1...) custom-call(f32[8,512]{1,0:T(8,128)S(1)} %get-tuple-element.37.refs_0_.caps_ref, ...), custom_call_target="tpu_custom_call" | custom-call | tf_op jit(solution)/shard_map/pallas_call | solution.py:33
  22.1 1.0 %collective-permute-start.8 = (bf16[512,128]{1,0:T(8,128)(2,1)S(1)}, bf16[512,128]{1,0:T(8,128)(2,1)S(1)}, u32[]{:S(2)}, u32[]{:S(2)}) collective-permute-start(bf16[512,128]{1,0:T(8,128)(2,1)S(1)} %get-tuple-element.51), channel_id=1, source_target_pairs={{0,2},{2,0},{4,6},{6,4},{8,10},{10,8},{12,14},{14,12},{16,18},{18,... | collective-permute-start | bytes 393224 | tf_op jit(solution)/shard_map/ppermute | solution.py:327
  23.1 0.9 %collective-permute-start.9 = (bf16[512,128]{1,0:T(8,128)(2,1)S(1)}, bf16[512,128]{1,0:T(8,128)(2,1)S(1)}, u32[]{:S(2)}, u32[]{:S(2)}) collective-permute-start(bf16[512,128]{1,0:T(8,128)(2,1)S(1)} %get-tuple-element.52), channel_id=1, source_target_pairs={{0,4},{2,6},{4,0},{6,2},{8,12},{10,14},{12,8},{14,10},{16,20},{18,... | collective-permute-start | bytes 393224 | tf_op jit(solution)/shard_map/ppermute | solution.py:327
  24.0 1.6 %collective-permute-start.10 = (bf16[512,128]{1,0:T(8,128)(2,1)S(1)}, bf16[512,128]{1,0:T(8,128)(2,1)S(1)}, u32[]{:S(2)}, u32[]{:S(2)}) collective-permute-start(bf16[512,128]{1,0:T(8,128)(2,1)S(1)} %get-tuple-element.53), channel_id=1, source_target_pairs={{0,6},{2,4},{4,2},{6,0},{8,14},{10,12},{12,10},{14,8},{16,22},{18,... | collective-permute-start | bytes 393224 | tf_op jit(solution)/shard_map/ppermute | solution.py:327
  25.6 2.0 %shard_map.97 = (bf16[2560,512]{1,0:T(8,128)(2,1)S(1)}, f32[1,128]{1,0:T(1,128)S(1)}, f32[512,128]{1,0:T(8,128)S(1)}, f32[512,128]{1,0:T(8,128)S(1)}, bf16[528,1...) custom-call(bf16[2048,512]{1,0:T(8,128)(2,1)S(1)} %get-tuple-element.42.probs_ref, ...), custom_call_target="tpu_custom_call" | custom-call | tf_op jit(solution)/shard_map/pallas_call | solution.py:33
  27.6 1.0 %collective-permute-start.12 = (bf16[528,128]{1,0:T(8,128)(2,1)S(1)}, bf16[528,128]{1,0:T(8,128)(2,1)S(1)}, u32[]{:S(2)}, u32[]{:S(2)}) collective-permute-start(bf16[528,128]{1,0:T(8,128)(2,1)S(1)} %get-tuple-element.60), channel_id=1, source_target_pairs={{0,2},{2,0},{4,6},{6,4},{8,10},{10,8},{12,14},{14,12},{16,18},{18,... | collective-permute-start | bytes 405512 | tf_op jit(solution)/shard_map/ppermute | solution.py:327
  28.6 1.1 %collective-permute-start.13 = (bf16[528,128]{1,0:T(8,128)(2,1)S(1)}, bf16[528,128]{1,0:T(8,128)(2,1)S(1)}, u32[]{:S(2)}, u32[]{:S(2)}) collective-permute-start(bf16[528,128]{1,0:T(8,128)(2,1)S(1)} %get-tuple-element.61), channel_id=1, source_target_pairs={{0,4},{2,6},{4,0},{6,2},{8,12},{10,14},{12,8},{14,10},{16,20},{18,... | collective-permute-start | bytes 405512 | tf_op jit(solution)/shard_map/ppermute | solution.py:327
  29.8 1.4 %collective-permute-start.14 = (bf16[528,128]{1,0:T(8,128)(2,1)S(1)}, bf16[528,128]{1,0:T(8,128)(2,1)S(1)}, u32[]{:S(2)}, u32[]{:S(2)}) collective-permute-start(bf16[528,128]{1,0:T(8,128)(2,1)S(1)} %get-tuple-element.62), channel_id=1, source_target_pairs={{0,6},{2,4},{4,2},{6,0},{8,14},{10,12},{12,10},{14,8},{16,22},{18,... | collective-permute-start | bytes 405512 | tf_op jit(solution)/shard_map/ppermute | solution.py:327
  31.6 1.8 %collective-permute-start.11 = (bf16[512,128]{1,0:T(8,128)(2,1)S(1)}, bf16[512,128]{1,0:T(8,128)(2,1)S(1)}, u32[]{:S(2)}, u32[]{:S(2)}) collective-permute-start(bf16[512,128]{1,0:T(8,128)(2,1)S(1)} %get-tuple-element.55), channel_id=1, source_target_pairs={{0,24},{2,26},{4,28},{6,30},{8,0},{10,2},{12,4},{14,6},{16,8},{18,... | collective-permute-start | bytes 393224 | tf_op jit(solution)/shard_map/ppermute | solution.py:324
  33.4 1.0 %collective-permute-done.13.refs_1_ = bf16[528,128]{1,0:T(8,128)(2,1)S(1)} collective-permute-done((bf16[528,128]{1,0:T(8,128)(2,1)S(1)}, bf16[528,128]{1,0:T(8,128)(2,1)S(1)}, u32[]{:S(2)}, u32[]{:S(2)}) %collective-permute-start.13) | collective-permute-done | bytes 135200 | tf_op jit(solution)/shard_map/ppermute | solution.py:327
  34.3 1.4 %collective-permute-done.14.refs_2_ = bf16[528,128]{1,0:T(8,128)(2,1)S(1)} collective-permute-done((bf16[528,128]{1,0:T(8,128)(2,1)S(1)}, bf16[528,128]{1,0:T(8,128)(2,1)S(1)}, u32[]{:S(2)}, u32[]{:S(2)}) %collective-permute-start.14) | collective-permute-done | bytes 135200 | tf_op jit(solution)/shard_map/ppermute | solution.py:327
  36.0 1.8 %collective-permute-start.15 = (bf16[528,128]{1,0:T(8,128)(2,1)S(1)}, bf16[528,128]{1,0:T(8,128)(2,1)S(1)}, u32[]{:S(2)}, u32[]{:S(2)}) collective-permute-start(bf16[528,128]{1,0:T(8,128)(2,1)S(1)} %get-tuple-element.64), channel_id=1, source_target_pairs={{0,24},{2,26},{4,28},{6,30},{8,0},{10,2},{12,4},{14,6},{16,8},{18,... | collective-permute-start | bytes 405512 | tf_op jit(solution)/shard_map/ppermute | solution.py:324
  38.0 0.7 %collective-permute-start.16 = (f32[1,128]{1,0:T(1,128)S(1)}, f32[1,128]{1,0:T(1,128)S(1)}, u32[]{:S(2)}, u32[]{:S(2)}) collective-permute-start(f32[1,128]{1,0:T(1,128)S(1)} %get-tuple-element.67.sink_ref), channel_id=1, source_target_pairs={{0,16},{2,18},{4,20},{6,22},{8,24},{10,26},{12,28},{14,30},{16,0},... | collective-permute-start | bytes 1544 | tf_op jit(solution)/shard_map/ppermute | solution.py:324
  38.7 1.5 %shard_map.99 = (bf16[128,512]{1,0:T(8,128)(2,1)}, bf16[128,2048]{1,0:T(8,128)(2,1)}, f32[1,128]{1,0:T(1,128)S(1)}) custom-call(bf16[2560,512]{1,0:T(8,128)(2,1)S(1)} %get-tuple-element.48.gscores_ref, f32[512,128]{1,0:T(8,128)S(1)} %get-tuple-element.54.own_ref, bf16[512,128]{1,0:T(8,128)(2,1)S(1)} %collective-permute-done.11.last_ref, ...), custom_call_target="tpu_custom_call" | custom-call | flops 335544320 | tf_op jit(solution)/shard_map/pallas_call | solution.py:33
  40.2 2.8 %collective-permute-done.17.refs_1_ = f32[1,128]{1,0:T(1,128)S(1)} collective-permute-done((f32[1,128]{1,0:T(1,128)S(1)}, f32[1,128]{1,0:T(1,128)S(1)}, u32[]{:S(2)}, u32[]{:S(2)}) %collective-permute-start.17) | collective-permute-done | bytes 544 | tf_op jit(solution)/shard_map/ppermute | solution.py:324
  43.2 0.7 %shard_map.101 = (bf16[128,512]{1,0:T(8,128)(2,1)}, f32[1,128]{1,0:T(1,128)S(1)}) custom-call(f32[512,128]{1,0:T(8,128)S(1)} %get-tuple-element.63.own_ref, bf16[528,128]{1,0:T(8,128)(2,1)S(1)} %collective-permute-done.15.last_ref), custom_call_target="tpu_custom_call" | custom-call | tf_op jit(solution)/shard_map/pallas_call | solution.py:33
  44.3 0.5 %shard_map.103 = f32[16]{0:T(128)} custom-call(f32[1,128]{1,0:T(1,128)S(1)} %add.3.sink_ref, f32[1,128]{1,0:T(1,128)S(1)} %get-tuple-element.69.done_ref), custom_call_target="tpu_custom_call" | custom-call | tf_op jit(solution)/shard_map/pallas_call | solution.py:33
  (24 shorter events, 2.0 us)
Async XLA Ops:
  0.6 8.8 %collective-permute-start = (bf16[128,512]{1,0:T(8,128)(2,1)}, bf16[128,512]{1,0:T(8,128)(2,1)S(1)}, u32[]{:S(2)}, u32[]{:S(2)}) collective-permute-start(bf16[128,512]{1,0:T(8,128)(2,1)} %bitcast.11), channel_id=1, source_target_pairs={{0,8},{2,10},{4,12},{6,14},{8,16},{10,18},{12,20},{14,22},{16,24},... | collective-permute-start | bytes 393224 | tf_op jit(solution)/shard_map/ppermute | solution.py:324
  4.7 0.7 %copy-start = (s32[1,16]{1,0:T(1,128)S(1)}, s32[1,16]{1,0:T(1,128)}, u32[]{:S(2)}) copy-start(s32[1,16]{1,0:T(1,128)} %docs_ref.1) | copy-start | bytes 196
  5.4 0.7 %copy-start.1 = (f32[16]{0:T(128)S(1)}, f32[16]{0:T(128)}, u32[]{:S(2)}) copy-start(f32[16]{0:T(128)} %sinks_ref.1) | copy-start | bytes 196
  6.6 7.7 %collective-permute-start.4 = (bf16[128,512]{1,0:T(8,128)(2,1)S(1)}, bf16[128,512]{1,0:T(8,128)(2,1)S(1)}, u32[]{:S(2)}, u32[]{:S(2)}) collective-permute-start(bf16[128,512]{1,0:T(8,128)(2,1)S(1)} %get-tuple-element.44), channel_id=1, source_target_pairs={{0,8},{2,10},{4,12},{6,14},{8,16},{10,18},{12,20},{14,22},{16,24},... | collective-permute-start | bytes 393224 | tf_op jit(solution)/shard_map/ppermute | solution.py:324
  9.5 8.0 %collective-permute-start.1 = (bf16[128,512]{1,0:T(8,128)(2,1)S(1)}, bf16[128,512]{1,0:T(8,128)(2,1)S(1)}, u32[]{:S(2)}, u32[]{:S(2)}) collective-permute-start(bf16[128,512]{1,0:T(8,128)(2,1)S(1)} %get-tuple-element.39), channel_id=1, source_target_pairs={{0,2},{2,0},{4,6},{6,4},{8,10},{10,8},{12,14},{14,12},{16,18},{18,... | collective-permute-start | bytes 393224 | tf_op jit(solution)/shard_map/ppermute | solution.py:327
  11.0 7.4 %collective-permute-start.2 = (bf16[128,512]{1,0:T(8,128)(2,1)S(1)}, bf16[128,512]{1,0:T(8,128)(2,1)S(1)}, u32[]{:S(2)}, u32[]{:S(2)}) collective-permute-start(bf16[128,512]{1,0:T(8,128)(2,1)S(1)} %get-tuple-element.40), channel_id=1, source_target_pairs={{0,4},{2,6},{4,0},{6,2},{8,12},{10,14},{12,8},{14,10},{16,20},{18,... | collective-permute-start | bytes 393224 | tf_op jit(solution)/shard_map/ppermute | solution.py:327
  12.6 7.4 %collective-permute-start.3 = (bf16[128,512]{1,0:T(8,128)(2,1)S(1)}, bf16[128,512]{1,0:T(8,128)(2,1)S(1)}, u32[]{:S(2)}, u32[]{:S(2)}) collective-permute-start(bf16[128,512]{1,0:T(8,128)(2,1)S(1)} %get-tuple-element.41), channel_id=1, source_target_pairs={{0,6},{2,4},{4,2},{6,0},{8,14},{10,12},{12,10},{14,8},{16,22},{18,... | collective-permute-start | bytes 393224 | tf_op jit(solution)/shard_map/ppermute | solution.py:327
  14.4 9.6 %collective-permute-start.5 = (bf16[128,512]{1,0:T(8,128)(2,1)S(1)}, bf16[128,512]{1,0:T(8,128)(2,1)S(1)}, u32[]{:S(2)}, u32[]{:S(2)}) collective-permute-start(bf16[128,512]{1,0:T(8,128)(2,1)S(1)} %get-tuple-element.45), channel_id=1, source_target_pairs={{0,2},{2,0},{4,6},{6,4},{8,10},{10,8},{12,14},{14,12},{16,18},{18,... | collective-permute-start | bytes 393224 | tf_op jit(solution)/shard_map/ppermute | solution.py:327
  16.0 9.7 %collective-permute-start.6 = (bf16[128,512]{1,0:T(8,128)(2,1)S(1)}, bf16[128,512]{1,0:T(8,128)(2,1)S(1)}, u32[]{:S(2)}, u32[]{:S(2)}) collective-permute-start(bf16[128,512]{1,0:T(8,128)(2,1)S(1)} %get-tuple-element.46), channel_id=1, source_target_pairs={{0,4},{2,6},{4,0},{6,2},{8,12},{10,14},{12,8},{14,10},{16,20},{18,... | collective-permute-start | bytes 393224 | tf_op jit(solution)/shard_map/ppermute | solution.py:327
  17.5 8.1 %collective-permute-start.7 = (bf16[128,512]{1,0:T(8,128)(2,1)S(1)}, bf16[128,512]{1,0:T(8,128)(2,1)S(1)}, u32[]{:S(2)}, u32[]{:S(2)}) collective-permute-start(bf16[128,512]{1,0:T(8,128)(2,1)S(1)} %get-tuple-element.47), channel_id=1, source_target_pairs={{0,6},{2,4},{4,2},{6,0},{8,14},{10,12},{12,10},{14,8},{16,22},{18,... | collective-permute-start | bytes 393224 | tf_op jit(solution)/shard_map/ppermute | solution.py:327
  22.1 7.7 %collective-permute-start.8 = (bf16[512,128]{1,0:T(8,128)(2,1)S(1)}, bf16[512,128]{1,0:T(8,128)(2,1)S(1)}, u32[]{:S(2)}, u32[]{:S(2)}) collective-permute-start(bf16[512,128]{1,0:T(8,128)(2,1)S(1)} %get-tuple-element.51), channel_id=1, source_target_pairs={{0,2},{2,0},{4,6},{6,4},{8,10},{10,8},{12,14},{14,12},{16,18},{18,... | collective-permute-start | bytes 393224 | tf_op jit(solution)/shard_map/ppermute | solution.py:327
  23.1 8.1 %collective-permute-start.9 = (bf16[512,128]{1,0:T(8,128)(2,1)S(1)}, bf16[512,128]{1,0:T(8,128)(2,1)S(1)}, u32[]{:S(2)}, u32[]{:S(2)}) collective-permute-start(bf16[512,128]{1,0:T(8,128)(2,1)S(1)} %get-tuple-element.52), channel_id=1, source_target_pairs={{0,4},{2,6},{4,0},{6,2},{8,12},{10,14},{12,8},{14,10},{16,20},{18,... | collective-permute-start | bytes 393224 | tf_op jit(solution)/shard_map/ppermute | solution.py:327
  24.0 7.5 %collective-permute-start.10 = (bf16[512,128]{1,0:T(8,128)(2,1)S(1)}, bf16[512,128]{1,0:T(8,128)(2,1)S(1)}, u32[]{:S(2)}, u32[]{:S(2)}) collective-permute-start(bf16[512,128]{1,0:T(8,128)(2,1)S(1)} %get-tuple-element.53), channel_id=1, source_target_pairs={{0,6},{2,4},{4,2},{6,0},{8,14},{10,12},{12,10},{14,8},{16,22},{18,... | collective-permute-start | bytes 393224 | tf_op jit(solution)/shard_map/ppermute | solution.py:327
  27.6 5.7 %collective-permute-start.12 = (bf16[528,128]{1,0:T(8,128)(2,1)S(1)}, bf16[528,128]{1,0:T(8,128)(2,1)S(1)}, u32[]{:S(2)}, u32[]{:S(2)}) collective-permute-start(bf16[528,128]{1,0:T(8,128)(2,1)S(1)} %get-tuple-element.60), channel_id=1, source_target_pairs={{0,2},{2,0},{4,6},{6,4},{8,10},{10,8},{12,14},{14,12},{16,18},{18,... | collective-permute-start | bytes 405512 | tf_op jit(solution)/shard_map/ppermute | solution.py:327
  28.6 5.7 %collective-permute-start.13 = (bf16[528,128]{1,0:T(8,128)(2,1)S(1)}, bf16[528,128]{1,0:T(8,128)(2,1)S(1)}, u32[]{:S(2)}, u32[]{:S(2)}) collective-permute-start(bf16[528,128]{1,0:T(8,128)(2,1)S(1)} %get-tuple-element.61), channel_id=1, source_target_pairs={{0,4},{2,6},{4,0},{6,2},{8,12},{10,14},{12,8},{14,10},{16,20},{18,... | collective-permute-start | bytes 405512 | tf_op jit(solution)/shard_map/ppermute | solution.py:327
  29.8 6.0 %collective-permute-start.14 = (bf16[528,128]{1,0:T(8,128)(2,1)S(1)}, bf16[528,128]{1,0:T(8,128)(2,1)S(1)}, u32[]{:S(2)}, u32[]{:S(2)}) collective-permute-start(bf16[528,128]{1,0:T(8,128)(2,1)S(1)} %get-tuple-element.62), channel_id=1, source_target_pairs={{0,6},{2,4},{4,2},{6,0},{8,14},{10,12},{12,10},{14,8},{16,22},{18,... | collective-permute-start | bytes 405512 | tf_op jit(solution)/shard_map/ppermute | solution.py:327
  31.6 7.1 %collective-permute-start.11 = (bf16[512,128]{1,0:T(8,128)(2,1)S(1)}, bf16[512,128]{1,0:T(8,128)(2,1)S(1)}, u32[]{:S(2)}, u32[]{:S(2)}) collective-permute-start(bf16[512,128]{1,0:T(8,128)(2,1)S(1)} %get-tuple-element.55), channel_id=1, source_target_pairs={{0,24},{2,26},{4,28},{6,30},{8,0},{10,2},{12,4},{14,6},{16,8},{18,... | collective-permute-start | bytes 393224 | tf_op jit(solution)/shard_map/ppermute | solution.py:324
  36.0 7.1 %collective-permute-start.15 = (bf16[528,128]{1,0:T(8,128)(2,1)S(1)}, bf16[528,128]{1,0:T(8,128)(2,1)S(1)}, u32[]{:S(2)}, u32[]{:S(2)}) collective-permute-start(bf16[528,128]{1,0:T(8,128)(2,1)S(1)} %get-tuple-element.64), channel_id=1, source_target_pairs={{0,24},{2,26},{4,28},{6,30},{8,0},{10,2},{12,4},{14,6},{16,8},{18,... | collective-permute-start | bytes 405512 | tf_op jit(solution)/shard_map/ppermute | solution.py:324
  37.7 5.3 %collective-permute-start.17 = (f32[1,128]{1,0:T(1,128)S(1)}, f32[1,128]{1,0:T(1,128)S(1)}, u32[]{:S(2)}, u32[]{:S(2)}) collective-permute-start(f32[1,128]{1,0:T(1,128)S(1)} %get-tuple-element.67.sink_ref), channel_id=1, source_target_pairs={{0,8},{2,10},{4,12},{6,14},{8,16},{10,18},{12,20},{14,22},{16,24},... | collective-permute-start | bytes 1544 | tf_op jit(solution)/shard_map/ppermute | solution.py:324
  38.0 5.0 %collective-permute-start.16 = (f32[1,128]{1,0:T(1,128)S(1)}, f32[1,128]{1,0:T(1,128)S(1)}, u32[]{:S(2)}, u32[]{:S(2)}) collective-permute-start(f32[1,128]{1,0:T(1,128)S(1)} %get-tuple-element.67.sink_ref), channel_id=1, source_target_pairs={{0,16},{2,18},{4,20},{6,22},{8,24},{10,26},{12,28},{14,30},{16,0},... | collective-permute-start | bytes 1544 | tf_op jit(solution)/shard_map/ppermute | solution.py:324
  43.1 1.2 %collective-permute-start.18 = (f32[1,128]{1,0:T(1,128)S(1)}, f32[1,128]{1,0:T(1,128)S(1)}, u32[]{:S(2)}, u32[]{:S(2)}) collective-permute-start(f32[1,128]{1,0:T(1,128)S(1)} %shard_map.102), channel_id=1, source_target_pairs={{0,1},{1,0},{2,3},{3,2},{4,5},{5,4},{6,7},{7,6},{8,9},{9,8},{10,11... | collective-permute-start | bytes 1544 | tf_op jit(solution)/shard_map/ppermute | solution.py:327
